TPU v7x, 512 devices: a whole 4x8x8 slice. The times are simulated.
512 devices in a mesh: dp: 8 (over z), seq: 16 (over y, core), mp: 4 (over x).
Axes of the slice: x: 4, y: 8, z: 8, core: 2. Of those that a mesh axis runs over, the one named last changes fastest.
Arguments:
- tokens: bfloat16 [65536, 4096], P(('dp', 'seq'), 'mp'), parts along dimension 0, may hold values from -30 to 30
- heavy_index: int32 [8192], P(('dp', 'seq')), parts along dimension 0, may hold values from -1 to 8191, as said below
- norm_gain: float32 [4096], P('mp'), may hold values from 0.1 to 1.9
- router: bfloat16 [4096], P('mp'), may hold values from -0.09375 to 0.09375
- w_up: bfloat16 [4096, 8192], P('mp', 'seq'), may hold values from -0.09375 to 0.09375
- w_down: bfloat16 [8192, 4096], P('seq', 'mp'), may hold values from -0.0625 to 0.0625
Outputs:
- mixed: bfloat16 [65536, 4096], P(('dp', 'seq'), 'mp'), parts along dimension 0
There are 8 independent parts, one for each index of `dp`. A program takes and returns all parts, laid end to end along the dimension named above; an argument that names none is the same for every part. Nothing has to cross between parts.
Inputs may be any that keep to these rules, and one draw needn't show every extreme that they name: `heavy_index`: the 64 slots of each index of seq hold, in rising order, the positions of that index's own routed tokens, then -1. Every index has 0 to 64 routed tokens, some index exactly 64, and all together exactly 512.
All inputs are finite; a program needn't handle non-finite values.
Results may differ from a plain program's by a relative error of at most 0.0035.
Values may be sent and summed in bfloat16 or wider, within the bound.
No kernel may reach another device: no remote copies, remote signals or barrier semaphores. Data moves between devices by JAX's collectives and lax.ppermute only.
A program may use at most 64 MiB of HBM per device.

v0:
```python
import jax
import jax.numpy as jnp
from jax import lax
from jax.sharding import PartitionSpec as P

D = 4096


def finish_hidden(up_part):
    summed = lax.psum(up_part.astype(jnp.bfloat16), "mp").astype(jnp.float32)
    return jax.nn.gelu(summed, approximate=True).astype(jnp.bfloat16)


def owner_terms(hidden, w_down):
    return lax.psum_scatter(
        jnp.dot(hidden, w_down, preferred_element_type=jnp.float32).astype(jnp.bfloat16),
        "seq",
        scatter_dimension=0,
        tiled=True,
    ).astype(jnp.float32)


def per_device(tokens, heavy_index, norm_gain, router, w_up, w_down):
    tok_rows = tokens.shape[0]
    seq_rank = lax.axis_index("seq")
    local_index = heavy_index - seq_rank * tok_rows
    is_valid = heavy_index >= 0
    picker = (local_index[:, None] == jnp.arange(tok_rows, dtype=jnp.int32)[None, :]).astype(
        jnp.bfloat16
    )
    selected = jnp.dot(picker, tokens, preferred_element_type=jnp.float32)
    square_part = jnp.sum(selected * selected, axis=1)
    router_part = jnp.sum(selected * (norm_gain * router.astype(jnp.float32)), axis=1)
    square_sums, router_sums = lax.psum((square_part, router_part), "mp")
    inverse = lax.rsqrt(square_sums / D + 1e-06)
    scores = jax.nn.sigmoid(router_sums * inverse)
    normed = (selected * inverse[:, None] * norm_gain).astype(jnp.bfloat16)
    up_part = jnp.dot(
        lax.all_gather(normed, "seq", axis=0, tiled=True), w_up, preferred_element_type=jnp.float32
    )
    hidden = finish_hidden(up_part)
    heavy_out = owner_terms(hidden, w_down)
    addition = scores[:, None] * heavy_out * is_valid[:, None].astype(jnp.float32)
    placed = jnp.dot(picker.T.astype(jnp.float32), addition, precision=lax.Precision.HIGHEST)
    return (tokens.astype(jnp.float32) + placed).astype(jnp.bfloat16)


def solution(mesh):
    placed = (
        P(("dp", "seq"), "mp"),
        P(("dp", "seq")),
        P("mp"),
        P("mp"),
        P("mp", "seq"),
        P("seq", "mp"),
    )
    return jax.shard_map(
        per_device, mesh=mesh, in_specs=placed, out_specs=P(("dp", "seq"), "mp"), check_vma=False
    )
```

profile of v0, /device:TPU:1, one launch (start us, length us, event | category | flops | bytes accessed | tf_op | source)
XLA Modules:
  0.0 201.2 jit_solution(18137676887949994000)
XLA Ops:
  6.5 0.0 copy-start
  6.5 0.0 all-gather.2.cloned.1.call-start
  6.5 0.7 broadcast_subtract_fusion
  7.3 0.7 convert_multiply_fusion.3
  8.0 1.7 multiply_reduce_fusion.1
  9.7 9.3 %all-reduce = (f32[64]{0:T(128)S(1)}, f32[64]{0:T(128)S(1)}) all-reduce(f32[64]{0:T(128)S(1)} %get-tuple-element.6, f32[64]{0:T(128)S(1)} %get-tuple-element.5), channel_id=1, replica_groups=mesh['dp'=8,'seq'=16,'mp'=4] {'mp'}, use_global_device_ids=true, to_apply=%region_3.0 | all-reduce | flops 128 | bytes 1024 | tf_op jit(solution)/shard_map/psum | solution.py:34
  19.0 1.4 multiply_convert_fusion
  20.4 0.0 all-gather.2.cloned.1.call-update
  20.4 0.0 all-reduce.3.cloned.1.call-start
  20.5 46.9 %all-gather.2.cloned.1.call-done = bf16[1024,1024]{1,0:T(8,128)(2,1)} async-done(((bf16[64,1024]{1,0:T(8,128)(2,1)}), bf16[1024,1024]{1,0:T(8,128)(2,1)}) %all-gather.2.cloned.1.call-update) | async-done | bytes 2097168 | tf_op jit(solution)/shard_map/all_gather | solution.py:39
  67.4 4.1 %convolution_convert_fusion.1 = bf16[1024,512]{1,0:T(8,128)(2,1)} fusion(bf16[1024,1024]{1,0:T(8,128)(2,1)} %all-gather.2.cloned.1.call-done, bf16[1024,512]{1,0:T(8,128)(2,1)} %param.10), kind=kOutput, calls=%fused_computation.12 | convolution fusion | flops 1074266112 | bytes 4194304 | tf_op jit(solution)/shard_map/dot_general | solution.py:38
  71.5 0.0 all-reduce.3.cloned.1.call-update
  71.5 0.0 reduce-scatter.2.cloned.1.call-start
  71.6 53.7 %all-reduce.3.cloned.1.call-done = bf16[1024,512]{1,0:T(8,128)(2,1)} async-done(((bf16[1024,512]{1,0:T(8,128)(2,1)}), bf16[1024,512]{1,0:T(8,128)(2,1)}) %all-reduce.3.cloned.1.call-update) | async-done | bytes 1048592 | tf_op jit(solution)/shard_map/psum | solution.py:10
  125.3 0.0 copy-done
  125.3 4.1 %convolution_convert_fusion = bf16[1024,1024]{1,0:T(8,128)(2,1)} fusion(bf16[512,1024]{1,0:T(8,128)(2,1)S(1)} %copy-done, bf16[1024,512]{1,0:T(8,128)(2,1)} %all-reduce.3.cloned.1.call-done), kind=kOutput, calls=%fused_computation.11 | convolution fusion | flops 1080033280 | bytes 4194304 | tf_op jit(solution)/shard_map/dot_general | solution.py:16
  129.3 0.0 copy-start.2
  129.3 0.0 copy-start.1
  129.3 0.0 reduce-scatter.2.cloned.1.call-update
  129.4 0.6 copy-done.2
  130.0 61.6 %reduce-scatter.2.cloned.1.call-done = bf16[64,1024]{1,0:T(8,128)(2,1)} async-done(((bf16[1024,1024]{1,0:T(8,128)(2,1)}), bf16[64,1024]{1,0:T(8,128)(2,1)}) %reduce-scatter.2.cloned.1.call-update) | async-done | bytes 131088 | tf_op jit(solution)/shard_map/reduce_scatter | solution.py:15
  191.6 0.0 copy-done.1
  191.6 3.1 %add_convert_fusion = bf16[512,1024]{1,0:T(8,128)(2,1)} fusion(bf16[512,1024]{1,0:T(8,128)(2,1)S(1)} %copy-done.1, bf16[64,1024]{1,0:T(8,128)(2,1)} %reduce-scatter.2.cloned.1.call-done, f32[64]{0:T(128)S(1)} %compare_convert_fusion, f32[64]{0:T(128)S(1)} %get-tuple-element.9, s32[64]{0:T(128)S(1)} %broadcast_subtract_fusion), kind=kOutput, calls=%fused_computation.10 | convolution fusion | flops 404455424 | bytes 2228992 | tf_op jit(solution)/shard_map/dot_general | solution.py:44
  (2 shorter events, 0.0 us)
Async XLA Ops:
  6.5 118.7 %copy-start = (bf16[512,1024]{1,0:T(8,128)(2,1)S(1)}, bf16[512,1024]{1,0:T(8,128)(2,1)}, u32[]{:S(2)}) copy-start(bf16[512,1024]{1,0:T(8,128)(2,1)} %param.11) | copy-start | bytes 3145732
  6.5 60.9 %all-gather.2.cloned.1.call-start = ((), (), s32[]{:S(2)}) async-start(), calls=%async_computation.1 | async-start | bytes 2228224 | tf_op jit(solution)/shard_map/all_gather | solution.py:39
  20.4 104.8 %all-reduce.3.cloned.1.call-start = ((), (), s32[]{:S(2)}) async-start(), calls=%async_computation.2 | async-start | bytes 2097152 | tf_op jit(solution)/shard_map/psum | solution.py:10
  71.5 120.1 %reduce-scatter.2.cloned.1.call-start = ((), (), s32[]{:S(2)}) async-start(), calls=%async_computation.3 | async-start | bytes 2228224 | tf_op jit(solution)/shard_map/reduce_scatter | solution.py:15
  129.3 0.7 copy-start.2
  129.3 62.3 %copy-start.1 = (bf16[512,1024]{1,0:T(8,128)(2,1)S(1)}, bf16[512,1024]{1,0:T(8,128)(2,1)}, u32[]{:S(2)}) copy-start(bf16[512,1024]{1,0:T(8,128)(2,1)} %param.6) | copy-start | bytes 3145732
Sparse Core Ops, SparseCore 0:
  20.6 46.8 all-gather.1
  71.7 53.5 all-reduce.2
  129.5 62.0 reduce-scatter.1
where the time goes:
time: 202 us; the launch traced here: 201 us
  waiting for transfers between devices  162 us (80%)
  between operations  13.1 us (6%)
  matrix products  12.9 us (6%)
  blocking collectives  9.3 us (5%)
  other arithmetic  2.91 us (1%)
    reduce_scatter x1, waiting for transfers between devices, owner_terms(): lax.psum_scatter(jnp.dot(hidden, w_down, preferred_element_type=jnp.float...  61.6 us
    psum x1, waiting for transfers between devices, finish_hidden(): summed = lax.psum(up_part.astype(jnp.bfloat16), 'mp').astype(jnp.float32)  53.7 us
    all_gather x1, waiting for transfers between devices, per_device(): lax.all_gather(normed, 'seq', axis=0, tiled=True)  46.9 us
    psum x1, blocking collectives, per_device(): square_sums, router_sums = lax.psum((square_part, router_part), 'mp')  9.3 us
    dot_general x1, matrix products, per_device(): jnp.dot(lax.all_gather(normed, 'seq', axis=0, tiled=True), w_up, preferre...  4.08 us
    dot_general x1, matrix products, owner_terms(): jnp.dot(hidden, w_down, preferred_element_type=jnp.float32)  4.06 us
  transfers between devices with their start and end apart: 3, of which 3 were waited for; matrix products, arithmetic and copies ran while one was open for 0% of the time, Pallas kernels for 0%

commit v1 on v0

v1 whole, which is shorter than its diff:
```python
import jax
import jax.numpy as jnp
from jax import lax
from jax.sharding import Mesh, PartitionSpec as P

D = 4096
BF = jnp.bfloat16
F32 = jnp.float32


def halves(value):
    high = value.astype(BF)
    return high, (value - high.astype(F32)).astype(BF)


def per_device(tokens, heavy_index, norm_gain, router, w_up, w_down):
    tok_rows, width = tokens.shape
    slots = heavy_index.shape[0]
    hidden_width = w_up.shape[1]
    chips = lax.axis_size("y")
    parts = lax.axis_size("mp")
    cores = [(0, 1), (1, 0)]
    seq_rank = lax.axis_index("y") * 2 + lax.axis_index("core")
    local_index = heavy_index - seq_rank * tok_rows
    hits = local_index[:, None] == jnp.arange(tok_rows, dtype=jnp.int32)[None, :]
    picker = hits.astype(BF)
    selected = jnp.dot(picker, tokens, preferred_element_type=F32).astype(BF)

    spread = jnp.broadcast_to(selected[None], (chips, slots, width))
    mine = lax.all_to_all(spread, "y", 0, 0, tiled=True).reshape(chips * slots, width)
    other = lax.ppermute(mine, "core", cores)
    rows = jnp.concatenate([mine, other])
    total = rows.shape[0]
    chunk = total // parts

    raw = rows.astype(F32)
    square_part = jnp.sum(raw * raw, axis=1)
    router_part = jnp.sum(raw * (norm_gain * router.astype(F32)), axis=1)
    up_part = jnp.dot((raw * norm_gain).astype(BF), w_up, preferred_element_type=F32).astype(BF)
    sums = jnp.stack([square_part.reshape(parts, chunk), router_part.reshape(parts, chunk)], axis=1)
    sums = jnp.stack(halves(sums), axis=2).reshape(parts, -1, hidden_width)
    sums = jnp.pad(sums, ((0, 0), (0, 16 - sums.shape[1]), (0, 0)))
    packed = jnp.concatenate([up_part.reshape(parts, chunk, hidden_width), sums], axis=1)
    packed = lax.all_to_all(packed, "mp", 0, 0, tiled=True).astype(F32)
    summed = jnp.sum(packed, axis=0)
    sums = summed[chunk:].reshape(-1)[: 4 * chunk].reshape(2, 2, chunk).sum(axis=1)
    inverse = lax.rsqrt(sums[0] / D + 1e-06)
    scores = jax.nn.sigmoid(sums[1] * inverse)
    hidden = jax.nn.gelu(summed[:chunk] * inverse[:, None], approximate=True) * scores[:, None]
    hidden = jnp.broadcast_to(hidden.astype(BF)[None], (parts, chunk, hidden_width))
    hidden = lax.all_to_all(hidden, "mp", 0, 0, tiled=True).reshape(total, hidden_width)

    down = jnp.dot(hidden, w_down, preferred_element_type=F32)
    half = total // 2
    away = lax.ppermute(down[half:].astype(BF), "core", cores)
    chip_sum = (down[:half] + away.astype(F32)).astype(BF).reshape(chips, slots, width)
    addition = jnp.sum(lax.all_to_all(chip_sum, "y", 0, 0, tiled=True).astype(F32), axis=0)
    placed = jnp.dot(picker.T.astype(F32), addition, precision=lax.Precision.HIGHEST)
    return (tokens.astype(F32) + placed).astype(BF)


def solution(mesh):
    dp, seq, mp = mesh.devices.shape
    fine = Mesh(mesh.devices.reshape(dp, seq // 2, 2, mp), ("dp", "y", "core", "mp"))
    seq = ("y", "core")
    rows = ("dp",) + seq
    placed = (P(rows, "mp"), P(rows), P("mp"), P("mp"), P("mp", seq), P(seq, "mp"))
    return jax.shard_map(
        per_device, mesh=fine, in_specs=placed, out_specs=P(rows, "mp"), check_vma=False
    )
```

time: 202 us -> 126 us (0.62)
  waiting for transfers between devices: 162 us -> 4.5 us
  blocking collectives: 9.3 us -> 100 us
  between operations: 13.1 us -> 0.18 us
  starting transfers between devices: 0.09 us -> 10.1 us
  matrix products: 12.9 us -> 7.44 us
    all_to_all x0 -> x4, blocking collectives: none -> 100 us  [the longest x1 33.4 us: per_device(): lax.all_to_all(spread, 'y', 0, 0, tiled=True).reshape(chips * slots, width)]
    reduce_scatter x1 -> x0, waiting for transfers between devices: 61.6 us -> none  [owner_terms(): lax.psum_scatter(jnp.dot(hidden, w_down, preferred_element_type=jnp.float...]
    psum x1 -> x0, waiting for transfers between devices: 53.7 us -> none  [finish_hidden(): summed = lax.psum(up_part.astype(jnp.bfloat16), 'mp').astype(jnp.float32)]
    all_gather x1 -> x0, waiting for transfers between devices: 46.9 us -> none  [per_device(): lax.all_gather(normed, 'seq', axis=0, tiled=True)]
    ppermute x0 -> x2, starting transfers between devices: none -> 10.1 us  [the longest x1 5.62 us: per_device(): other = lax.ppermute(mine, 'core', cores)]
    psum x1 -> x0, blocking collectives: 9.3 us -> none  [per_device(): square_sums, router_sums = lax.psum((square_part, router_part), 'mp')]
    dot_general x4, matrix products: 12.9 us -> 7.44 us  [the longest x1 2.48 us: per_device(): jnp.dot((raw * norm_gain).astype(BF), w_up, preferred_element_type=F32)]
    ppermute x0 -> x2, waiting for transfers between devices: none -> 4.5 us  [the longest x1 2.26 us: per_device(): away = lax.ppermute(down[half:].astype(BF), 'core', cores)]
  transfers between devices with their start and end apart: 3 -> 2, of which waited for: 3 -> 2; matrix products, arithmetic and copies ran while one was open for 0% -> 0% of each run, Pallas kernels for 0% -> 0%
where the time goes in v1:
time: 126 us; the launch traced here: 125 us
  blocking collectives  100 us (79%)
  starting transfers between devices  10.1 us (8%)
  matrix products  7.44 us (6%)
  waiting for transfers between devices  4.5 us (4%)
  other arithmetic  2.68 us (2%)
    all_to_all x1, blocking collectives, per_device(): lax.all_to_all(spread, 'y', 0, 0, tiled=True).reshape(chips * slots, width)  33.4 us
    all_to_all x1, blocking collectives, per_device(): lax.all_to_all(chip_sum, 'y', 0, 0, tiled=True).astype(F32)  31.8 us
    all_to_all x1, blocking collectives, per_device(): packed = lax.all_to_all(packed, 'mp', 0, 0, tiled=True).astype(F32)  19 us
    all_to_all x1, blocking collectives, per_device(): lax.all_to_all(hidden, 'mp', 0, 0, tiled=True).reshape(total, hidden_width)  15.9 us
    ppermute x1, starting transfers between devices, per_device(): other = lax.ppermute(mine, 'core', cores)  5.62 us
    ppermute x1, starting transfers between devices, per_device(): away = lax.ppermute(down[half:].astype(BF), 'core', cores)  4.45 us
  transfers between devices with their start and end apart: 2, of which 2 were waited for; matrix products, arithmetic and copies ran while one was open for 0% of the time, Pallas kernels for 0%

profile of v1, /device:TPU:1, one launch (start us, length us, event | category | flops | bytes accessed | tf_op | source)
XLA Modules:
  0.0 125.4 jit_solution(10642371102339969914)
XLA Ops:
  0.0 0.0 copy-start
  0.0 0.7 broadcast_subtract_fusion
  0.8 0.0 copy-start.2
  0.8 0.0 copy-start.3
  0.8 1.6 %convolution_convert_fusion = bf16[64,1024]{1,0:T(8,128)(2,1)S(1)} fusion(bf16[512,1024]{1,0:T(8,128)(2,1)} %param.6, s32[64]{0:T(128)S(1)} %broadcast_subtract_fusion), kind=kOutput, calls=%fused_computation.18 | convolution fusion | flops 67207168 | bytes 1179904 | tf_op jit(solution)/shard_map/dot_general | solution.py:27
  2.3 0.1 broadcast_in_dim.4
  2.5 33.4 %all_to_all.20 = bf16[8,64,1024]{2,1,0:T(8,128)(2,1)S(1)} all-to-all(bf16[8,64,1024]{2,1,0:T(8,128)(2,1)S(1)} %broadcast_in_dim.4), channel_id=1, replica_groups=mesh['dp'=8,'y'=8,'core'=2,'mp'=4] {'y'}, dimensions={0} | all-to-all | bytes 2097152 | tf_op jit(solution)/shard_map/all_to_all | solution.py:30
  35.9 5.6 %collective-permute-start = (bf16[512,1024]{1,0:T(8,128)(2,1)S(1)}, bf16[512,1024]{1,0:T(8,128)(2,1)S(1)}, u32[]{:S(2)}, u32[]{:S(2)}) collective-permute-start(bf16[512,1024]{1,0:T(8,128)(2,1)S(1)} %bitcast.13), channel_id=1, source_target_pairs={{0,4},{4,0},{1,5},{5,1},{2,6},{6,2},{3,7},{7,3},{8,12},{12,8},{9,1... | collective-permute-start | bytes 3145736 | tf_op jit(solution)/shard_map/ppermute | solution.py:31
  41.5 0.0 copy-done.2
  41.5 0.0 copy-done.3
  41.5 2.2 %collective-permute-done = bf16[512,1024]{1,0:T(8,128)(2,1)S(1)} collective-permute-done((bf16[512,1024]{1,0:T(8,128)(2,1)S(1)}, bf16[512,1024]{1,0:T(8,128)(2,1)S(1)}, u32[]{:S(2)}, u32[]{:S(2)}) %collective-permute-start) | collective-permute-done | bytes 1048608 | tf_op jit(solution)/shard_map/ppermute | solution.py:31
  43.8 0.8 fusion.1
  44.6 2.5 %fusion.8 = bf16[1024,512]{1,0:T(8,128)(2,1)S(1)} fusion(bf16[1024,512]{1,0:T(8,128)(2,1)} %param.10, f32[1024]{0:T(1024)S(1)} %copy-done.2, bf16[512,1024]{1,0:T(8,128)(2,1)S(1)} %collective-permute-done, bf16[512,1024]{1,0:T(8,128)(2,1)S(1)} %bitcast.15), kind=kOutput, calls=%fused_computation.17 | convolution fusion | flops 1080557568 | bytes 4198400 | tf_op jit(solution)/shard_map/dot_general | solution.py:39
  47.1 0.1 fusion.11
  47.2 19.0 %all_to_all.21 = bf16[4,272,512]{2,1,0:T(8,128)(2,1)S(1)} all-to-all(bf16[4,272,512]{2,1,0:T(8,128)(2,1)S(1)} %fusion.11), channel_id=1, replica_groups=mesh['dp'=8,'y'=8,'core'=2,'mp'=4] {'mp'}, dimensions={0} | all-to-all | bytes 2228224 | tf_op jit(solution)/shard_map/all_to_all | solution.py:44
  66.2 0.2 convert_reduce_fusion
  66.5 0.3 fusion.20
  66.8 0.1 broadcast_in_dim.5
  66.9 15.9 %all_to_all.22 = bf16[4,256,512]{2,1,0:T(8,128)(2,1)S(1)} all-to-all(bf16[4,256,512]{2,1,0:T(8,128)(2,1)S(1)} %broadcast_in_dim.5), channel_id=1, replica_groups=mesh['dp'=8,'y'=8,'core'=2,'mp'=4] {'mp'}, dimensions={0} | all-to-all | bytes 2097152 | tf_op jit(solution)/shard_map/all_to_all | solution.py:51
  82.8 0.0 copy-done
  82.8 1.3 %fusion.27 = f32[1024,1024]{1,0:T(8,128)S(1)} fusion(bf16[1024,512]{1,0:T(8,128)(2,1)S(1)} %bitcast.18, bf16[512,1024]{1,0:T(8,128)(2,1)S(1)} %copy-done), kind=kOutput, calls=%fused_computation.45 | convolution fusion | flops 1073741824 | bytes 6291456 | tf_op jit(solution)/shard_map/dot_general | solution.py:53
  84.1 0.2 slice.46
  84.2 4.5 %collective-permute-start.1 = (bf16[512,1024]{1,0:T(8,128)(2,1)S(1)}, bf16[512,1024]{1,0:T(8,128)(2,1)S(1)}, u32[]{:S(2)}, u32[]{:S(2)}) collective-permute-start(bf16[512,1024]{1,0:T(8,128)(2,1)S(1)} %slice.46), channel_id=1, source_target_pairs={{0,4},{4,0},{1,5},{5,1},{2,6},{6,2},{3,7},{7,3},{8,12},{12,8},{9,1... | collective-permute-start | bytes 3145736 | tf_op jit(solution)/shard_map/ppermute | solution.py:55
  88.7 2.3 %collective-permute-done.1 = bf16[512,1024]{1,0:T(8,128)(2,1)S(1)} collective-permute-done((bf16[512,1024]{1,0:T(8,128)(2,1)S(1)}, bf16[512,1024]{1,0:T(8,128)(2,1)S(1)}, u32[]{:S(2)}, u32[]{:S(2)}) %collective-permute-start.1) | collective-permute-done | bytes 1048608 | tf_op jit(solution)/shard_map/ppermute | solution.py:55
  90.9 0.4 fusion.6
  91.3 0.0 copy-start.1
  91.3 31.8 %all_to_all.23 = bf16[8,64,1024]{2,1,0:T(8,128)(2,1)S(1)} all-to-all(bf16[8,64,1024]{2,1,0:T(8,128)(2,1)S(1)} %bitcast.16), channel_id=1, replica_groups=mesh['dp'=8,'y'=8,'core'=2,'mp'=4] {'y'}, dimensions={0} | all-to-all | bytes 2097152 | tf_op jit(solution)/shard_map/all_to_all | solution.py:57
  123.1 0.2 convert_reduce_fusion.1
  123.3 0.0 copy-done.1
  123.3 2.1 %add_convert_fusion = bf16[512,1024]{1,0:T(8,128)(2,1)} fusion(bf16[512,1024]{1,0:T(8,128)(2,1)S(1)} %copy-done.1, f32[64,1024]{1,0:T(8,128)S(1)} %convert_reduce_fusion.1, s32[64]{0:T(128)S(1)} %broadcast_subtract_fusion), kind=kOutput, calls=%fused_computation.14 | convolution fusion | flops 404258816 | bytes 2359552 | tf_op jit(solution)/shard_map/dot_general | solution.py:58
  (10 shorter events, 0.1 us)
Async XLA Ops:
  0.0 82.8 %copy-start = (bf16[512,1024]{1,0:T(8,128)(2,1)S(1)}, bf16[512,1024]{1,0:T(8,128)(2,1)}, u32[]{:S(2)}) copy-start(bf16[512,1024]{1,0:T(8,128)(2,1)} %param.11) | copy-start | bytes 3145732
  0.8 40.8 %copy-start.2 = (f32[1024]{0:T(1024)S(1)}, f32[1024]{0:T(1024)}, u32[]{:S(2)}) copy-start(f32[1024]{0:T(1024)} %param.8) | copy-start | bytes 12292
  0.8 40.8 %copy-start.3 = (bf16[1024]{0:T(1024)(128)(2,1)S(1)}, bf16[1024]{0:T(1024)(128)(2,1)}, u32[]{:S(2)}) copy-start(bf16[1024]{0:T(1024)(128)(2,1)} %param.9) | copy-start | bytes 6148
  35.9 7.9 %collective-permute-start = (bf16[512,1024]{1,0:T(8,128)(2,1)S(1)}, bf16[512,1024]{1,0:T(8,128)(2,1)S(1)}, u32[]{:S(2)}, u32[]{:S(2)}) collective-permute-start(bf16[512,1024]{1,0:T(8,128)(2,1)S(1)} %bitcast.13), channel_id=1, source_target_pairs={{0,4},{4,0},{1,5},{5,1},{2,6},{6,2},{3,7},{7,3},{8,12},{12,8},{9,1... | collective-permute-start | bytes 3145736 | tf_op jit(solution)/shard_map/ppermute | solution.py:31
  84.2 6.7 %collective-permute-start.1 = (bf16[512,1024]{1,0:T(8,128)(2,1)S(1)}, bf16[512,1024]{1,0:T(8,128)(2,1)S(1)}, u32[]{:S(2)}, u32[]{:S(2)}) collective-permute-start(bf16[512,1024]{1,0:T(8,128)(2,1)S(1)} %slice.46), channel_id=1, source_target_pairs={{0,4},{4,0},{1,5},{5,1},{2,6},{6,2},{3,7},{7,3},{8,12},{12,8},{9,1... | collective-permute-start | bytes 3145736 | tf_op jit(solution)/shard_map/ppermute | solution.py:55
  91.3 31.9 %copy-start.1 = (bf16[512,1024]{1,0:T(8,128)(2,1)S(1)}, bf16[512,1024]{1,0:T(8,128)(2,1)}, u32[]{:S(2)}) copy-start(bf16[512,1024]{1,0:T(8,128)(2,1)} %param.6) | copy-start | bytes 3145732

commit v2 on v1

v2 whole, which is shorter than its diff:
```python
import jax
import jax.numpy as jnp
from jax import lax
from jax.sharding import Mesh, PartitionSpec as P

D = 4096
ROUTED = 512
EMPTY = 31.5
LIMIT = 30.5
SCALE = 2048.0
BF = jnp.bfloat16
F16 = jnp.float16
F32 = jnp.float32
I32 = jnp.int32


def halves(value):
    high = value.astype(BF)
    return high, (value - high.astype(F32)).astype(BF)


def per_device(tokens, heavy_index, norm_gain, router, w_up, w_down):
    tok_rows, width = tokens.shape
    slots = heavy_index.shape[0]
    hidden_width = w_up.shape[1]
    chips = lax.axis_size("y")
    parts = lax.axis_size("mp")
    core = lax.axis_index("core")
    owners = 2 * chips
    used_rows = ROUTED
    chunk = used_rows // parts
    seq_rank = lax.axis_index("y") * 2 + core
    local_index = heavy_index - seq_rank * tok_rows
    token_iota = jnp.arange(tok_rows, dtype=I32)
    picker = (local_index[:, None] == token_iota[None, :]).astype(BF)
    selected = jnp.dot(picker, tokens, preferred_element_type=F32)
    selected = jnp.where(heavy_index[:, None] >= 0, selected, EMPTY)

    rows = lax.all_gather((selected * SCALE).astype(F16), ("y", "core"), tiled=True)
    rows = (rows.astype(F32) * (1.0 / SCALE)).astype(BF)

    used = (rows[:, 0].reshape(owners, slots) < LIMIT).astype(I32)
    counts = jnp.sum(used, axis=1)
    earlier = jnp.arange(owners)[None, :] < jnp.arange(owners)[:, None]
    first = jnp.sum(jnp.where(earlier, counts[None, :], 0), axis=1)
    slot_iota = jnp.arange(slots, dtype=I32)
    place = jnp.where(slot_iota[None] < counts[:, None], first[:, None] + slot_iota[None], -1)
    row_iota = jnp.arange(used_rows, dtype=I32)
    compactor = (row_iota[:, None] == place.reshape(owners * slots)[None, :]).astype(BF)
    raw = jnp.dot(compactor, rows, preferred_element_type=F32)

    square_part = jnp.sum(raw * raw, axis=1).reshape(parts, 1, chunk)
    router_part = jnp.sum(raw * (norm_gain * router.astype(F32)), axis=1).reshape(parts, 1, chunk)
    up_part = jnp.dot((raw * norm_gain).astype(BF), w_up, preferred_element_type=F32).astype(BF)
    sums = jnp.concatenate([square_part, router_part], axis=1)
    sums = jnp.pad(sums, ((0, 0), (0, 14), (0, hidden_width // 2 - chunk)))
    packed = jnp.concatenate(
        [up_part.reshape(parts, chunk, hidden_width), jnp.concatenate(halves(sums), axis=2)], axis=1
    )
    summed = jnp.sum(lax.all_to_all(packed, "mp", 0, 0, tiled=True).astype(F32), axis=0)
    sums = summed[chunk : chunk + 2].reshape(2, 2, -1).sum(axis=1)[:, :chunk]
    inverse = lax.rsqrt(sums[0] / D + 1e-06)
    scores = jax.nn.sigmoid(sums[1] * inverse)
    hidden = jax.nn.gelu(summed[:chunk] * inverse[:, None], approximate=True) * scores[:, None]
    hidden = jnp.broadcast_to(hidden.astype(BF)[None], (parts, chunk, hidden_width))
    hidden = lax.all_to_all(hidden, "mp", 0, 0, tiled=True).reshape(used_rows, hidden_width)

    pairs = place.reshape(chips, 2, slots)
    swapped = jnp.where(core == 0, pairs, pairs[:, ::-1])
    ordered = swapped.transpose(1, 0, 2).reshape(owners * slots)
    expander = (ordered[:, None] == row_iota[None, :]).astype(BF)
    hidden = jnp.dot(expander, hidden, preferred_element_type=F32).astype(BF)
    down = jnp.dot(hidden, w_down, preferred_element_type=F32)
    half = chips * slots
    away = lax.ppermute(down[half:].astype(BF), "core", [(0, 1), (1, 0)])
    chip_sum = (down[:half] + away.astype(F32)).astype(BF).reshape(chips, slots, width)
    addition = jnp.sum(lax.all_to_all(chip_sum, "y", 0, 0, tiled=True).astype(F32), axis=0)
    placed = jnp.dot(picker.T.astype(F32), addition, precision=lax.Precision.HIGHEST)
    return (tokens.astype(F32) + placed).astype(BF)


def solution(mesh):
    dp, seq, mp = mesh.devices.shape
    fine = Mesh(mesh.devices.reshape(dp, seq // 2, 2, mp), ("dp", "y", "core", "mp"))
    seq = ("y", "core")
    rows = ("dp",) + seq
    placed = (P(rows, "mp"), P(rows), P("mp"), P("mp"), P("mp", seq), P(seq, "mp"))
    return jax.shard_map(
        per_device, mesh=fine, in_specs=placed, out_specs=P(rows, "mp"), check_vma=False
    )
```

time: 126 us -> 110 us (0.87)
  blocking collectives: 100 us -> 60 us
  waiting for transfers between devices: 4.5 us -> 20.2 us
  other arithmetic: 2.68 us -> 5.92 us
  local copies, waits for them, and re-layouts: 0.4 us -> 3.15 us
  matrix products: 7.44 us -> 9.59 us
    all_to_all x3 -> x0, blocking collectives: 68.4 us -> none  [the longest x1 33.4 us: per_device(): lax.all_to_all(spread, 'y', 0, 0, tiled=True).reshape(chips * slots, width)]
    all_gather x0 -> x1, blocking collectives: none -> 29.4 us  [per_device(): lax.all_gather((selected * SCALE).astype(F16), ('y', 'core'), tiled=True)]
    all_to_all x0 -> x2, waiting for transfers between devices: none -> 17.9 us  [the longest x1 9.82 us: per_device(): lax.all_to_all(packed, 'mp', 0, 0, tiled=True).astype(F32)]
    all_to_all x0 -> x2, starting transfers between devices: none -> 6.95 us  [the longest x1 3.48 us: per_device(): lax.all_to_all(packed, 'mp', 0, 0, tiled=True).astype(F32)]
    ppermute x2 -> x1, starting transfers between devices: 10.1 us -> 4.07 us  [per_device(): away = lax.ppermute(down[half:].astype(BF), 'core', [(0, 1), (1, 0)])]
    dot_general x1, matrix products: 1.26 us -> 3.77 us  [per_device(): down = jnp.dot(hidden, w_down, preferred_element_type=F32)]
    ppermute x2 -> x1, waiting for transfers between devices: 4.5 us -> 2.26 us  [per_device(): away = lax.ppermute(down[half:].astype(BF), 'core', [(0, 1), (1, 0)])]
    dot_general x1, matrix products: 2.48 us -> 0.71 us  [per_device(): jnp.dot((raw * norm_gain).astype(BF), w_up, preferred_element_type=F32)]
  transfers between devices with their start and end apart: 2 -> 3, of which waited for: 2 -> 3; matrix products, arithmetic and copies ran while one was open for 0% -> 0% of each run, Pallas kernels for 0% -> 0%
where the time goes in v2:
time: 110 us
  blocking collectives  60 us (55%)
  waiting for transfers between devices  20.2 us (18%)
  starting transfers between devices  11 us (10%)
  matrix products  9.59 us (9%)
  other arithmetic  5.92 us (5%)
  local copies, waits for them, and re-layouts  3.15 us (3%)
    all_to_all x1, blocking collectives, per_device(): lax.all_to_all(chip_sum, 'y', 0, 0, tiled=True).astype(F32)  30.6 us
    all_gather x1, blocking collectives, per_device(): lax.all_gather((selected * SCALE).astype(F16), ('y', 'core'), tiled=True)  29.4 us
    all_to_all x1, waiting for transfers between devices, per_device(): lax.all_to_all(packed, 'mp', 0, 0, tiled=True).astype(F32)  9.82 us
    all_to_all x1, waiting for transfers between devices, per_device(): lax.all_to_all(hidden, 'mp', 0, 0, tiled=True)  8.08 us
    ppermute x1, starting transfers between devices, per_device(): away = lax.ppermute(down[half:].astype(BF), 'core', [(0, 1), (1, 0)])  4.07 us
    dot_general x1, matrix products, per_device(): down = jnp.dot(hidden, w_down, preferred_element_type=F32)  3.77 us
    all_to_all x1, starting transfers between devices, per_device(): lax.all_to_all(packed, 'mp', 0, 0, tiled=True).astype(F32)  3.48 us
    all_to_all x1, starting transfers between devices, per_device(): lax.all_to_all(hidden, 'mp', 0, 0, tiled=True)  3.47 us
  transfers between devices with their start and end apart: 3, of which 3 were waited for; matrix products, arithmetic and copies ran while one was open for 0% of the time, Pallas kernels for 0%

profile of v2, /device:TPU:1, one launch (start us, length us, event | category | flops | bytes accessed | tf_op | source)
XLA Modules:
  0.0 110.0 jit_solution(8822433515685132024)
XLA Ops:
  0.0 0.0 copy-start
  0.0 0.7 broadcast_compare_fusion
  0.8 0.7 broadcast_subtract_fusion
  1.4 1.6 %fusion.6 = f16[64,1024]{1,0:T(8,128)(2,1)S(1)} fusion(bf16[512,1024]{1,0:T(8,128)(2,1)} %param.6, pred[64]{0:T(512)(128)(4,1)S(1)} %broadcast_compare_fusion, s32[64]{0:T(128)S(1)} %broadcast_subtract_fusion), kind=kOutput, calls=%fused_computation.19 | convolution fusion | flops 67338240 | bytes 1179968 | tf_op jit(solution)/shard_map/dot_general | solution.py:36
  3.0 29.4 %all-gather.1 = f16[1024,1024]{1,0:T(8,128)(2,1)S(1)} all-gather(f16[64,1024]{1,0:T(8,128)(2,1)S(1)} %fusion.6), channel_id=1, replica_groups=mesh['dp'=8,'y'=8,'core'=2,'mp'=4] {'y','core'}, dimensions={0}, use_global_device_ids=true | all-gather | bytes 2228224 | tf_op jit(solution)/shard_map/all_gather | solution.py:39
  32.4 0.0 copy-start.3
  32.4 0.0 copy-start.4
  32.4 0.6 multiply_convert_fusion
  32.9 0.2 convert_reduce_fusion.2
  33.2 0.1 reshape.110
  33.2 0.1 reduce_sum.63
  33.4 0.1 select_reduce_fusion
  33.5 0.1 add_select_fusion
  33.5 0.1 select_n.36
  33.6 0.0 copy-done.3
  33.6 0.0 copy-done.4
  33.6 0.0 copy-start.2
  33.6 1.4 %multiply_reduce_fusion.1 = (f32[512]{0:T(512)S(1)}, f32[512]{0:T(512)S(1)}, f32[512,1024]{1,0:T(8,128)S(1)}) fusion(f32[1024]{0:T(1024)S(1)} %convert_multiply_fusion, f16[1024,1024]{1,0:T(8,128)(2,1)S(1)} %all-gather.1, s32[1024]{0:T(1024)S(1)} %select_n.36), kind=kOutput, calls=%fused_computation.7 | convolution fusion | flops 1079507968 | bytes 4206592 | tf_op jit(solution)/shard_map/dot_general | solution.py:50
  35.1 0.0 copy-done.2
  35.1 0.7 convolution_convert_fusion
  35.8 0.9 maximum_maximum_fusion
  36.7 3.5 %all-to-all-start = ((bf16[4,144,512]{2,1,0:T(8,128)(2,1)}), bf16[4,144,512]{2,1,0:T(8,128)(2,1)S(1)}, u32[]{:S(2)}, u32[]{:S(2)}) async-start(bf16[4,144,512]{2,1,0:T(8,128)(2,1)} %maximum_maximum_fusion), calls=%async_computation | async-start | bytes 1179648 | tf_op jit(solution)/shard_map/all_to_all | solution.py:60
  40.2 0.1 add.65
  40.3 0.1 lt.58
  40.4 0.1 copy.10
  40.4 0.1 copy.9
  40.5 9.8 %all-to-all-done = bf16[4,144,512]{2,1,0:T(8,128)(2,1)S(1)} async-done(((bf16[4,144,512]{2,1,0:T(8,128)(2,1)}), bf16[4,144,512]{2,1,0:T(8,128)(2,1)S(1)}, u32[]{:S(2)}, u32[]{:S(2)}) %all-to-all-start) | async-done | bytes 589856 | tf_op jit(solution)/shard_map/all_to_all | solution.py:60
  50.3 0.1 convert_reduce_fusion.1
  50.5 0.2 fusion.19
  50.7 0.8 broadcast_in_dim.58
  51.5 3.5 %all-to-all-start.1 = ((bf16[4,128,512]{2,1,0:T(8,128)(2,1)}), bf16[4,128,512]{2,1,0:T(8,128)(2,1)S(1)}, u32[]{:S(2)}, u32[]{:S(2)}) async-start(bf16[4,128,512]{2,1,0:T(8,128)(2,1)} %broadcast_in_dim.58), calls=%async_computation.1 | async-start | bytes 1048576 | tf_op jit(solution)/shard_map/all_to_all | solution.py:66
  55.0 0.1 add_select_fusion.1
  55.1 0.1 eq.48
  55.2 8.1 %all-to-all-done.1 = bf16[4,128,512]{2,1,0:T(8,128)(2,1)S(1)} async-done(((bf16[4,128,512]{2,1,0:T(8,128)(2,1)}), bf16[4,128,512]{2,1,0:T(8,128)(2,1)S(1)}, u32[]{:S(2)}, u32[]{:S(2)}) %all-to-all-start.1) | async-done | bytes 524320 | tf_op jit(solution)/shard_map/all_to_all | solution.py:66
  63.2 0.0 copy-done
  63.3 3.8 %fusion.4 = f32[1024,1024]{1,0:T(8,128)} fusion(bf16[512,1024]{1,0:T(8,128)(2,1)S(1)} %copy-done, bf16[512,512]{1,0:T(8,128)(2,1)S(1)} %bitcast.26, s32[1024]{0:T(1024)S(1)} %eq.48), kind=kOutput, calls=%fused_computation.14 | convolution fusion | flops 1611661312 | bytes 5771264 | tf_op jit(solution)/shard_map/dot_general | solution.py:73
  67.0 1.7 %slice.63 = bf16[512,1024]{1,0:T(8,128)(2,1)S(1)} slice(f32[1024,1024]{1,0:T(8,128)} %fusion.4), slice={[512:1024], [0:1024]} | slice | bytes 2097152 | tf_op jit(solution)/shard_map/slice | solution.py:75
  68.8 4.1 %collective-permute-start = (bf16[512,1024]{1,0:T(8,128)(2,1)S(1)}, bf16[512,1024]{1,0:T(8,128)(2,1)S(1)}, u32[]{:S(2)}, u32[]{:S(2)}) collective-permute-start(bf16[512,1024]{1,0:T(8,128)(2,1)S(1)} %slice.63), channel_id=1, source_target_pairs={{0,4},{4,0},{1,5},{5,1},{2,6},{6,2},{3,7},{7,3},{8,12},{12,8},{9,1... | collective-permute-start | bytes 3145736 | tf_op jit(solution)/shard_map/ppermute | solution.py:75
  72.8 2.3 %collective-permute-done = bf16[512,1024]{1,0:T(8,128)(2,1)S(1)} collective-permute-done((bf16[512,1024]{1,0:T(8,128)(2,1)S(1)}, bf16[512,1024]{1,0:T(8,128)(2,1)S(1)}, u32[]{:S(2)}, u32[]{:S(2)}) %collective-permute-start) | collective-permute-done | bytes 1048608 | tf_op jit(solution)/shard_map/ppermute | solution.py:75
  75.1 2.0 %fusion = bf16[512,1024]{1,0:T(8,128)(2,1)S(1)} fusion(f32[1024,1024]{1,0:T(8,128)} %fusion.4, bf16[512,1024]{1,0:T(8,128)(2,1)S(1)} %collective-permute-done), kind=kLoop, calls=%fused_computation.3 | loop fusion | flops 1572864 | bytes 4194304 | tf_op jit(solution)/shard_map/convert_element_type | solution.py:76
  77.1 0.0 copy-start.1
  77.1 30.6 %all_to_all.15 = bf16[8,64,1024]{2,1,0:T(8,128)(2,1)S(1)} all-to-all(bf16[8,64,1024]{2,1,0:T(8,128)(2,1)S(1)} %bitcast.24), channel_id=1, replica_groups=mesh['dp'=8,'y'=8,'core'=2,'mp'=4] {'y'}, dimensions={0} | all-to-all | bytes 2097152 | tf_op jit(solution)/shard_map/all_to_all | solution.py:77
  107.7 0.2 convert_reduce_fusion
  107.9 0.0 copy-done.1
  107.9 2.1 %add_convert_fusion = bf16[512,1024]{1,0:T(8,128)(2,1)} fusion(bf16[512,1024]{1,0:T(8,128)(2,1)S(1)} %copy-done.1, f32[64,1024]{1,0:T(8,128)S(1)} %convert_reduce_fusion, s32[64]{0:T(128)S(1)} %broadcast_subtract_fusion), kind=kOutput, calls=%fused_computation.4 | convolution fusion | flops 404258816 | bytes 2359552 | tf_op jit(solution)/shard_map/dot_general | solution.py:78
  (9 shorter events, 0.1 us)
Async XLA Ops:
  0.0 63.3 %copy-start = (bf16[512,1024]{1,0:T(8,128)(2,1)S(1)}, bf16[512,1024]{1,0:T(8,128)(2,1)}, u32[]{:S(2)}) copy-start(bf16[512,1024]{1,0:T(8,128)(2,1)} %param.11) | copy-start | bytes 3145732
  32.4 1.2 %copy-start.3 = (f32[1024]{0:T(1024)S(1)}, f32[1024]{0:T(1024)}, u32[]{:S(2)}) copy-start(f32[1024]{0:T(1024)} %param.8) | copy-start | bytes 12292
  32.4 1.2 %copy-start.4 = (bf16[1024]{0:T(1024)(128)(2,1)S(1)}, bf16[1024]{0:T(1024)(128)(2,1)}, u32[]{:S(2)}) copy-start(bf16[1024]{0:T(1024)(128)(2,1)} %param.9) | copy-start | bytes 6148
  33.6 1.5 %copy-start.2 = (bf16[1024,512]{1,0:T(8,128)(2,1)S(1)}, bf16[1024,512]{1,0:T(8,128)(2,1)}, u32[]{:S(2)}) copy-start(bf16[1024,512]{1,0:T(8,128)(2,1)} %param.10) | copy-start | bytes 3145732
  36.7 13.6 %all-to-all-start = ((bf16[4,144,512]{2,1,0:T(8,128)(2,1)}), bf16[4,144,512]{2,1,0:T(8,128)(2,1)S(1)}, u32[]{:S(2)}, u32[]{:S(2)}) async-start(bf16[4,144,512]{2,1,0:T(8,128)(2,1)} %maximum_maximum_fusion), calls=%async_computation | async-start | bytes 1179648 | tf_op jit(solution)/shard_map/all_to_all | solution.py:60
  51.5 11.7 %all-to-all-start.1 = ((bf16[4,128,512]{2,1,0:T(8,128)(2,1)}), bf16[4,128,512]{2,1,0:T(8,128)(2,1)S(1)}, u32[]{:S(2)}, u32[]{:S(2)}) async-start(bf16[4,128,512]{2,1,0:T(8,128)(2,1)} %broadcast_in_dim.58), calls=%async_computation.1 | async-start | bytes 1048576 | tf_op jit(solution)/shard_map/all_to_all | solution.py:66
  68.8 6.3 %collective-permute-start = (bf16[512,1024]{1,0:T(8,128)(2,1)S(1)}, bf16[512,1024]{1,0:T(8,128)(2,1)S(1)}, u32[]{:S(2)}, u32[]{:S(2)}) collective-permute-start(bf16[512,1024]{1,0:T(8,128)(2,1)S(1)} %slice.63), channel_id=1, source_target_pairs={{0,4},{4,0},{1,5},{5,1},{2,6},{6,2},{3,7},{7,3},{8,12},{12,8},{9,1... | collective-permute-start | bytes 3145736 | tf_op jit(solution)/shard_map/ppermute | solution.py:75
  77.1 30.8 %copy-start.1 = (bf16[512,1024]{1,0:T(8,128)(2,1)S(1)}, bf16[512,1024]{1,0:T(8,128)(2,1)}, u32[]{:S(2)}) copy-start(bf16[512,1024]{1,0:T(8,128)(2,1)} %param.6) | copy-start | bytes 3145732

commit v3 on v2

--- a/solution.py
+++ b/solution.py
@@ -34,13 +34,12 @@
     token_iota = jnp.arange(tok_rows, dtype=I32)
     picker = (local_index[:, None] == token_iota[None, :]).astype(BF)
     selected = jnp.dot(picker, tokens, preferred_element_type=F32)
-    selected = jnp.where(heavy_index[:, None] >= 0, selected, EMPTY)
+    selected = jnp.where(local_index[:, None] >= 0, selected, EMPTY)
 
     rows = lax.all_gather((selected * SCALE).astype(F16), ("y", "core"), tiled=True)
+    marks = rows[:, :1].astype(F32).reshape(owners, slots)
+    counts = jnp.sum((marks < LIMIT * SCALE).astype(I32), axis=1)
     rows = (rows.astype(F32) * (1.0 / SCALE)).astype(BF)
-
-    used = (rows[:, 0].reshape(owners, slots) < LIMIT).astype(I32)
-    counts = jnp.sum(used, axis=1)
     earlier = jnp.arange(owners)[None, :] < jnp.arange(owners)[:, None]
     first = jnp.sum(jnp.where(earlier, counts[None, :], 0), axis=1)
     slot_iota = jnp.arange(slots, dtype=I32)
@@ -57,6 +56,10 @@
     packed = jnp.concatenate(
         [up_part.reshape(parts, chunk, hidden_width), jnp.concatenate(halves(sums), axis=2)], axis=1
     )
+    pairs = place.reshape(chips, 2, slots)
+    own_place = jnp.where(core == 0, pairs[:, 0], pairs[:, 1]).reshape(chips * slots)
+    other_place = jnp.where(core == 0, pairs[:, 1], pairs[:, 0]).reshape(chips * slots)
+    packed, own_place, other_place = lax.optimization_barrier((packed, own_place, other_place))
     summed = jnp.sum(lax.all_to_all(packed, "mp", 0, 0, tiled=True).astype(F32), axis=0)
     sums = summed[chunk : chunk + 2].reshape(2, 2, -1).sum(axis=1)[:, :chunk]
     inverse = lax.rsqrt(sums[0] / D + 1e-06)
@@ -65,17 +68,20 @@
     hidden = jnp.broadcast_to(hidden.astype(BF)[None], (parts, chunk, hidden_width))
     hidden = lax.all_to_all(hidden, "mp", 0, 0, tiled=True).reshape(used_rows, hidden_width)
 
-    pairs = place.reshape(chips, 2, slots)
-    swapped = jnp.where(core == 0, pairs, pairs[:, ::-1])
-    ordered = swapped.transpose(1, 0, 2).reshape(owners * slots)
-    expander = (ordered[:, None] == row_iota[None, :]).astype(BF)
-    hidden = jnp.dot(expander, hidden, preferred_element_type=F32).astype(BF)
-    down = jnp.dot(hidden, w_down, preferred_element_type=F32)
-    half = chips * slots
-    away = lax.ppermute(down[half:].astype(BF), "core", [(0, 1), (1, 0)])
-    chip_sum = (down[:half] + away.astype(F32)).astype(BF).reshape(chips, slots, width)
-    addition = jnp.sum(lax.all_to_all(chip_sum, "y", 0, 0, tiled=True).astype(F32), axis=0)
-    placed = jnp.dot(picker.T.astype(F32), addition, precision=lax.Precision.HIGHEST)
+    def down(places):
+        expander = (places[:, None] == row_iota[None, :]).astype(BF)
+        wanted = jnp.dot(expander, hidden, preferred_element_type=F32).astype(BF)
+        return jnp.dot(wanted, w_down, preferred_element_type=F32)
+
+    away = lax.ppermute(down(other_place).astype(BF), "core", [(0, 1), (1, 0)])
+    chip_sum = (down(own_place) + away.astype(F32)).astype(BF).reshape(chips, slots, width)
+    targets = jnp.broadcast_to(local_index[None], (chips, slots)).reshape(chips * slots)
+    chip_sum, targets = lax.optimization_barrier((chip_sum, targets))
+    terms = lax.all_to_all(chip_sum, "y", 0, 0, tiled=True).reshape(chips * slots, width)
+    placer = (targets[:, None] == token_iota[None, :]).astype(BF)
+    placed = lax.dot_general(
+        placer, terms, (((0,), (0,)), ((), ())), preferred_element_type=F32
+    )
     return (tokens.astype(F32) + placed).astype(BF)
 
 

time: 110 us -> 106 us (0.964)
  blocking collectives: 60 us -> 83.5 us
  waiting for transfers between devices: 20.2 us -> 2.52 us
  starting transfers between devices: 11 us -> 3.77 us
  other arithmetic: 5.92 us -> 1.77 us
  matrix products: 9.59 us -> 12.9 us
  local copies, waits for them, and re-layouts: 3.15 us -> 0.6 us
    all_to_all x1 -> x3, blocking collectives: 30.6 us -> 54.1 us  [the longest x1 30.6 us: per_device(): lax.all_to_all(chip_sum, 'y', 0, 0, tiled=True)]
    all_to_all x2 -> x0, waiting for transfers between devices: 17.9 us -> none  [the longest x1 9.82 us: per_device(): lax.all_to_all(packed, 'mp', 0, 0, tiled=True).astype(F32)]
    all_to_all x2 -> x0, starting transfers between devices: 6.95 us -> none  [the longest x1 3.48 us: per_device(): lax.all_to_all(packed, 'mp', 0, 0, tiled=True).astype(F32)]
    convert_element_type x3 -> x1, other arithmetic: 2.74 us -> 0.21 us  [per_device(): counts = jnp.sum((marks < LIMIT * SCALE).astype(I32), axis=1)]
    dot_general x1, matrix products: 0.71 us -> 2.57 us  [per_device(): jnp.dot((raw * norm_gain).astype(BF), w_up, preferred_element_type=F32)]
    slice x1 -> x0, local copies, waits for them, and re-layouts: 1.74 us -> none  [per_device(): away = lax.ppermute(down[half:].astype(BF), 'core', [(0, 1), (1, 0)])]
    dot_general x1, matrix products: 1.44 us -> 2.68 us  [per_device(): raw = jnp.dot(compactor, rows, preferred_element_type=F32)]
    dot_general x2 -> x3, matrix products: 5.88 us -> 6.06 us  [the longest x2 4.25 us: down(): return jnp.dot(wanted, w_down, preferred_element_type=F32)]
  transfers between devices with their start and end apart: 3 -> 1, of which waited for: 3 -> 1; matrix products, arithmetic and copies ran while one was open for 0% -> 0% of each run, Pallas kernels for 0% -> 0%
where the time goes in v3:
time: 106 us; the launch traced here: 105 us
  blocking collectives  83.5 us (79%)
  matrix products  12.9 us (12%)
  starting transfers between devices  3.77 us (4%)
  waiting for transfers between devices  2.52 us (2%)
  other arithmetic  1.77 us (2%)
    all_to_all x1, blocking collectives, per_device(): lax.all_to_all(chip_sum, 'y', 0, 0, tiled=True)  30.6 us
    all_gather x1, blocking collectives, per_device(): lax.all_gather((selected * SCALE).astype(F16), ('y', 'core'), tiled=True)  29.4 us
    all_to_all x1, blocking collectives, per_device(): lax.all_to_all(packed, 'mp', 0, 0, tiled=True).astype(F32)  12.6 us
    all_to_all x1, blocking collectives, per_device(): lax.all_to_all(hidden, 'mp', 0, 0, tiled=True)  11 us
    dot_general x2, matrix products, down(): return jnp.dot(wanted, w_down, preferred_element_type=F32)  4.25 us
    ppermute x1, starting transfers between devices, per_device(): away = lax.ppermute(down(other_place).astype(BF), 'core', [(0, 1), (1, 0)])  3.77 us
    dot_general x1, matrix products, per_device(): raw = jnp.dot(compactor, rows, preferred_element_type=F32)  2.68 us
    dot_general x1, matrix products, per_device(): jnp.dot((raw * norm_gain).astype(BF), w_up, preferred_element_type=F32)  2.57 us
  transfers between devices with their start and end apart: 1, of which 1 were waited for; matrix products, arithmetic and copies ran while one was open for 0% of the time, Pallas kernels for 0%

profile of v3, /device:TPU:1, one launch (start us, length us, event | category | flops | bytes accessed | tf_op | source)
XLA Modules:
  0.0 105.2 jit_solution(14297622816802141027)
XLA Ops:
  0.0 0.0 copy-start
  0.0 0.0 copy-start.2
  0.0 0.0 copy-start.3
  0.0 0.7 broadcast_compare_fusion
  0.8 1.6 %fusion.4 = f16[64,1024]{1,0:T(8,128)(2,1)S(1)} fusion(bf16[512,1024]{1,0:T(8,128)(2,1)} %param.6, pred[64]{0:T(512)(128)(4,1)S(1)} %get-tuple-element.19, s32[64]{0:T(128)S(1)} %get-tuple-element.20), kind=kOutput, calls=%fused_computation.17 | convolution fusion | flops 67338240 | bytes 1179968 | tf_op jit(solution)/shard_map/dot_general | solution.py:36
  2.3 29.4 %all-gather.1 = f16[1024,1024]{1,0:T(8,128)(2,1)S(1)} all-gather(f16[64,1024]{1,0:T(8,128)(2,1)S(1)} %fusion.4), channel_id=1, replica_groups=mesh['dp'=8,'y'=8,'core'=2,'mp'=4] {'y','core'}, dimensions={0}, use_global_device_ids=true | all-gather | bytes 2228224 | tf_op jit(solution)/shard_map/all_gather | solution.py:39
  31.7 0.2 convert_reduce_fusion.1
  31.9 0.1 reshape.130
  32.0 0.1 reduce_sum.54
  32.1 0.1 select_reduce_fusion
  32.2 0.1 add_select_fusion
  32.3 0.1 select_n.45
  32.4 0.0 copy-done.2
  32.4 0.0 copy-done.3
  32.4 2.7 %multiply_reduce_fusion.1 = (f32[512]{0:T(512)S(1)}, f32[512]{0:T(512)S(1)}, f32[512,1024]{1,0:T(8,128)}) fusion(f32[1024]{0:T(1024)S(1)} %convert_multiply_fusion, f16[1024,1024]{1,0:T(8,128)(2,1)S(1)} %all-gather.1, s32[1024]{0:T(1024)S(1)} %select_n.45), kind=kOutput, calls=%fused_computation.5 | convolution fusion | flops 1079507968 | bytes 4206592 | tf_op jit(solution)/shard_map/dot_general | solution.py:49
  35.1 0.1 add.67
  35.2 0.1 lt.65
  35.3 0.1 compare_select_fusion
  35.4 0.1 select_n.49
  35.5 0.1 select_n.51
  35.6 2.6 %convolution_convert_fusion.3 = bf16[512,512]{1,0:T(8,128)(2,1)S(1)} fusion(bf16[1024,512]{1,0:T(8,128)(2,1)} %param.10, f32[512,1024]{1,0:T(8,128)} %get-tuple-element.21, f32[1024]{0:T(1024)S(1)} %copy-done.2), kind=kOutput, calls=%fused_computation.12 | convolution fusion | flops 538181632 | bytes 3674112 | tf_op jit(solution)/shard_map/dot_general | solution.py:53
  38.2 12.6 %all_to_all.15 = bf16[4,144,512]{2,1,0:T(8,128)(2,1)S(1)} all-to-all(bf16[4,144,512]{2,1,0:T(8,128)(2,1)S(1)} %maximum_maximum_fusion), channel_id=1, replica_groups=mesh['dp'=8,'y'=8,'core'=2,'mp'=4] {'mp'}, dimensions={0} | all-to-all | bytes 1179648 | tf_op jit(solution)/shard_map/all_to_all | solution.py:63
  50.8 0.1 convert_reduce_fusion
  50.9 0.2 fusion.20
  51.1 11.0 %all_to_all.16 = bf16[4,128,512]{2,1,0:T(8,128)(2,1)S(1)} all-to-all(bf16[4,128,512]{2,1,0:T(8,128)(2,1)S(1)} %broadcast_in_dim.40), channel_id=1, replica_groups=mesh['dp'=8,'y'=8,'core'=2,'mp'=4] {'mp'}, dimensions={0} | all-to-all | bytes 1048576 | tf_op jit(solution)/shard_map/all_to_all | solution.py:69
  62.1 0.0 copy-done
  62.1 2.0 %convolution_convert_fusion = bf16[512,1024]{1,0:T(8,128)(2,1)} fusion(bf16[512,1024]{1,0:T(8,128)(2,1)S(1)} %copy-done, bf16[512,512]{1,0:T(8,128)(2,1)S(1)} %bitcast.28, s32[512]{0:T(512)S(1)} %select_n.51), kind=kOutput, calls=%fused_computation.9 | convolution fusion | flops 806354944 | bytes 2623488 | tf_op jit(solution)/shard_map/dot_general | solution.py:74
  64.1 3.8 %collective-permute-start = (bf16[512,1024]{1,0:T(8,128)(2,1)}, bf16[512,1024]{1,0:T(8,128)(2,1)}, u32[]{:S(2)}, u32[]{:S(2)}) collective-permute-start(bf16[512,1024]{1,0:T(8,128)(2,1)} %convolution_convert_fusion), channel_id=1, source_target_pairs={{0,4},{4,0},{1,5},{5,1},{2,6},{6,2},{3,7},{7,3},{8,12},{12,8},{9,1... | collective-permute-start | bytes 3145736 | tf_op jit(solution)/shard_map/ppermute | solution.py:76
  67.9 0.1 reshape.128
  68.0 2.5 %collective-permute-done = bf16[512,1024]{1,0:T(8,128)(2,1)} collective-permute-done((bf16[512,1024]{1,0:T(8,128)(2,1)}, bf16[512,1024]{1,0:T(8,128)(2,1)}, u32[]{:S(2)}, u32[]{:S(2)}) %collective-permute-start) | collective-permute-done | bytes 1048608 | tf_op jit(solution)/shard_map/ppermute | solution.py:76
  70.5 2.3 %add_convert_fusion.1 = bf16[512,1024]{1,0:T(8,128)(2,1)S(1)} fusion(bf16[512,1024]{1,0:T(8,128)(2,1)} %collective-permute-done, bf16[512,1024]{1,0:T(8,128)(2,1)S(1)} %copy-done, bf16[512,512]{1,0:T(8,128)(2,1)S(1)} %bitcast.29, s32[512]{0:T(512)S(1)} %select_n.49), kind=kOutput, calls=%fused_computation.3 | convolution fusion | flops 807403520 | bytes 3672064 | tf_op jit(solution)/shard_map/dot_general | solution.py:74
  72.8 0.0 copy-start.1
  72.8 30.6 %all_to_all.17 = bf16[8,64,1024]{2,1,0:T(8,128)(2,1)S(1)} all-to-all(bf16[8,64,1024]{2,1,0:T(8,128)(2,1)S(1)} %bitcast.26), channel_id=1, replica_groups=mesh['dp'=8,'y'=8,'core'=2,'mp'=4] {'y'}, dimensions={0} | all-to-all | bytes 2097152 | tf_op jit(solution)/shard_map/all_to_all | solution.py:80
  103.4 0.0 copy-done.1
  103.4 1.8 %add_convert_fusion = bf16[512,1024]{1,0:T(8,128)(2,1)} fusion(bf16[512,1024]{1,0:T(8,128)(2,1)S(1)} %copy-done.1, bf16[512,1024]{1,0:T(8,128)(2,1)S(1)} %bitcast.27, s32[512]{0:T(512)S(1)} %reshape.128), kind=kOutput, calls=%fused_computation.2 | convolution fusion | flops 538705920 | bytes 3147776 | tf_op jit(solution)/shard_map/dot_general | solution.py:82
  (12 shorter events, 0.2 us)
Async XLA Ops:
  0.0 62.1 %copy-start = (bf16[512,1024]{1,0:T(8,128)(2,1)S(1)}, bf16[512,1024]{1,0:T(8,128)(2,1)}, u32[]{:S(2)}) copy-start(bf16[512,1024]{1,0:T(8,128)(2,1)} %param.11) | copy-start | bytes 3145732
  0.0 32.4 %copy-start.2 = (f32[1024]{0:T(1024)S(1)}, f32[1024]{0:T(1024)}, u32[]{:S(2)}) copy-start(f32[1024]{0:T(1024)} %param.8) | copy-start | bytes 12292
  0.0 32.4 %copy-start.3 = (bf16[1024]{0:T(1024)(128)(2,1)S(1)}, bf16[1024]{0:T(1024)(128)(2,1)}, u32[]{:S(2)}) copy-start(bf16[1024]{0:T(1024)(128)(2,1)} %param.9) | copy-start | bytes 6148
  64.1 6.4 %collective-permute-start = (bf16[512,1024]{1,0:T(8,128)(2,1)}, bf16[512,1024]{1,0:T(8,128)(2,1)}, u32[]{:S(2)}, u32[]{:S(2)}) collective-permute-start(bf16[512,1024]{1,0:T(8,128)(2,1)} %convolution_convert_fusion), channel_id=1, source_target_pairs={{0,4},{4,0},{1,5},{5,1},{2,6},{6,2},{3,7},{7,3},{8,12},{12,8},{9,1... | collective-permute-start | bytes 3145736 | tf_op jit(solution)/shard_map/ppermute | solution.py:76
  72.8 30.6 %copy-start.1 = (bf16[512,1024]{1,0:T(8,128)(2,1)S(1)}, bf16[512,1024]{1,0:T(8,128)(2,1)}, u32[]{:S(2)}) copy-start(bf16[512,1024]{1,0:T(8,128)(2,1)} %param.6) | copy-start | bytes 3145732

commit v4 on v3

v4 whole, which is shorter than its diff:
```python
import jax
import jax.numpy as jnp
from jax import lax
from jax.sharding import Mesh, PartitionSpec as P

D = 4096
ROUTED = 512
EMPTY = 31.5
LIMIT = 30.5
SCALE = 2048.0
BF = jnp.bfloat16
F16 = jnp.float16
F32 = jnp.float32
I32 = jnp.int32
PAIR = [(0, 1), (1, 0)]


def halves(value):
    high = value.astype(BF)
    return high, (value - high.astype(F32)).astype(BF)


def per_device(tokens, heavy_index, norm_gain, router, w_up, w_down):
    tok_rows, width = tokens.shape
    slots = heavy_index.shape[0]
    hidden_width = w_up.shape[1]
    chips = lax.axis_size("yh") * 2
    parts = lax.axis_size("mp")
    core = lax.axis_index("core")
    side = lax.axis_index("yl")
    owners = 2 * chips
    share = slots // 2
    piece = -(-(ROUTED + owners) // (2 * parts * 8)) * 8
    room = parts * piece
    chunk = 2 * piece
    seq_rank = (lax.axis_index("yh") * 2 + side) * 2 + core
    local_index = heavy_index - seq_rank * tok_rows
    token_iota = jnp.arange(tok_rows, dtype=I32)
    picker = (local_index[:, None] == token_iota[None, :]).astype(BF)
    selected = jnp.dot(picker, tokens, preferred_element_type=F32)
    selected = jnp.where(local_index[:, None] >= 0, selected, EMPTY)

    rows = lax.all_gather((selected * SCALE).astype(F16), ("yh", "yl", "core"), tiled=True)
    rows, w_here = lax.optimization_barrier((rows, w_down))
    early = hidden_width * 3 // 4
    w_early = lax.ppermute(w_here[:early], "yl", PAIR)
    marks = rows[:, :1].astype(F32).reshape(owners, slots)
    counts = jnp.sum((marks < LIMIT * SCALE).astype(I32), axis=1)
    rows = (rows.astype(F32) * (1.0 / SCALE)).astype(BF)

    parity = jnp.arange(2, dtype=I32)
    number = (counts[:, None] + 1 - parity[None, :]) // 2
    earlier = jnp.arange(owners)[None, :] < jnp.arange(owners)[:, None]
    first = jnp.sum(jnp.where(earlier[:, :, None], number[None], 0), axis=1)
    share_iota = jnp.arange(share, dtype=I32)
    in_use = share_iota[None, :, None] < number[:, None, :]
    place = jnp.where(in_use, first[:, None, :] + share_iota[None, :, None], -1)
    spot = place // piece * chunk + parity[None, None, :] * piece + place % piece
    spot = jnp.where(in_use, spot, -1).reshape(owners * slots)
    row_iota = jnp.arange(parts * chunk, dtype=I32)
    compactor = (row_iota[:, None] == spot[None, :]).astype(BF)
    raw = jnp.dot(compactor, rows, preferred_element_type=BF)
    raw = raw.astype(F32)

    square_part = jnp.sum(raw * raw, axis=1).reshape(parts, 1, chunk)
    router_part = jnp.sum(raw * (norm_gain * router.astype(F32)), axis=1).reshape(parts, 1, chunk)
    up_part = jnp.dot((raw * norm_gain).astype(BF), w_up, preferred_element_type=F32).astype(BF)
    sums = jnp.concatenate([square_part, router_part], axis=1)
    sums = jnp.pad(sums, ((0, 0), (0, 14), (0, hidden_width // 2 - chunk)))
    packed = jnp.concatenate(
        [up_part.reshape(parts, chunk, hidden_width), jnp.concatenate(halves(sums), axis=2)], axis=1
    )
    mine = jnp.where(side == 0, place[:, :, 0], place[:, :, 1]).reshape(chips, 2, share)
    ordered = jnp.where(core == 0, mine, mine[:, ::-1]).transpose(1, 0, 2).reshape(owners * share)
    packed, ordered = lax.optimization_barrier((packed, ordered))
    packed = lax.all_to_all(packed, "mp", 0, 0, tiled=True)
    packed, w_early, w_rest = lax.optimization_barrier((packed, w_early, w_here[early:]))
    w_late = lax.ppermute(w_rest, "yl", PAIR)
    summed = jnp.sum(packed.astype(F32), axis=0)
    sums = summed[chunk : chunk + 2].reshape(2, 2, -1).sum(axis=1)[:, :chunk]
    inverse = lax.rsqrt(sums[0] / D + 1e-06)
    scores = jax.nn.sigmoid(sums[1] * inverse)
    hidden = jax.nn.gelu(summed[:chunk] * inverse[:, None], approximate=True) * scores[:, None]
    hidden = hidden.astype(BF).reshape(2, 1, piece, hidden_width)
    hidden = jnp.broadcast_to(hidden, (2, parts, piece, hidden_width))
    hidden = lax.all_to_all(
        hidden.reshape(2 * parts, piece, hidden_width), ("yl", "mp"), 0, 0, tiled=True
    ).reshape(2, room, hidden_width)
    here = jnp.where(side == 0, hidden[0], hidden[1])
    near = jnp.where(side == 0, hidden[1], hidden[0])

    expander = (ordered[:, None] == jnp.arange(room, dtype=I32)[None, :]).astype(BF)
    wanted = jnp.dot(
        expander, jnp.concatenate([here, near], axis=1), preferred_element_type=F32
    ).astype(BF)
    wanted = lax.optimization_barrier(wanted)
    half = chips * share

    def down(some):
        total, at = 0.0, 0
        for w in (w_down, w_early, w_late):
            upto = at + w.shape[0]
            total += jnp.dot(some[:, at:upto], w, preferred_element_type=F32)
            at = upto
        return total

    away = lax.ppermute(down(wanted[half:]).astype(BF), "core", PAIR)
    chip_sum = (down(wanted[:half]) + away.astype(F32)).astype(BF).reshape(chips, share, width)
    targets = jnp.broadcast_to(local_index.reshape(share, 2).T[None], (chips // 2, 2, share))
    chip_sum, targets = lax.optimization_barrier((chip_sum, targets.reshape(chips * share)))
    terms = lax.all_to_all(chip_sum, ("yh", "yl"), 0, 0, tiled=True).reshape(chips * share, width)
    placer = (targets[:, None] == token_iota[None, :]).astype(BF)
    placed = lax.dot_general(
        placer, terms, (((0,), (0,)), ((), ())), preferred_element_type=F32
    )
    return (tokens.astype(F32) + placed).astype(BF)


def solution(mesh):
    dp, seq, mp = mesh.devices.shape
    names = ("dp", "yh", "yl", "core", "mp")
    fine = Mesh(mesh.devices.reshape(dp, seq // 4, 2, 2, mp), names)
    seq = names[1:4]
    rows = names[:4]
    placed = (P(rows, "mp"), P(rows), P("mp"), P("mp"), P("mp", seq), P(seq, "mp"))
    return jax.shard_map(
        per_device, mesh=fine, in_specs=placed, out_specs=P(rows, "mp"), check_vma=False
    )
```

time: 106 us -> 110 us (1.038)
  blocking collectives: 83.5 us -> 50.8 us
  waiting for transfers between devices: 2.52 us -> 18.5 us
  starting transfers between devices: 3.77 us -> 16.2 us
  local copies, waits for them, and re-layouts: 0.6 us -> 4.82 us
  other arithmetic: 1.77 us -> 4.68 us
  matrix products: 12.9 us -> 14.2 us
    all_to_all x3 -> x1, blocking collectives: 54.1 us -> 20.4 us  [per_device(): lax.all_to_all(chip_sum, ('yh', 'yl'), 0, 0, tiled=True)]
    all_to_all x0 -> x2, waiting for transfers between devices: none -> 14.7 us  [the longest x1 10.1 us: per_device(): packed = lax.all_to_all(packed, 'mp', 0, 0, tiled=True)]
    all_to_all x0 -> x2, starting transfers between devices: none -> 7.02 us  [the longest x1 3.54 us: per_device(): lax.all_to_all(hidden.reshape(2 * parts, piece, hidden_width), ('yl', 'mp...]
    ppermute x1 -> x3, starting transfers between devices: 3.77 us -> 9.14 us  [the longest x1 3.94 us: per_device(): away = lax.ppermute(down(wanted[half:]).astype(BF), 'core', PAIR)]
    dot_general x3 -> x8, matrix products: 6.93 us -> 9.09 us  [the longest x6 4.22 us: down(): total += jnp.dot(some[:, at:upto], w, preferred_element_type=F32)]
    slice x0 -> x2, local copies, waits for them, and re-layouts: none -> 1.65 us  [the longest x1 0.93 us: per_device(): w_early = lax.ppermute(w_here[:early], 'yl', PAIR)]
    ppermute x1 -> x3, waiting for transfers between devices: 2.52 us -> 3.82 us  [the longest x1 3.81 us: per_device(): w_late = lax.ppermute(w_rest, 'yl', PAIR)]
  transfers between devices with their start and end apart: 1 -> 5, of which waited for: 1 -> 3; matrix products, arithmetic and copies ran while one was open for 0% -> 13% of each run, Pallas kernels for 0% -> 0%
where the time goes in v4:
time: 110 us
  blocking collectives  50.8 us (46%)
  waiting for transfers between devices  18.5 us (17%)
  starting transfers between devices  16.2 us (15%)
  matrix products  14.2 us (13%)
  local copies, waits for them, and re-layouts  4.82 us (4%)
  other arithmetic  4.68 us (4%)
    all_gather x1, blocking collectives, per_device(): lax.all_gather((selected * SCALE).astype(F16), ('yh', 'yl', 'core'), tile...  30.4 us
    all_to_all x1, blocking collectives, per_device(): lax.all_to_all(chip_sum, ('yh', 'yl'), 0, 0, tiled=True)  20.4 us
    all_to_all x1, waiting for transfers between devices, per_device(): packed = lax.all_to_all(packed, 'mp', 0, 0, tiled=True)  10.1 us
    all_to_all x1, waiting for transfers between devices, per_device(): lax.all_to_all(hidden.reshape(2 * parts, piece, hidden_width), ('yl', 'mp...  4.59 us
    dot_general x6, matrix products, down(): total += jnp.dot(some[:, at:upto], w, preferred_element_type=F32)  4.22 us
    dot_general x1, matrix products, per_device(): raw = jnp.dot(compactor, rows, preferred_element_type=BF)  4.11 us
    ppermute x1, starting transfers between devices, per_device(): away = lax.ppermute(down(wanted[half:]).astype(BF), 'core', PAIR)  3.94 us
    ppermute x1, waiting for transfers between devices, per_device(): w_late = lax.ppermute(w_rest, 'yl', PAIR)  3.81 us
  transfers between devices with their start and end apart: 5, of which 3 were waited for; matrix products, arithmetic and copies ran while one was open for 13% of the time, Pallas kernels for 0%

profile of v4, /device:TPU:1, one launch (start us, length us, event | category | flops | bytes accessed | tf_op | source)
XLA Modules:
  0.0 109.5 jit_solution(15889272490327398643)
XLA Ops:
  0.0 0.8 broadcast_compare_fusion
  0.8 1.6 %fusion.14 = f16[64,1024]{1,0:T(8,128)(2,1)S(1)} fusion(bf16[512,1024]{1,0:T(8,128)(2,1)} %param.6, pred[64]{0:T(512)(128)(4,1)S(1)} %get-tuple-element.25, s32[64]{0:T(128)S(1)} %get-tuple-element.26), kind=kOutput, calls=%fused_computation.25 | convolution fusion | flops 67338240 | bytes 1179968 | tf_op jit(solution)/shard_map/dot_general | solution.py:40
  2.4 30.4 %all-gather.1 = f16[1024,1024]{1,0:T(8,128)(2,1)} all-gather(f16[64,1024]{1,0:T(8,128)(2,1)S(1)} %fusion.14), channel_id=1, replica_groups=mesh['dp'=8,'yh'=4,'yl'=2,'core'=2,'mp'=4] {'yh','yl','core'}, dimensions={0}, use_global_device_ids=true | all-gather | bytes 2228224 | tf_op jit(solution)/shard_map/all_gather | solution.py:43
  32.8 0.9 slice.69
  33.8 1.9 %collective-permute-start = (bf16[384,1024]{1,0:T(8,128)(2,1)}, bf16[384,1024]{1,0:T(8,128)(2,1)S(1)}, u32[]{:S(2)}, u32[]{:S(2)}) collective-permute-start(bf16[384,1024]{1,0:T(8,128)(2,1)} %slice.69), channel_id=1, source_target_pairs={{0,8},{8,0},{1,9},{9,1},{2,10},{10,2},{3,11},{11,3},{4,12},{12,4},... | collective-permute-start | bytes 2359304 | tf_op jit(solution)/shard_map/ppermute | solution.py:46
  35.7 1.2 %convert_reduce_fusion.1 = s32[1024]{0:T(1024)S(1)} fusion(f16[1024,1024]{1,0:T(8,128)(2,1)} %all-gather.1), kind=kLoop, calls=%fused_computation.31 | loop fusion | flops 3072 | bytes 6144 | tf_op jit(solution)/shard_map/convert_element_type | solution.py:48
  36.9 0.1 reshape.232
  36.9 0.1 reduce_sum.54
  37.1 0.1 iota_compare_fusion.10
  37.2 0.1 select_reduce_fusion
  37.3 0.1 broadcast_select_fusion.2
  37.4 0.2 copy.14
  37.5 0.2 add.132
  37.7 0.2 copy.13
  37.9 0.2 lt.61
  38.1 0.2 add.134
  38.4 4.1 %fusion.1 = (f32[576]{0:T(1024)S(1)}, f32[576]{0:T(1024)S(1)}, bf16[576,1024]{1,0:T(8,128)(2,1)}) fusion(f32[1024]{0:T(1024)S(1)} %convert_multiply_fusion.3, f16[1024,1024]{1,0:T(8,128)(2,1)} %all-gather.1, s32[1024]{0:T(1024)S(1)} %fusion.44), kind=kOutput, calls=%fused_computation.5 | convolution fusion | flops 1214643200 | bytes 3289600 | tf_op jit(solution)/shard_map/dot_general | solution.py:62
  42.5 0.1 reshape.223
  42.6 0.1 reshape.224
  42.7 2.0 %convolution_convert_fusion.1 = bf16[576,512]{1,0:T(8,128)(2,1)S(1)} fusion(bf16[1024,512]{1,0:T(8,128)(2,1)S(1)} %copy-done, bf16[576,1024]{1,0:T(8,128)(2,1)} %get-tuple-element.33, f32[1024]{0:T(1024)S(1)} %copy-done.4), kind=kOutput, calls=%fused_computation.17 | convolution fusion | flops 606044160 | bytes 2822144 | tf_op jit(solution)/shard_map/dot_general | solution.py:67
  44.8 0.1 reshape.225
  44.9 0.9 maximum_maximum_fusion
  45.8 3.5 %all-to-all-start = ((bf16[4,160,512]{2,1,0:T(8,128)(2,1)}), bf16[4,160,512]{2,1,0:T(8,128)(2,1)S(1)}, u32[]{:S(2)}, u32[]{:S(2)}) async-start(bf16[4,160,512]{2,1,0:T(8,128)(2,1)} %maximum_maximum_fusion), calls=%async_computation | async-start | bytes 1310720 | tf_op jit(solution)/shard_map/all_to_all | solution.py:76
  49.3 0.7 slice.70
  50.0 10.1 %all-to-all-done = bf16[4,160,512]{2,1,0:T(8,128)(2,1)S(1)} async-done(((bf16[4,160,512]{2,1,0:T(8,128)(2,1)}), bf16[4,160,512]{2,1,0:T(8,128)(2,1)S(1)}, u32[]{:S(2)}, u32[]{:S(2)}) %all-to-all-start) | async-done | bytes 655392 | tf_op jit(solution)/shard_map/all_to_all | solution.py:76
  60.1 0.1 convert_reduce_fusion
  60.2 0.0 copy-start.3
  60.2 0.7 copy-done.3
  61.0 1.2 %fusion.27 = bf16[144,512]{1,0:T(8,128)(2,1)S(1)} fusion(f32[160,512]{1,0:T(8,128)} %copy-done.3, f32[144]{0:T(256)S(1)} %add_divide_fusion, f32[144]{0:T(256)S(1)} %bitcast.33), kind=kLoop, calls=%fused_computation.44 | loop fusion | flops 811008 | bytes 443520 | tf_op jit(solution)/shard_map/convert_element_type | solution.py:84
  62.2 0.9 broadcast_in_dim.53
  63.0 3.5 %all-to-all-start.1 = ((bf16[8,72,512]{2,1,0:T(8,128)(2,1)}), bf16[8,72,512]{2,1,0:T(8,128)(2,1)S(1)}, u32[]{:S(2)}, u32[]{:S(2)}) async-start(bf16[8,72,512]{2,1,0:T(8,128)(2,1)} %bitcast.22), calls=%async_computation.1 | async-start | bytes 1179648 | tf_op jit(solution)/shard_map/all_to_all | solution.py:86
  66.6 0.1 reshape.229
  66.7 0.1 copy.16
  66.8 0.1 reshape.230
  66.8 3.3 %collective-permute-start.1 = (bf16[128,1024]{1,0:T(8,128)(2,1)}, bf16[128,1024]{1,0:T(8,128)(2,1)}, u32[]{:S(2)}, u32[]{:S(2)}) collective-permute-start(bf16[128,1024]{1,0:T(8,128)(2,1)} %slice.70), channel_id=1, source_target_pairs={{0,8},{8,0},{1,9},{9,1},{2,10},{10,2},{3,11},{11,3},{4,12},{12,4},... | collective-permute-start | bytes 786440 | tf_op jit(solution)/shard_map/ppermute | solution.py:78
  70.1 4.6 %all-to-all-done.1 = bf16[8,72,512]{2,1,0:T(8,128)(2,1)S(1)} async-done(((bf16[8,72,512]{2,1,0:T(8,128)(2,1)}), bf16[8,72,512]{2,1,0:T(8,128)(2,1)S(1)}, u32[]{:S(2)}, u32[]{:S(2)}) %all-to-all-start.1) | async-done | bytes 589856 | tf_op jit(solution)/shard_map/all_to_all | solution.py:86
  74.8 0.8 convolution_convert_fusion
  75.5 0.4 fusion.28
  76.0 3.8 %collective-permute-done.1 = bf16[128,1024]{1,0:T(8,128)(2,1)} collective-permute-done((bf16[128,1024]{1,0:T(8,128)(2,1)}, bf16[128,1024]{1,0:T(8,128)(2,1)}, u32[]{:S(2)}, u32[]{:S(2)}) %collective-permute-start.1) | collective-permute-done | bytes 262176 | tf_op jit(solution)/shard_map/ppermute | solution.py:78
  79.8 1.2 %fusion.35 = f32[256,1024]{1,0:T(8,128)S(1)} fusion(bf16[128,1024]{1,0:T(8,128)(2,1)} %collective-permute-done.1, bf16[512,1024]{1,0:T(8,128)(2,1)S(1)} %convolution_convert_fusion), kind=kOutput, calls=%fused_computation.56 | convolution fusion | flops 67108864 | bytes 1376256 | tf_op jit(solution)/shard_map/dot_general | solution.py:103
  81.0 0.4 fusion.8
  81.5 3.9 %collective-permute-start.2 = (bf16[256,1024]{1,0:T(8,128)(2,1)S(1)}, bf16[256,1024]{1,0:T(8,128)(2,1)S(1)}, u32[]{:S(2)}, u32[]{:S(2)}) collective-permute-start(bf16[256,1024]{1,0:T(8,128)(2,1)S(1)} %fusion.8), channel_id=1, source_target_pairs={{0,4},{4,0},{1,5},{5,1},{2,6},{6,2},{3,7},{7,3},{8,12},{12,8},{9,1... | collective-permute-start | bytes 1572872 | tf_op jit(solution)/shard_map/ppermute | solution.py:107
  85.4 1.2 %fusion.37 = f32[256,1024]{1,0:T(8,128)S(1)} fusion(bf16[128,1024]{1,0:T(8,128)(2,1)} %collective-permute-done.1, bf16[512,1024]{1,0:T(8,128)(2,1)S(1)} %convolution_convert_fusion), kind=kOutput, calls=%fused_computation.58 | convolution fusion | flops 67108864 | bytes 1376256 | tf_op jit(solution)/shard_map/dot_general | solution.py:103
  86.7 0.4 fusion.30
  87.1 0.0 copy-start.2
  87.1 0.5 fusion.9
  87.6 20.4 %all_to_all.15 = bf16[8,32,1024]{2,1,0:T(8,128)(2,1)S(1)} all-to-all(bf16[8,32,1024]{2,1,0:T(8,128)(2,1)S(1)} %bitcast.24), channel_id=1, replica_groups=mesh['dp'=8,'yh'=4,'yl'=2,'core'=2,'mp'=4] {'yh','yl'}, dimensions={0} | all-to-all | bytes 1048576 | tf_op jit(solution)/shard_map/all_to_all | solution.py:111
  108.0 1.5 %add_convert_fusion = bf16[512,1024]{1,0:T(8,128)(2,1)} fusion(bf16[512,1024]{1,0:T(8,128)(2,1)S(1)} %copy-done.2, bf16[256,1024]{1,0:T(8,128)(2,1)S(1)} %bitcast.23, s32[256]{0:T(256)S(1)} %reshape.230), kind=kOutput, calls=%fused_computation.9 | convolution fusion | flops 270139392 | bytes 2622464 | tf_op jit(solution)/shard_map/dot_general | solution.py:113
  (31 shorter events, 0.3 us)
Async XLA Ops:
  0.0 42.7 %copy-start = (bf16[1024,512]{1,0:T(8,128)(2,1)S(1)}, bf16[1024,512]{1,0:T(8,128)(2,1)}, u32[]{:S(2)}) copy-start(bf16[1024,512]{1,0:T(8,128)(2,1)} %param.10) | copy-start | bytes 3145732
  0.0 32.8 %copy-start.1 = (bf16[512,1024]{1,0:T(8,128)(2,1)S(1)}, bf16[512,1024]{1,0:T(8,128)(2,1)}, u32[]{:S(2)}) copy-start(bf16[512,1024]{1,0:T(8,128)(2,1)} %param.11) | copy-start | bytes 3145732
  32.8 5.5 %copy-start.4 = (f32[1024]{0:T(1024)S(1)}, f32[1024]{0:T(1024)}, u32[]{:S(2)}) copy-start(f32[1024]{0:T(1024)} %param.8) | copy-start | bytes 12292
  32.8 5.5 %copy-start.5 = (bf16[1024]{0:T(1024)(128)(2,1)S(1)}, bf16[1024]{0:T(1024)(128)(2,1)}, u32[]{:S(2)}) copy-start(bf16[1024]{0:T(1024)(128)(2,1)} %param.9) | copy-start | bytes 6148
  33.8 26.4 %collective-permute-start = (bf16[384,1024]{1,0:T(8,128)(2,1)}, bf16[384,1024]{1,0:T(8,128)(2,1)S(1)}, u32[]{:S(2)}, u32[]{:S(2)}) collective-permute-start(bf16[384,1024]{1,0:T(8,128)(2,1)} %slice.69), channel_id=1, source_target_pairs={{0,8},{8,0},{1,9},{9,1},{2,10},{10,2},{3,11},{11,3},{4,12},{12,4},... | collective-permute-start | bytes 2359304 | tf_op jit(solution)/shard_map/ppermute | solution.py:46
  45.8 14.3 %all-to-all-start = ((bf16[4,160,512]{2,1,0:T(8,128)(2,1)}), bf16[4,160,512]{2,1,0:T(8,128)(2,1)S(1)}, u32[]{:S(2)}, u32[]{:S(2)}) async-start(bf16[4,160,512]{2,1,0:T(8,128)(2,1)} %maximum_maximum_fusion), calls=%async_computation | async-start | bytes 1310720 | tf_op jit(solution)/shard_map/all_to_all | solution.py:76
  60.2 0.7 copy-start.3
  63.0 11.7 %all-to-all-start.1 = ((bf16[8,72,512]{2,1,0:T(8,128)(2,1)}), bf16[8,72,512]{2,1,0:T(8,128)(2,1)S(1)}, u32[]{:S(2)}, u32[]{:S(2)}) async-start(bf16[8,72,512]{2,1,0:T(8,128)(2,1)} %bitcast.22), calls=%async_computation.1 | async-start | bytes 1179648 | tf_op jit(solution)/shard_map/all_to_all | solution.py:86
  66.8 13.0 %collective-permute-start.1 = (bf16[128,1024]{1,0:T(8,128)(2,1)}, bf16[128,1024]{1,0:T(8,128)(2,1)}, u32[]{:S(2)}, u32[]{:S(2)}) collective-permute-start(bf16[128,1024]{1,0:T(8,128)(2,1)} %slice.70), channel_id=1, source_target_pairs={{0,8},{8,0},{1,9},{9,1},{2,10},{10,2},{3,11},{11,3},{4,12},{12,4},... | collective-permute-start | bytes 786440 | tf_op jit(solution)/shard_map/ppermute | solution.py:78
  81.5 5.6 %collective-permute-start.2 = (bf16[256,1024]{1,0:T(8,128)(2,1)S(1)}, bf16[256,1024]{1,0:T(8,128)(2,1)S(1)}, u32[]{:S(2)}, u32[]{:S(2)}) collective-permute-start(bf16[256,1024]{1,0:T(8,128)(2,1)S(1)} %fusion.8), channel_id=1, source_target_pairs={{0,4},{4,0},{1,5},{5,1},{2,6},{6,2},{3,7},{7,3},{8,12},{12,8},{9,1... | collective-permute-start | bytes 1572872 | tf_op jit(solution)/shard_map/ppermute | solution.py:107
  87.1 20.9 %copy-start.2 = (bf16[512,1024]{1,0:T(8,128)(2,1)S(1)}, bf16[512,1024]{1,0:T(8,128)(2,1)}, u32[]{:S(2)}) copy-start(bf16[512,1024]{1,0:T(8,128)(2,1)} %param.6) | copy-start | bytes 3145732

commit v5 on v3

v5 whole, which is shorter than its diff:
```python
import functools

import jax
import jax.numpy as jnp
from jax import lax
from jax.experimental import pallas as pl
from jax.experimental.pallas import tpu as pltpu
from jax.sharding import Mesh, PartitionSpec as P

D = 4096
ROUTED = 512
EMPTY = 31.5
LIMIT = 30.5
SCALE = 2048.0
BF = jnp.bfloat16
F16 = jnp.float16
F32 = jnp.float32
I32 = jnp.int32


def iota(shape, axis):
    return lax.broadcasted_iota(I32, shape, axis)


def up_kernel(slots, core_ref, rows_ref, gain_ref, route_ref, w_ref, out_ref, place_ref):
    count = rows_ref.shape[0]
    parts, chunk = out_ref.shape[:2]
    total = parts * chunk
    hidden_width = w_ref.shape[1]
    core = core_ref[0]
    pick = (iota((8, 128), 1) == 0).astype(BF)
    marks = lax.dot_general(
        pick, rows_ref[:, :128], (((1,), (1,)), ((), ())), preferred_element_type=F32
    )
    used = (marks < LIMIT).astype(F32).astype(BF)
    owner = (iota((count, 128), 0) // slots == iota((count, 128), 1)).astype(BF)
    numbers = jnp.dot(used, owner, preferred_element_type=F32).astype(BF)

    def places(owner_of, length):
        lanes = iota((128, length), 0)
        before = (lanes < owner_of((128, length))).astype(BF)
        same = (lanes == owner_of((128, length))).astype(BF)
        first = jnp.dot(numbers, before, preferred_element_type=F32).astype(I32)
        number = jnp.dot(numbers, same, preferred_element_type=F32).astype(I32)
        slot = iota((8, length), 1) % slots
        return jnp.where(slot < number, first + slot, -1)

    place = places(lambda shape: iota(shape, 1) // slots, count)
    half = count // 2
    place_ref[:8] = places(lambda shape: iota(shape, 1) // slots * 2 + core, half)
    place_ref[8:] = places(lambda shape: iota(shape, 1) // slots * 2 + (1 - core), half)

    compactor = (iota((total, count), 0) == place[:1]).astype(F32).astype(BF)
    raw = jnp.dot(compactor, rows_ref[...], preferred_element_type=F32)
    square = jnp.sum(raw * raw, axis=1, keepdims=True)
    route = jnp.sum(raw * route_ref[...], axis=1, keepdims=True)
    up_part = jnp.dot((raw * gain_ref[...]).astype(BF), w_ref[...], preferred_element_type=F32)
    out_ref[:, :, :hidden_width] = up_part.astype(BF).reshape(parts, chunk, hidden_width)
    square_high = square.astype(BF).astype(F32)
    route_high = route.astype(BF).astype(F32)
    lane = iota((total, 128), 1)
    sums = jnp.where(lane == 0, square_high, 0.0)
    sums = jnp.where(lane == 1, square - square_high, sums)
    sums = jnp.where(lane == 2, route_high, sums)
    sums = jnp.where(lane == 3, route - route_high, sums)
    out_ref[:, :, hidden_width:] = sums.astype(BF).reshape(parts, chunk, 128)


def up_call(core, rows, gain, route, w_up, slots, parts):
    vmem = pl.BlockSpec(memory_space=pltpu.VMEM)
    return pl.pallas_call(
        functools.partial(up_kernel, slots),
        out_shape=(
            jax.ShapeDtypeStruct((parts, ROUTED // parts, w_up.shape[1] + 128), BF),
            jax.ShapeDtypeStruct((16, rows.shape[0] // 2), I32),
        ),
        in_specs=[pl.BlockSpec(memory_space=pltpu.SMEM)] + [vmem] * 4,
        out_specs=(vmem, vmem),
        compiler_params=pltpu.CompilerParams(vmem_limit_bytes=40 * 1024 * 1024),
    )(core.reshape(1), rows, gain, route, w_up)


def per_device(tokens, heavy_index, norm_gain, router, w_up, w_down):
    tok_rows, width = tokens.shape
    slots = heavy_index.shape[0]
    hidden_width = w_up.shape[1]
    chips = lax.axis_size("y")
    parts = lax.axis_size("mp")
    core = lax.axis_index("core")
    used_rows = ROUTED
    chunk = used_rows // parts
    seq_rank = lax.axis_index("y") * 2 + core
    local_index = heavy_index - seq_rank * tok_rows
    token_iota = jnp.arange(tok_rows, dtype=I32)
    picker = (local_index[:, None] == token_iota[None, :]).astype(BF)
    selected = jnp.dot(picker, tokens, preferred_element_type=F32)
    selected = jnp.where(local_index[:, None] >= 0, selected, EMPTY)

    rows = lax.all_gather((selected * SCALE).astype(F16), ("y", "core"), tiled=True)
    rows = (rows.astype(F32) * (1.0 / SCALE)).astype(BF)
    gain = norm_gain[None]
    route = gain * router.astype(F32)[None]
    packed, place = up_call(core, rows, gain, route, w_up, slots, parts)
    own_place, other_place = place[0], place[8]
    packed, own_place, other_place = lax.optimization_barrier((packed, own_place, other_place))
    summed = jnp.sum(lax.all_to_all(packed, "mp", 0, 0, tiled=True).astype(F32), axis=0)
    sums = summed[:, hidden_width:]
    inverse = lax.rsqrt((sums[:, :1] + sums[:, 1:2]) / D + 1e-06)
    scores = jax.nn.sigmoid((sums[:, 2:3] + sums[:, 3:4]) * inverse)
    hidden = jax.nn.gelu(summed[:, :hidden_width] * inverse, approximate=True) * scores
    hidden = jnp.broadcast_to(hidden.astype(BF)[None], (parts, chunk, hidden_width))
    hidden = lax.all_to_all(hidden, "mp", 0, 0, tiled=True).reshape(used_rows, hidden_width)

    row_iota = jnp.arange(used_rows, dtype=I32)

    def wanted(places):
        expander = (places[:, None] == row_iota[None, :]).astype(BF)
        return jnp.dot(expander, hidden, preferred_element_type=F32).astype(BF)

    leave = lax.optimization_barrier(wanted(other_place))
    stay = lax.optimization_barrier(wanted(own_place))
    leave = jnp.dot(leave, w_down, preferred_element_type=F32).astype(BF)
    away = lax.ppermute(leave, "core", [(0, 1), (1, 0)])
    stay = lax.optimization_barrier(jnp.dot(stay, w_down, preferred_element_type=F32))
    chip_sum = (stay + away.astype(F32)).astype(BF).reshape(chips, slots, width)
    targets = jnp.broadcast_to(local_index[None], (chips, slots)).reshape(chips * slots)
    chip_sum, targets = lax.optimization_barrier((chip_sum, targets))
    terms = lax.all_to_all(chip_sum, "y", 0, 0, tiled=True).reshape(chips * slots, width)
    placer = (targets[:, None] == token_iota[None, :]).astype(BF)
    placed = lax.dot_general(
        placer, terms, (((0,), (0,)), ((), ())), preferred_element_type=F32
    )
    return (tokens.astype(F32) + placed).astype(BF)


def solution(mesh):
    dp, seq, mp = mesh.devices.shape
    fine = Mesh(mesh.devices.reshape(dp, seq // 2, 2, mp), ("dp", "y", "core", "mp"))
    seq = ("y", "core")
    rows = ("dp",) + seq
    placed = (P(rows, "mp"), P(rows), P("mp"), P("mp"), P("mp", seq), P(seq, "mp"))
    return jax.shard_map(
        per_device, mesh=fine, in_specs=placed, out_specs=P(rows, "mp"), check_vma=False
    )
```

time: 106 us -> 102 us (0.962)
  matrix products: 12.9 us -> 6.73 us
  Pallas kernels: 0 us -> 2.31 us
  waiting for transfers between devices: 2.52 us -> 1.18 us
    dot_general x4, matrix products: 9.49 us -> 3.36 us  [the longest x1 1.69 us: per_device(): leave = jnp.dot(leave, w_down, preferred_element_type=F32).astype(BF)]
    pallas_call x0 -> x1, Pallas kernels: none -> 2.31 us  [up_call(): pl.pallas_call(functools.partial(up_kernel, slots), out_shape=(jax.ShapeD...]
    ppermute x1, waiting for transfers between devices: 2.52 us -> 1.18 us  [per_device(): away = lax.ppermute(leave, 'core', [(0, 1), (1, 0)])]
  transfers between devices with their start and end apart: 1 -> 1, of which waited for: 1 -> 1; matrix products, arithmetic and copies ran while one was open for 0% -> 1% of each run, Pallas kernels for 0% -> 0%
where the time goes in v5:
time: 102 us; the launch traced here: 101 us
  blocking collectives  83.4 us (82%)
  matrix products  6.73 us (7%)
  starting transfers between devices  4.34 us (4%)
  Pallas kernels  2.31 us (2%)
  other arithmetic  2.03 us (2%)
  local copies, waits for them, and re-layouts  1.21 us (1%)
  waiting for transfers between devices  1.18 us (1%)
    all_to_all x1, blocking collectives, per_device(): lax.all_to_all(chip_sum, 'y', 0, 0, tiled=True)  30.6 us
    all_gather x1, blocking collectives, per_device(): lax.all_gather((selected * SCALE).astype(F16), ('y', 'core'), tiled=True)  29.4 us
    all_to_all x1, blocking collectives, per_device(): lax.all_to_all(packed, 'mp', 0, 0, tiled=True).astype(F32)  13 us
    all_to_all x1, blocking collectives, per_device(): lax.all_to_all(hidden, 'mp', 0, 0, tiled=True)  10.4 us
    ppermute x1, starting transfers between devices, per_device(): away = lax.ppermute(leave, 'core', [(0, 1), (1, 0)])  4.34 us
    pallas_call x1, Pallas kernels, up_call(): pl.pallas_call(functools.partial(up_kernel, slots), out_shape=(jax.ShapeD...  2.31 us
  transfers between devices with their start and end apart: 1, of which 1 were waited for; matrix products, arithmetic and copies ran while one was open for 1% of the time, Pallas kernels for 0%

profile of v5, /device:TPU:1, one launch (start us, length us, event | category | flops | bytes accessed | tf_op | source)
XLA Modules:
  0.0 101.4 jit_solution(15440797525622385676)
XLA Ops:
  0.0 0.0 copy-start
  0.0 0.7 broadcast_compare_fusion
  0.8 1.6 %fusion.1 = f16[64,1024]{1,0:T(8,128)(2,1)S(1)} fusion(bf16[512,1024]{1,0:T(8,128)(2,1)} %param.6, pred[64]{0:T(512)(128)(4,1)S(1)} %get-tuple-element.19, s32[64]{0:T(128)S(1)} %get-tuple-element.20), kind=kOutput, calls=%fused_computation.9 | convolution fusion | flops 67338240 | bytes 1179968 | tf_op jit(solution)/shard_map/dot_general | solution.py:96
  2.3 29.4 %all-gather.1 = f16[1024,1024]{1,0:T(8,128)(2,1)S(1)} all-gather(f16[64,1024]{1,0:T(8,128)(2,1)S(1)} %fusion.1), channel_id=1, replica_groups=mesh['dp'=8,'y'=8,'core'=2,'mp'=4] {'y','core'}, dimensions={0}, use_global_device_ids=true | all-gather | bytes 2228224 | tf_op jit(solution)/shard_map/all_gather | solution.py:99
  31.7 0.0 copy-start.2
  31.7 0.0 copy-start.4
  31.7 0.0 copy-start.1
  31.7 0.6 multiply_convert_fusion.rows_ref
  32.3 0.1 copy-done.2
  32.4 0.0 copy-done.4
  32.4 0.6 copy-done.1
  33.0 2.3 %shard_map.64 = (bf16[4,128,640]{2,1,0:T(8,128)(2,1)S(1)}, s32[16,512]{1,0:T(8,128)S(1)}) custom-call(s32[1]{0:T(128)} %bitcast.core_ref, bf16[1024,1024]{1,0:T(8,128)(2,1)S(1)} %multiply_convert_fusion.rows_ref, f32[1,1024]{1,0:T(1,128)S(1)} %bitcast.20, f32[1,1024]{1,0:T(1,128)S(1)} %bitcast.21, bf16[1024,512]{1,0:T(8,128)(2,1)S(1)} %copy-done.1), custom_call_target="tpu_custom_call" | custom-call | tf_op jit(solution)/shard_map/pallas_call | solution.py:71
  35.3 13.0 %all_to_all.15 = bf16[4,128,640]{2,1,0:T(8,128)(2,1)S(1)} all-to-all(bf16[4,128,640]{2,1,0:T(8,128)(2,1)S(1)} %get-tuple-element.15), channel_id=1, replica_groups=mesh['dp'=8,'y'=8,'core'=2,'mp'=4] {'mp'}, dimensions={0} | all-to-all | bytes 1310720 | tf_op jit(solution)/shard_map/all_to_all | solution.py:106
  48.3 0.1 convert_reduce_fusion
  48.4 0.1 fusion.16
  48.5 0.1 copy.12
  48.6 0.1 copy.13
  48.7 0.1 copy.14
  48.7 0.1 copy.15
  48.9 0.2 fusion.13
  49.1 10.4 %all_to_all.16 = bf16[4,128,512]{2,1,0:T(8,128)(2,1)S(1)} all-to-all(bf16[4,128,512]{2,1,0:T(8,128)(2,1)S(1)} %broadcast_in_dim.21), channel_id=1, replica_groups=mesh['dp'=8,'y'=8,'core'=2,'mp'=4] {'mp'}, dimensions={0} | all-to-all | bytes 1048576 | tf_op jit(solution)/shard_map/all_to_all | solution.py:112
  59.5 0.5 convolution_convert_fusion.1
  60.0 0.0 copy-done
  60.0 1.7 %convolution_convert_fusion = bf16[512,1024]{1,0:T(8,128)(2,1)} fusion(bf16[512,512]{1,0:T(8,128)(2,1)S(1)} %convolution_convert_fusion.1, bf16[512,1024]{1,0:T(8,128)(2,1)S(1)} %copy-done), kind=kOutput, calls=%fused_computation.3 | convolution fusion | flops 537395200 | bytes 2621440 | tf_op jit(solution)/shard_map/dot_general | solution.py:122
  61.7 4.3 %collective-permute-start = (bf16[512,1024]{1,0:T(8,128)(2,1)}, bf16[512,1024]{1,0:T(8,128)(2,1)S(1)}, u32[]{:S(2)}, u32[]{:S(2)}) collective-permute-start(bf16[512,1024]{1,0:T(8,128)(2,1)} %convolution_convert_fusion), channel_id=1, source_target_pairs={{0,4},{4,0},{1,5},{5,1},{2,6},{6,2},{3,7},{7,3},{8,12},{12,8},{9,1... | collective-permute-start | bytes 3145736 | tf_op jit(solution)/shard_map/ppermute | solution.py:123
  66.0 0.1 reshape.27
  66.1 0.5 convolution_convert_fusion.2
  66.6 0.7 fusion.18
  67.3 1.2 %collective-permute-done = bf16[512,1024]{1,0:T(8,128)(2,1)S(1)} collective-permute-done((bf16[512,1024]{1,0:T(8,128)(2,1)}, bf16[512,1024]{1,0:T(8,128)(2,1)S(1)}, u32[]{:S(2)}, u32[]{:S(2)}) %collective-permute-start) | collective-permute-done | bytes 1048608 | tf_op jit(solution)/shard_map/ppermute | solution.py:123
  68.5 0.4 add_convert_fusion.1
  68.9 0.0 copy-start.3
  68.9 30.6 %all_to_all.17 = bf16[8,64,1024]{2,1,0:T(8,128)(2,1)S(1)} all-to-all(bf16[8,64,1024]{2,1,0:T(8,128)(2,1)S(1)} %bitcast.22), channel_id=1, replica_groups=mesh['dp'=8,'y'=8,'core'=2,'mp'=4] {'y'}, dimensions={0} | all-to-all | bytes 2097152 | tf_op jit(solution)/shard_map/all_to_all | solution.py:128
  99.5 0.0 copy-done.3
  99.5 1.8 %add_convert_fusion = bf16[512,1024]{1,0:T(8,128)(2,1)} fusion(bf16[512,1024]{1,0:T(8,128)(2,1)S(1)} %copy-done.3, bf16[512,1024]{1,0:T(8,128)(2,1)S(1)} %bitcast.23, s32[512]{0:T(512)S(1)} %reshape.27), kind=kOutput, calls=%fused_computation.1 | convolution fusion | flops 538705920 | bytes 3147776 | tf_op jit(solution)/shard_map/dot_general | solution.py:130
  (5 shorter events, 0.1 us)
Async XLA Ops:
  0.0 60.0 %copy-start = (bf16[512,1024]{1,0:T(8,128)(2,1)S(1)}, bf16[512,1024]{1,0:T(8,128)(2,1)}, u32[]{:S(2)}) copy-start(bf16[512,1024]{1,0:T(8,128)(2,1)} %param.11) | copy-start | bytes 3145732
  31.7 0.7 copy-start.2
  31.7 0.7 copy-start.4
  31.7 1.3 %copy-start.1 = (bf16[1024,512]{1,0:T(8,128)(2,1)S(1)}, bf16[1024,512]{1,0:T(8,128)(2,1)}, u32[]{:S(2)}) copy-start(bf16[1024,512]{1,0:T(8,128)(2,1)} %w_ref.1) | copy-start | bytes 3145732
  61.7 6.8 %collective-permute-start = (bf16[512,1024]{1,0:T(8,128)(2,1)}, bf16[512,1024]{1,0:T(8,128)(2,1)S(1)}, u32[]{:S(2)}, u32[]{:S(2)}) collective-permute-start(bf16[512,1024]{1,0:T(8,128)(2,1)} %convolution_convert_fusion), channel_id=1, source_target_pairs={{0,4},{4,0},{1,5},{5,1},{2,6},{6,2},{3,7},{7,3},{8,12},{12,8},{9,1... | collective-permute-start | bytes 3145736 | tf_op jit(solution)/shard_map/ppermute | solution.py:123
  68.9 30.6 %copy-start.3 = (bf16[512,1024]{1,0:T(8,128)(2,1)S(1)}, bf16[512,1024]{1,0:T(8,128)(2,1)}, u32[]{:S(2)}) copy-start(bf16[512,1024]{1,0:T(8,128)(2,1)} %param.6) | copy-start | bytes 3145732

commit v6 on v5

--- a/solution.py
+++ b/solution.py
@@ -12,6 +12,8 @@
 EMPTY = 31.5
 LIMIT = 30.5
 SCALE = 2048.0
+GRANT = 58 * 1024 * 1024
+UP_GRANT = 48 * 1024 * 1024
 BF = jnp.bfloat16
 F16 = jnp.float16
 F32 = jnp.float32
@@ -22,10 +24,53 @@
     return lax.broadcasted_iota(I32, shape, axis)
 
 
-def up_kernel(slots, core_ref, rows_ref, gain_ref, route_ref, w_ref, out_ref, place_ref):
+def select_kernel(start_ref, index_hbm, tokens_hbm, out_ref, index_ref, tokens_ref, sems):
+    copies = [
+        pltpu.make_async_copy(index_hbm, index_ref, sems.at[0]),
+        pltpu.make_async_copy(tokens_hbm, tokens_ref, sems.at[1]),
+    ]
+    for copy in copies:
+        copy.start()
+    copies[0].wait()
+    tok_rows = tokens_ref.shape[0]
+    slots = out_ref.shape[0]
+    local = index_ref[...] - start_ref[0]
+    picker = (iota((tok_rows, slots), 0) == local).astype(F32).astype(BF)
+    rows = (((0,), (0,)), ((), ()))
+    copies[1].wait()
+    selected = lax.dot_general(picker, tokens_ref[...], rows, preferred_element_type=F32)
+    unused = ((local < 0) & (iota((8, slots), 0) == 0)).astype(F32).astype(BF)
+    mark = jnp.full((8, out_ref.shape[1]), EMPTY, BF)
+    selected += lax.dot_general(unused, mark, rows, preferred_element_type=F32)
+    out_ref[...] = (selected * SCALE).astype(BF)
+
+
+def select_call(start, index, tokens):
+    vmem = pl.BlockSpec(memory_space=pltpu.VMEM)
+    return pl.pallas_call(
+        select_kernel,
+        out_shape=jax.ShapeDtypeStruct((index.shape[0], tokens.shape[1]), BF),
+        in_specs=[pl.BlockSpec(memory_space=pltpu.SMEM)]
+        + [pl.BlockSpec(memory_space=pl.ANY)] * 2,
+        out_specs=vmem,
+        scratch_shapes=[
+            pltpu.VMEM((1,) + index.shape, I32),
+            pltpu.VMEM(tokens.shape, BF),
+            pltpu.SemaphoreType.DMA((2,)),
+        ],
+        compiler_params=pltpu.CompilerParams(vmem_limit_bytes=GRANT),
+    )(start.reshape(1), index.reshape(1, -1), tokens)
+
+
+def up_kernel(
+    slots, core_ref, rows_ref, gain_ref, route_ref, w_hbm, out_ref, place_ref, w_ref, w_sem
+):
+    w_copy = pltpu.make_async_copy(w_hbm, w_ref, w_sem)
+    w_copy.start()
     count = rows_ref.shape[0]
-    parts, chunk = out_ref.shape[:2]
-    total = parts * chunk
+    parts = out_ref.shape[0]
+    total = ROUTED
+    chunk = total // parts
     hidden_width = w_ref.shape[1]
     core = core_ref[0]
     pick = (iota((8, 128), 1) == 0).astype(BF)
@@ -54,8 +99,6 @@
     raw = jnp.dot(compactor, rows_ref[...], preferred_element_type=F32)
     square = jnp.sum(raw * raw, axis=1, keepdims=True)
     route = jnp.sum(raw * route_ref[...], axis=1, keepdims=True)
-    up_part = jnp.dot((raw * gain_ref[...]).astype(BF), w_ref[...], preferred_element_type=F32)
-    out_ref[:, :, :hidden_width] = up_part.astype(BF).reshape(parts, chunk, hidden_width)
     square_high = square.astype(BF).astype(F32)
     route_high = route.astype(BF).astype(F32)
     lane = iota((total, 128), 1)
@@ -63,7 +106,14 @@
     sums = jnp.where(lane == 1, square - square_high, sums)
     sums = jnp.where(lane == 2, route_high, sums)
     sums = jnp.where(lane == 3, route - route_high, sums)
-    out_ref[:, :, hidden_width:] = sums.astype(BF).reshape(parts, chunk, 128)
+    sums = jnp.transpose(sums)[:16].astype(BF)
+    scaled = (raw * gain_ref[...]).astype(BF)
+    w_copy.wait()
+    up_part = jnp.dot(scaled, w_ref[...], preferred_element_type=F32)
+    out_ref[:, :chunk, :] = up_part.astype(BF).reshape(parts, chunk, hidden_width)
+    out_ref[:, chunk:, 128:] = jnp.zeros((parts, 16, hidden_width - 128), BF)
+    for m in range(parts):
+        out_ref[m, chunk:, :128] = sums[:, m * chunk : (m + 1) * chunk]
 
 
 def up_call(core, rows, gain, route, w_up, slots, parts):
@@ -71,12 +121,15 @@
     return pl.pallas_call(
         functools.partial(up_kernel, slots),
         out_shape=(
-            jax.ShapeDtypeStruct((parts, ROUTED // parts, w_up.shape[1] + 128), BF),
+            jax.ShapeDtypeStruct((parts, ROUTED // parts + 16, w_up.shape[1]), BF),
             jax.ShapeDtypeStruct((16, rows.shape[0] // 2), I32),
         ),
-        in_specs=[pl.BlockSpec(memory_space=pltpu.SMEM)] + [vmem] * 4,
+        in_specs=[pl.BlockSpec(memory_space=pltpu.SMEM)]
+        + [vmem] * 3
+        + [pl.BlockSpec(memory_space=pl.ANY)],
         out_specs=(vmem, vmem),
-        compiler_params=pltpu.CompilerParams(vmem_limit_bytes=40 * 1024 * 1024),
+        scratch_shapes=[pltpu.VMEM(w_up.shape, BF), pltpu.SemaphoreType.DMA],
+        compiler_params=pltpu.CompilerParams(vmem_limit_bytes=UP_GRANT),
     )(core.reshape(1), rows, gain, route, w_up)
 
 
@@ -92,11 +145,9 @@
     seq_rank = lax.axis_index("y") * 2 + core
     local_index = heavy_index - seq_rank * tok_rows
     token_iota = jnp.arange(tok_rows, dtype=I32)
-    picker = (local_index[:, None] == token_iota[None, :]).astype(BF)
-    selected = jnp.dot(picker, tokens, preferred_element_type=F32)
-    selected = jnp.where(local_index[:, None] >= 0, selected, EMPTY)
+    selected = select_call(seq_rank * tok_rows, heavy_index, tokens)
 
-    rows = lax.all_gather((selected * SCALE).astype(F16), ("y", "core"), tiled=True)
+    rows = lax.all_gather(selected.astype(F16), ("y", "core"), tiled=True)
     rows = (rows.astype(F32) * (1.0 / SCALE)).astype(BF)
     gain = norm_gain[None]
     route = gain * router.astype(F32)[None]
@@ -104,10 +155,10 @@
     own_place, other_place = place[0], place[8]
     packed, own_place, other_place = lax.optimization_barrier((packed, own_place, other_place))
     summed = jnp.sum(lax.all_to_all(packed, "mp", 0, 0, tiled=True).astype(F32), axis=0)
-    sums = summed[:, hidden_width:]
+    sums = summed[chunk : chunk + 4, :chunk].T
     inverse = lax.rsqrt((sums[:, :1] + sums[:, 1:2]) / D + 1e-06)
     scores = jax.nn.sigmoid((sums[:, 2:3] + sums[:, 3:4]) * inverse)
-    hidden = jax.nn.gelu(summed[:, :hidden_width] * inverse, approximate=True) * scores
+    hidden = jax.nn.gelu(summed[:chunk] * inverse, approximate=True) * scores
     hidden = jnp.broadcast_to(hidden.astype(BF)[None], (parts, chunk, hidden_width))
     hidden = lax.all_to_all(hidden, "mp", 0, 0, tiled=True).reshape(used_rows, hidden_width)
 

time: 102 us -> 102 us (level)
  Pallas kernels: 2.31 us -> 5.11 us
  matrix products: 6.73 us -> 5.18 us
    pallas_call x0 -> x1, Pallas kernels: none -> 2.36 us  [select_call(): pl.pallas_call(select_kernel, out_shape=jax.ShapeDtypeStruct((index.shape...]
    dot_general x1 -> x0, matrix products: 1.56 us -> none  [per_device(): selected = jnp.dot(picker, tokens, preferred_element_type=F32)]
where the time goes in v6:
time: 102 us
  blocking collectives  83.5 us (82%)
  matrix products  5.18 us (5%)
  Pallas kernels  5.11 us (5%)
  starting transfers between devices  3.77 us (4%)
  other arithmetic  2.21 us (2%)
  waiting for transfers between devices  1.16 us (1%)
    all_to_all x1, blocking collectives, per_device(): lax.all_to_all(chip_sum, 'y', 0, 0, tiled=True)  30.6 us
    all_gather x1, blocking collectives, per_device(): rows = lax.all_gather(selected.astype(F16), ('y', 'core'), tiled=True)  29.4 us
    all_to_all x1, blocking collectives, per_device(): lax.all_to_all(packed, 'mp', 0, 0, tiled=True).astype(F32)  12.6 us
    all_to_all x1, blocking collectives, per_device(): lax.all_to_all(hidden, 'mp', 0, 0, tiled=True)  11 us
    ppermute x1, starting transfers between devices, per_device(): away = lax.ppermute(leave, 'core', [(0, 1), (1, 0)])  3.77 us
    pallas_call x1, Pallas kernels, up_call(): pl.pallas_call(functools.partial(up_kernel, slots), out_shape=(jax.ShapeD...  2.75 us
    pallas_call x1, Pallas kernels, select_call(): pl.pallas_call(select_kernel, out_shape=jax.ShapeDtypeStruct((index.shape...  2.36 us
  transfers between devices with their start and end apart: 1, of which 1 were waited for; matrix products, arithmetic and copies ran while one was open for 1% of the time, Pallas kernels for 0%

profile of v6, /device:TPU:1, one launch (start us, length us, event | category | flops | bytes accessed | tf_op | source)
XLA Modules:
  0.0 101.9 jit_solution(862155440597422591)
XLA Ops:
  0.0 0.0 copy-start
  0.0 2.4 %shard_map.64 = bf16[64,1024]{1,0:T(8,128)(2,1)} custom-call(s32[1]{0:T(128)} %bitcast.1.start_ref, s32[1,64]{1,0:T(1,128)} %bitcast.31, bf16[512,1024]{1,0:T(8,128)(2,1)} %tokens_hbm.1), custom_call_target="tpu_custom_call" | custom-call | tf_op jit(solution)/shard_map/pallas_call | solution.py:50
  2.4 0.9 convert_element_type.43
  3.3 29.4 %all-gather.1 = f16[1024,1024]{1,0:T(8,128)(2,1)S(1)} all-gather(f16[64,1024]{1,0:T(8,128)(2,1)S(1)} %convert_element_type.43), channel_id=1, replica_groups=mesh['dp'=8,'y'=8,'core'=2,'mp'=4] {'y','core'}, dimensions={0}, use_global_device_ids=true | all-gather | bytes 2228224 | tf_op jit(solution)/shard_map/all_gather | solution.py:150
  32.7 0.0 copy-start.2
  32.7 0.0 copy-start.4
  32.7 0.0 copy-start.1
  32.7 0.6 multiply_convert_fusion.rows_ref
  33.3 0.1 copy-done.2
  33.4 0.0 copy-done.4
  33.4 0.6 copy-done.1
  34.0 2.8 %shard_map.65 = (bf16[4,144,512]{2,1,0:T(8,128)(2,1)S(1)}, s32[16,512]{1,0:T(8,128)S(1)}) custom-call(s32[1]{0:T(128)} %bitcast.core_ref, bf16[1024,1024]{1,0:T(8,128)(2,1)S(1)} %multiply_convert_fusion.rows_ref, f32[1,1024]{1,0:T(1,128)S(1)} %bitcast.22, f32[1,1024]{1,0:T(1,128)S(1)} %bitcast.23, bf16[1024,512]{1,0:T(8,128)(2,1)S(1)} %copy-done.1), custom_call_target="tpu_custom_call" | custom-call | tf_op jit(solution)/shard_map/pallas_call | solution.py:121
  36.7 12.6 %all_to_all.15 = bf16[4,144,512]{2,1,0:T(8,128)(2,1)S(1)} all-to-all(bf16[4,144,512]{2,1,0:T(8,128)(2,1)S(1)} %get-tuple-element.15), channel_id=1, replica_groups=mesh['dp'=8,'y'=8,'core'=2,'mp'=4] {'mp'}, dimensions={0} | all-to-all | bytes 1179648 | tf_op jit(solution)/shard_map/all_to_all | solution.py:157
  49.3 0.1 convert_reduce_fusion
  49.4 0.2 fusion.11
  49.6 11.0 %all_to_all.16 = bf16[4,128,512]{2,1,0:T(8,128)(2,1)S(1)} all-to-all(bf16[4,128,512]{2,1,0:T(8,128)(2,1)S(1)} %broadcast_in_dim.7), channel_id=1, replica_groups=mesh['dp'=8,'y'=8,'core'=2,'mp'=4] {'mp'}, dimensions={0} | all-to-all | bytes 1048576 | tf_op jit(solution)/shard_map/all_to_all | solution.py:163
  60.6 0.0 copy-start.5
  60.6 0.5 convolution_convert_fusion.1
  61.1 0.0 copy-done
  61.1 1.7 %convolution_convert_fusion = bf16[512,1024]{1,0:T(8,128)(2,1)} fusion(bf16[512,512]{1,0:T(8,128)(2,1)S(1)} %convolution_convert_fusion.1, bf16[512,1024]{1,0:T(8,128)(2,1)S(1)} %copy-done), kind=kOutput, calls=%fused_computation.3 | convolution fusion | flops 537395200 | bytes 2621440 | tf_op jit(solution)/shard_map/dot_general | solution.py:173
  62.8 3.8 %collective-permute-start = (bf16[512,1024]{1,0:T(8,128)(2,1)}, bf16[512,1024]{1,0:T(8,128)(2,1)S(1)}, u32[]{:S(2)}, u32[]{:S(2)}) collective-permute-start(bf16[512,1024]{1,0:T(8,128)(2,1)} %convolution_convert_fusion), channel_id=1, source_target_pairs={{0,4},{4,0},{1,5},{5,1},{2,6},{6,2},{3,7},{7,3},{8,12},{12,8},{9,1... | collective-permute-start | bytes 3145736 | tf_op jit(solution)/shard_map/ppermute | solution.py:174
  66.6 0.0 copy-done.5
  66.6 0.1 reshape.32
  66.7 0.5 convolution_convert_fusion.2
  67.2 0.7 fusion.13
  67.9 1.2 %collective-permute-done = bf16[512,1024]{1,0:T(8,128)(2,1)S(1)} collective-permute-done((bf16[512,1024]{1,0:T(8,128)(2,1)}, bf16[512,1024]{1,0:T(8,128)(2,1)S(1)}, u32[]{:S(2)}, u32[]{:S(2)}) %collective-permute-start) | collective-permute-done | bytes 1048608 | tf_op jit(solution)/shard_map/ppermute | solution.py:174
  69.1 0.4 add_convert_fusion.1
  69.5 0.0 copy-start.3
  69.5 30.6 %all_to_all.17 = bf16[8,64,1024]{2,1,0:T(8,128)(2,1)S(1)} all-to-all(bf16[8,64,1024]{2,1,0:T(8,128)(2,1)S(1)} %bitcast.24), channel_id=1, replica_groups=mesh['dp'=8,'y'=8,'core'=2,'mp'=4] {'y'}, dimensions={0} | all-to-all | bytes 2097152 | tf_op jit(solution)/shard_map/all_to_all | solution.py:179
  100.1 0.0 copy-done.3
  100.1 1.8 %add_convert_fusion = bf16[512,1024]{1,0:T(8,128)(2,1)} fusion(bf16[512,1024]{1,0:T(8,128)(2,1)S(1)} %copy-done.3, bf16[512,1024]{1,0:T(8,128)(2,1)S(1)} %bitcast.25, s32[512]{0:T(512)S(1)} %reshape.32), kind=kOutput, calls=%fused_computation.1 | convolution fusion | flops 538705920 | bytes 3147776 | tf_op jit(solution)/shard_map/dot_general | solution.py:181
  (7 shorter events, 0.1 us)
Async XLA Ops:
  0.0 61.1 %copy-start = (bf16[512,1024]{1,0:T(8,128)(2,1)S(1)}, bf16[512,1024]{1,0:T(8,128)(2,1)}, u32[]{:S(2)}) copy-start(bf16[512,1024]{1,0:T(8,128)(2,1)} %param.11) | copy-start | bytes 3145732
  32.7 0.7 copy-start.2
  32.7 0.7 copy-start.4
  32.7 1.3 %copy-start.1 = (bf16[1024,512]{1,0:T(8,128)(2,1)S(1)}, bf16[1024,512]{1,0:T(8,128)(2,1)}, u32[]{:S(2)}) copy-start(bf16[1024,512]{1,0:T(8,128)(2,1)} %w_hbm.1) | copy-start | bytes 3145732
  60.6 6.0 %copy-start.5 = (s32[64]{0:T(128)S(1)}, s32[64]{0:T(128)}, u32[]{:S(2)}) copy-start(s32[64]{0:T(128)} %param.7) | copy-start | bytes 772
  62.8 6.3 %collective-permute-start = (bf16[512,1024]{1,0:T(8,128)(2,1)}, bf16[512,1024]{1,0:T(8,128)(2,1)S(1)}, u32[]{:S(2)}, u32[]{:S(2)}) collective-permute-start(bf16[512,1024]{1,0:T(8,128)(2,1)} %convolution_convert_fusion), channel_id=1, source_target_pairs={{0,4},{4,0},{1,5},{5,1},{2,6},{6,2},{3,7},{7,3},{8,12},{12,8},{9,1... | collective-permute-start | bytes 3145736 | tf_op jit(solution)/shard_map/ppermute | solution.py:174
  69.5 30.6 %copy-start.3 = (bf16[512,1024]{1,0:T(8,128)(2,1)S(1)}, bf16[512,1024]{1,0:T(8,128)(2,1)}, u32[]{:S(2)}) copy-start(bf16[512,1024]{1,0:T(8,128)(2,1)} %tokens_hbm.1) | copy-start | bytes 3145732

commit v7 on v5

v7 whole, which is shorter than its diff:
```python
import functools

import jax
import jax.numpy as jnp
from jax import lax
from jax.experimental import pallas as pl
from jax.experimental.pallas import tpu as pltpu
from jax.sharding import Mesh, PartitionSpec as P

D = 4096
ROUTED = 512
EMPTY = 31.5
LIMIT = 30.5
SCALE = 2048.0
BF = jnp.bfloat16
F16 = jnp.float16
F32 = jnp.float32
I32 = jnp.int32


def iota(shape, axis):
    return lax.broadcasted_iota(I32, shape, axis)


def up_kernel(slots, core_ref, rows_ref, gain_ref, route_ref, w_ref, out_ref, place_ref):
    count = rows_ref.shape[0]
    parts = out_ref.shape[0]
    total = ROUTED
    chunk = total // parts
    hidden_width = w_ref.shape[1]
    core = core_ref[0]
    pick = (iota((8, 128), 1) == 0).astype(BF)
    marks = lax.dot_general(
        pick, rows_ref[:, :128], (((1,), (1,)), ((), ())), preferred_element_type=F32
    )
    used = (marks < LIMIT).astype(F32).astype(BF)
    owner = (iota((count, 128), 0) // slots == iota((count, 128), 1)).astype(BF)
    numbers = jnp.dot(used, owner, preferred_element_type=F32).astype(BF)

    def owners_of(owner):
        before = (iota((128, owner.shape[1]), 0) < owner).astype(BF)
        same = (iota((128, owner.shape[1]), 0) == owner).astype(BF)
        first = jnp.dot(numbers, before, preferred_element_type=F32).astype(I32)
        return first, jnp.dot(numbers, same, preferred_element_type=F32).astype(I32)

    first, number = owners_of(iota((1, count), 1) // slots)
    slot = iota((8, count), 1) % slots
    row = first + slot
    within = row % chunk
    spot = row - within + row % 2 * (chunk // 2) + within // 2
    spot = jnp.where(slot < number, spot, -1)
    share = slots // 2
    first, number = owners_of(iota((1, count // 2), 1) // share)
    row = first + (first + core) % 2 + 2 * (iota((8, count // 2), 1) % share)
    place_ref[:8] = jnp.where(row < first + number, (row - core) // 2, -1)
    place_ref[8:] = first

    compactor = (iota((total, count), 0) == spot[:1]).astype(F32).astype(BF)
    raw = jnp.dot(compactor, rows_ref[...], preferred_element_type=F32)
    square = jnp.sum(raw * raw, axis=1, keepdims=True)
    route = jnp.sum(raw * route_ref[...], axis=1, keepdims=True)
    square_high = square.astype(BF).astype(F32)
    route_high = route.astype(BF).astype(F32)
    lane = iota((total, 128), 1)
    sums = jnp.where(lane == 0, square_high, 0.0)
    sums = jnp.where(lane == 1, square - square_high, sums)
    sums = jnp.where(lane == 2, route_high, sums)
    sums = jnp.where(lane == 3, route - route_high, sums)
    sums = jnp.transpose(sums)[:16].astype(BF)
    scaled = (raw * gain_ref[...]).astype(BF)
    up_part = jnp.dot(scaled, w_ref[...], preferred_element_type=F32)
    out_ref[:, :chunk, :] = up_part.astype(BF).reshape(parts, chunk, hidden_width)
    out_ref[:, chunk:, 128:] = jnp.zeros((parts, 16, hidden_width - 128), BF)
    for m in range(parts):
        out_ref[m, chunk:, :128] = sums[:, m * chunk : (m + 1) * chunk]


def up_call(core, rows, gain, route, w_up, slots, parts):
    vmem = pl.BlockSpec(memory_space=pltpu.VMEM)
    return pl.pallas_call(
        functools.partial(up_kernel, slots),
        out_shape=(
            jax.ShapeDtypeStruct((parts, ROUTED // parts + 16, w_up.shape[1]), BF),
            jax.ShapeDtypeStruct((16, rows.shape[0] // 2), I32),
        ),
        in_specs=[pl.BlockSpec(memory_space=pltpu.SMEM)] + [vmem] * 4,
        out_specs=(vmem, vmem),
        compiler_params=pltpu.CompilerParams(vmem_limit_bytes=40 * 1024 * 1024),
    )(core.reshape(1), rows, gain, route, w_up)


def per_device(tokens, heavy_index, norm_gain, router, w_up, w_down):
    tok_rows, width = tokens.shape
    slots = heavy_index.shape[0]
    hidden_width = w_up.shape[1]
    chips = lax.axis_size("y")
    parts = lax.axis_size("mp")
    core = lax.axis_index("core")
    used_rows = ROUTED
    share = slots // 2
    chunk = used_rows // parts
    seq_rank = lax.axis_index("y") * 2 + core
    local_index = heavy_index - seq_rank * tok_rows
    token_iota = jnp.arange(tok_rows, dtype=I32)
    picker = (local_index[:, None] == token_iota[None, :]).astype(BF)
    selected = jnp.dot(picker, tokens, preferred_element_type=F32)
    selected = jnp.where(local_index[:, None] >= 0, selected, EMPTY)

    rows = lax.all_gather((selected * SCALE).astype(F16), ("y", "core"), tiled=True)
    rows = (rows.astype(F32) * (1.0 / SCALE)).astype(BF)
    gain = norm_gain[None]
    route = gain * router.astype(F32)[None]
    packed, place = up_call(core, rows, gain, route, w_up, slots, parts)
    mine, start = place[0], lax.dynamic_index_in_dim(place[8], seq_rank * share, keepdims=False)
    pairs = local_index.reshape(share, 2).T
    targets = jnp.where(start % 2 == 0, pairs, pairs[::-1])
    targets = jnp.broadcast_to(targets[None], (chips, 2, share)).reshape(chips * slots)
    packed, mine, targets = lax.optimization_barrier((packed, mine, targets))
    summed = jnp.sum(lax.all_to_all(packed, "mp", 0, 0, tiled=True).astype(F32), axis=0)
    sums = summed[chunk : chunk + 4, :chunk].T
    inverse = lax.rsqrt((sums[:, :1] + sums[:, 1:2]) / D + 1e-06)
    scores = jax.nn.sigmoid((sums[:, 2:3] + sums[:, 3:4]) * inverse)
    hidden = jax.nn.gelu(summed[:chunk] * inverse, approximate=True) * scores
    hidden = hidden.astype(BF).reshape(2, 1, chunk // 2, hidden_width)
    hidden = jnp.broadcast_to(hidden, (2, parts, chunk // 2, hidden_width))
    hidden = lax.all_to_all(
        hidden.reshape(2 * parts, chunk // 2, hidden_width), ("core", "mp"), 0, 0, tiled=True
    ).reshape(2, used_rows // 2, hidden_width)
    w_near = lax.ppermute(w_down, "core", [(0, 1), (1, 0)])
    here = jnp.where(core == 0, hidden[0], hidden[1])
    near = jnp.where(core == 0, hidden[1], hidden[0])

    expander = (mine[:, None] == jnp.arange(used_rows // 2, dtype=I32)[None, :]).astype(BF)
    wanted = jnp.dot(
        expander, jnp.concatenate([here, near], axis=1), preferred_element_type=F32
    ).astype(BF)
    wanted = lax.optimization_barrier(wanted)
    down = jnp.dot(wanted[:, :hidden_width], w_down, preferred_element_type=F32)
    down += jnp.dot(wanted[:, hidden_width:], w_near, preferred_element_type=F32)
    chip_sum = down.astype(BF).reshape(2 * chips, share, width)
    terms = lax.all_to_all(chip_sum, ("y", "core"), 0, 0, tiled=True).reshape(-1, width)
    placer = (targets[:, None] == token_iota[None, :]).astype(BF)
    placed = lax.dot_general(
        placer, terms, (((0,), (0,)), ((), ())), preferred_element_type=F32
    )
    return (tokens.astype(F32) + placed).astype(BF)


def solution(mesh):
    dp, seq, mp = mesh.devices.shape
    fine = Mesh(mesh.devices.reshape(dp, seq // 2, 2, mp), ("dp", "y", "core", "mp"))
    seq = ("y", "core")
    rows = ("dp",) + seq
    placed = (P(rows, "mp"), P(rows), P("mp"), P("mp"), P("mp", seq), P(seq, "mp"))
    return jax.shard_map(
        per_device, mesh=fine, in_specs=placed, out_specs=P(rows, "mp"), check_vma=False
    )
```

time: 102 us -> 102 us (level)
  blocking collectives: 83.4 us -> 74 us
  waiting for transfers between devices: 1.18 us -> 7.36 us
  starting transfers between devices: 4.34 us -> 6.37 us
  between operations: 0.13 us -> 2.09 us
  matrix products: 6.73 us -> 5.32 us
  local copies, waits for them, and re-layouts: 1.21 us -> 2.43 us
    all_to_all x2 -> x1, blocking collectives: 41 us -> 31.9 us  [per_device(): lax.all_to_all(chip_sum, ('y', 'core'), 0, 0, tiled=True).reshape(-1, width)]
    all_to_all x0 -> x1, waiting for transfers between devices: none -> 7.35 us  [per_device(): lax.all_to_all(hidden.reshape(2 * parts, chunk // 2, hidden_width), ('cor...]
    all_to_all x0 -> x1, starting transfers between devices: none -> 4.37 us  [per_device(): lax.all_to_all(hidden.reshape(2 * parts, chunk // 2, hidden_width), ('cor...]
    ppermute x1, starting transfers between devices: 4.34 us -> 2 us  [per_device(): w_near = lax.ppermute(w_down, 'core', [(0, 1), (1, 0)])]
    dot_general x4 -> x3, matrix products: 3.36 us -> 1.96 us  [the longest x1 0.75 us: per_device(): jnp.dot(wanted[:, hidden_width:], w_near, preferred_element_type=F32)]
    ppermute x1, waiting for transfers between devices: 1.18 us -> 0.01 us  [per_device(): w_near = lax.ppermute(w_down, 'core', [(0, 1), (1, 0)])]
  transfers between devices with their start and end apart: 1 -> 2, of which waited for: 1 -> 1; matrix products, arithmetic and copies ran while one was open for 1% -> 1% of each run, Pallas kernels for 0% -> 0%
where the time goes in v7:
time: 102 us; the launch traced here: 101 us
  blocking collectives  74 us (73%)
  waiting for transfers between devices  7.36 us (7%)
  starting transfers between devices  6.37 us (6%)
  matrix products  5.32 us (5%)
  local copies, waits for them, and re-layouts  2.43 us (2%)
  Pallas kernels  2.37 us (2%)
  between operations  2.09 us (2%)
  other arithmetic  1.58 us (2%)
    all_to_all x1, blocking collectives, per_device(): lax.all_to_all(chip_sum, ('y', 'core'), 0, 0, tiled=True).reshape(-1, width)  31.9 us
    all_gather x1, blocking collectives, per_device(): lax.all_gather((selected * SCALE).astype(F16), ('y', 'core'), tiled=True)  29.4 us
    all_to_all x1, blocking collectives, per_device(): lax.all_to_all(packed, 'mp', 0, 0, tiled=True).astype(F32)  12.7 us
    all_to_all x1, waiting for transfers between devices, per_device(): lax.all_to_all(hidden.reshape(2 * parts, chunk // 2, hidden_width), ('cor...  7.35 us
    all_to_all x1, starting transfers between devices, per_device(): lax.all_to_all(hidden.reshape(2 * parts, chunk // 2, hidden_width), ('cor...  4.37 us
    pallas_call x1, Pallas kernels, up_call(): pl.pallas_call(functools.partial(up_kernel, slots), out_shape=(jax.ShapeD...  2.37 us
  transfers between devices with their start and end apart: 2, of which 1 were waited for; matrix products, arithmetic and copies ran while one was open for 1% of the time, Pallas kernels for 0%

profile of v7, /device:TPU:1, one launch (start us, length us, event | category | flops | bytes accessed | tf_op | source)
XLA Modules:
  0.0 101.5 jit_solution(8728849854017784977)
XLA Ops:
  0.0 0.7 broadcast_compare_fusion
  0.7 1.6 %fusion.1 = f16[64,1024]{1,0:T(8,128)(2,1)S(1)} fusion(bf16[512,1024]{1,0:T(8,128)(2,1)} %param.6, pred[64]{0:T(512)(128)(4,1)S(1)} %get-tuple-element.17, s32[64]{0:T(128)S(1)} %get-tuple-element.18), kind=kOutput, calls=%fused_computation.7 | convolution fusion | flops 67338240 | bytes 1179968 | tf_op jit(solution)/shard_map/dot_general | solution.py:106
  2.2 29.4 %all-gather.1 = f16[1024,1024]{1,0:T(8,128)(2,1)S(1)} all-gather(f16[64,1024]{1,0:T(8,128)(2,1)S(1)} %fusion.1), channel_id=1, replica_groups=mesh['dp'=8,'y'=8,'core'=2,'mp'=4] {'y','core'}, dimensions={0}, use_global_device_ids=true | all-gather | bytes 2228224 | tf_op jit(solution)/shard_map/all_gather | solution.py:109
  31.6 0.0 copy-start.1
  31.6 0.0 copy-start.4
  31.6 0.0 copy-start
  31.6 0.6 multiply_convert_fusion.rows_ref
  32.2 0.1 copy-done.1
  32.3 0.0 copy-done.4
  32.3 0.6 copy-done
  32.9 2.4 %shard_map.64 = (bf16[4,144,512]{2,1,0:T(8,128)(2,1)S(1)}, s32[16,512]{1,0:T(8,128)S(1)}) custom-call(s32[1]{0:T(128)} %bitcast.core_ref, bf16[1024,1024]{1,0:T(8,128)(2,1)S(1)} %multiply_convert_fusion.rows_ref, f32[1,1024]{1,0:T(1,128)S(1)} %bitcast.22, f32[1,1024]{1,0:T(1,128)S(1)} %bitcast.23, bf16[1024,512]{1,0:T(8,128)(2,1)S(1)} %copy-done), custom_call_target="tpu_custom_call" | custom-call | tf_op jit(solution)/shard_map/pallas_call | solution.py:80
  35.3 0.6 constant_dynamic-slice_fusion
  37.8 0.1 reshape.39
  37.9 0.1 rev.3
  38.0 0.1 copy.8
  38.1 0.0 copy-start.2
  38.1 0.1 reshape.40
  38.2 12.7 %all_to_all.15 = bf16[4,144,512]{2,1,0:T(8,128)(2,1)S(1)} all-to-all(bf16[4,144,512]{2,1,0:T(8,128)(2,1)S(1)} %get-tuple-element.14), channel_id=1, replica_groups=mesh['dp'=8,'y'=8,'core'=2,'mp'=4] {'mp'}, dimensions={0} | all-to-all | bytes 1179648 | tf_op jit(solution)/shard_map/all_to_all | solution.py:119
  50.9 0.1 convert_reduce_fusion
  51.0 0.2 fusion.17
  51.2 0.8 broadcast_in_dim.41
  52.0 4.4 %all-to-all-start.1 = ((bf16[8,64,512]{2,1,0:T(8,128)(2,1)}), bf16[8,64,512]{2,1,0:T(8,128)(2,1)S(1)}, u32[]{:S(2)}, u32[]{:S(2)}) async-start(bf16[8,64,512]{2,1,0:T(8,128)(2,1)} %bitcast.10), calls=%async_computation.1 | async-start | bytes 1048576 | tf_op jit(solution)/shard_map/all_to_all | solution.py:126
  56.4 0.0 copy-done.2
  56.4 2.0 %collective-permute-start = (bf16[512,1024]{1,0:T(8,128)(2,1)S(1)}, bf16[512,1024]{1,0:T(8,128)(2,1)S(1)}, u32[]{:S(2)}, u32[]{:S(2)}) collective-permute-start(bf16[512,1024]{1,0:T(8,128)(2,1)S(1)} %copy-done.2), channel_id=1, source_target_pairs={{0,4},{4,0},{1,5},{5,1},{2,6},{6,2},{3,7},{7,3},{8,12},{12,8},{9,1... | collective-permute-start | bytes 3145736 | tf_op jit(solution)/shard_map/ppermute | solution.py:129
  58.4 7.4 %all-to-all-done.1 = bf16[8,64,512]{2,1,0:T(8,128)(2,1)S(1)} async-done(((bf16[8,64,512]{2,1,0:T(8,128)(2,1)}), bf16[8,64,512]{2,1,0:T(8,128)(2,1)S(1)}, u32[]{:S(2)}, u32[]{:S(2)}) %all-to-all-start.1) | async-done | bytes 524320 | tf_op jit(solution)/shard_map/all_to_all | solution.py:126
  65.8 0.5 convolution_convert_fusion
  66.3 0.7 fusion.3
  67.0 0.0 collective-permute-done
  67.0 0.8 add_convert_fusion.1
  67.8 0.0 copy-start.3
  67.8 31.9 %all_to_all.16 = bf16[16,32,1024]{2,1,0:T(8,128)(2,1)S(1)} all-to-all(bf16[16,32,1024]{2,1,0:T(8,128)(2,1)S(1)} %bitcast.24), channel_id=1, replica_groups=mesh['dp'=8,'y'=8,'core'=2,'mp'=4] {'y','core'}, dimensions={0} | all-to-all | bytes 2097152 | tf_op jit(solution)/shard_map/all_to_all | solution.py:141
  99.7 0.0 copy-done.3
  99.7 1.8 %add_convert_fusion = bf16[512,1024]{1,0:T(8,128)(2,1)} fusion(bf16[512,1024]{1,0:T(8,128)(2,1)S(1)} %copy-done.3, bf16[512,1024]{1,0:T(8,128)(2,1)S(1)} %bitcast.25, s32[512]{0:T(512)S(1)} %reshape.40), kind=kOutput, calls=%fused_computation.1 | convolution fusion | flops 538705920 | bytes 3147776 | tf_op jit(solution)/shard_map/dot_general | solution.py:143
  (7 shorter events, 0.1 us)
Async XLA Ops:
  31.6 0.7 copy-start.1
  31.6 0.7 copy-start.4
  31.6 1.3 %copy-start = (bf16[1024,512]{1,0:T(8,128)(2,1)S(1)}, bf16[1024,512]{1,0:T(8,128)(2,1)}, u32[]{:S(2)}) copy-start(bf16[1024,512]{1,0:T(8,128)(2,1)} %w_ref.1) | copy-start | bytes 3145732
  38.1 18.3 %copy-start.2 = (bf16[512,1024]{1,0:T(8,128)(2,1)S(1)}, bf16[512,1024]{1,0:T(8,128)(2,1)}, u32[]{:S(2)}) copy-start(bf16[512,1024]{1,0:T(8,128)(2,1)} %param.11) | copy-start | bytes 3145732
  52.0 13.7 %all-to-all-start.1 = ((bf16[8,64,512]{2,1,0:T(8,128)(2,1)}), bf16[8,64,512]{2,1,0:T(8,128)(2,1)S(1)}, u32[]{:S(2)}, u32[]{:S(2)}) async-start(bf16[8,64,512]{2,1,0:T(8,128)(2,1)} %bitcast.10), calls=%async_computation.1 | async-start | bytes 1048576 | tf_op jit(solution)/shard_map/all_to_all | solution.py:126
  56.4 10.6 %collective-permute-start = (bf16[512,1024]{1,0:T(8,128)(2,1)S(1)}, bf16[512,1024]{1,0:T(8,128)(2,1)S(1)}, u32[]{:S(2)}, u32[]{:S(2)}) collective-permute-start(bf16[512,1024]{1,0:T(8,128)(2,1)S(1)} %copy-done.2), channel_id=1, source_target_pairs={{0,4},{4,0},{1,5},{5,1},{2,6},{6,2},{3,7},{7,3},{8,12},{12,8},{9,1... | collective-permute-start | bytes 3145736 | tf_op jit(solution)/shard_map/ppermute | solution.py:129
  67.8 31.9 %copy-start.3 = (bf16[512,1024]{1,0:T(8,128)(2,1)S(1)}, bf16[512,1024]{1,0:T(8,128)(2,1)}, u32[]{:S(2)}) copy-start(bf16[512,1024]{1,0:T(8,128)(2,1)} %param.6) | copy-start | bytes 3145732

commit v8 on v7

--- a/solution.py
+++ b/solution.py
@@ -22,13 +22,15 @@
     return lax.broadcasted_iota(I32, shape, axis)
 
 
-def up_kernel(slots, core_ref, rows_ref, gain_ref, route_ref, w_ref, out_ref, place_ref):
+def up_kernel(
+    slots, core_ref, rank_ref, rows_ref, gain_ref, route_ref, w_ref, out_ref, place_ref
+):
     count = rows_ref.shape[0]
     parts = out_ref.shape[0]
     total = ROUTED
     chunk = total // parts
     hidden_width = w_ref.shape[1]
-    core = core_ref[0]
+    core, seq_rank = core_ref[0], rank_ref[0]
     pick = (iota((8, 128), 1) == 0).astype(BF)
     marks = lax.dot_general(
         pick, rows_ref[:, :128], (((1,), (1,)), ((), ())), preferred_element_type=F32
@@ -53,7 +55,7 @@
     first, number = owners_of(iota((1, count // 2), 1) // share)
     row = first + (first + core) % 2 + 2 * (iota((8, count // 2), 1) % share)
     place_ref[:8] = jnp.where(row < first + number, (row - core) // 2, -1)
-    place_ref[8:] = first
+    place_ref[8:] = owners_of(jnp.full((1, count // 2), seq_rank, I32))[0]
 
     compactor = (iota((total, count), 0) == spot[:1]).astype(F32).astype(BF)
     raw = jnp.dot(compactor, rows_ref[...], preferred_element_type=F32)
@@ -75,7 +77,7 @@
         out_ref[m, chunk:, :128] = sums[:, m * chunk : (m + 1) * chunk]
 
 
-def up_call(core, rows, gain, route, w_up, slots, parts):
+def up_call(core, seq_rank, rows, gain, route, w_up, slots, parts):
     vmem = pl.BlockSpec(memory_space=pltpu.VMEM)
     return pl.pallas_call(
         functools.partial(up_kernel, slots),
@@ -83,10 +85,10 @@
             jax.ShapeDtypeStruct((parts, ROUTED // parts + 16, w_up.shape[1]), BF),
             jax.ShapeDtypeStruct((16, rows.shape[0] // 2), I32),
         ),
-        in_specs=[pl.BlockSpec(memory_space=pltpu.SMEM)] + [vmem] * 4,
+        in_specs=[pl.BlockSpec(memory_space=pltpu.SMEM)] * 2 + [vmem] * 4,
         out_specs=(vmem, vmem),
         compiler_params=pltpu.CompilerParams(vmem_limit_bytes=40 * 1024 * 1024),
-    )(core.reshape(1), rows, gain, route, w_up)
+    )(core.reshape(1), seq_rank.reshape(1), rows, gain, route, w_up)
 
 
 def per_device(tokens, heavy_index, norm_gain, router, w_up, w_down):
@@ -110,13 +112,15 @@
     rows = (rows.astype(F32) * (1.0 / SCALE)).astype(BF)
     gain = norm_gain[None]
     route = gain * router.astype(F32)[None]
-    packed, place = up_call(core, rows, gain, route, w_up, slots, parts)
-    mine, start = place[0], lax.dynamic_index_in_dim(place[8], seq_rank * share, keepdims=False)
+    packed, place = up_call(core, seq_rank, rows, gain, route, w_up, slots, parts)
+    packed = lax.all_to_all(packed, "mp", 0, 0, tiled=True)
+    packed, place, local_index = lax.optimization_barrier((packed, place, local_index))
+    mine, start = place[0], place[8]
     pairs = local_index.reshape(share, 2).T
-    targets = jnp.where(start % 2 == 0, pairs, pairs[::-1])
-    targets = jnp.broadcast_to(targets[None], (chips, 2, share)).reshape(chips * slots)
-    packed, mine, targets = lax.optimization_barrier((packed, mine, targets))
-    summed = jnp.sum(lax.all_to_all(packed, "mp", 0, 0, tiled=True).astype(F32), axis=0)
+    evens = jnp.broadcast_to(pairs[None], (chips, 2, share)).reshape(chips * slots)
+    odds = jnp.broadcast_to(pairs[None, ::-1], (chips, 2, share)).reshape(chips * slots)
+    targets = jnp.where(start % 2 == 0, evens, odds)
+    summed = jnp.sum(packed.astype(F32), axis=0)
     sums = summed[chunk : chunk + 4, :chunk].T
     inverse = lax.rsqrt((sums[:, :1] + sums[:, 1:2]) / D + 1e-06)
     scores = jax.nn.sigmoid((sums[:, 2:3] + sums[:, 3:4]) * inverse)
@@ -126,6 +130,7 @@
     hidden = lax.all_to_all(
         hidden.reshape(2 * parts, chunk // 2, hidden_width), ("core", "mp"), 0, 0, tiled=True
     ).reshape(2, used_rows // 2, hidden_width)
+    hidden, targets = lax.optimization_barrier((hidden, targets))
     w_near = lax.ppermute(w_down, "core", [(0, 1), (1, 0)])
     here = jnp.where(core == 0, hidden[0], hidden[1])
     near = jnp.where(core == 0, hidden[1], hidden[0])

time: 102 us -> 98.9 us (0.970)
  between operations: 2.09 us -> 0.13 us
  transfers between devices with their start and end apart: 2 -> 2, of which waited for: 1 -> 1; matrix products, arithmetic and copies ran while one was open for 1% -> 2% of each run, Pallas kernels for 0% -> 0%
where the time goes in v8:
time: 98.9 us; the launch traced here: 98.5 us
  blocking collectives  74 us (75%)
  waiting for transfers between devices  6.8 us (7%)
  starting transfers between devices  6.38 us (6%)
  matrix products  5.31 us (5%)
  Pallas kernels  2.33 us (2%)
  local copies, waits for them, and re-layouts  2 us (2%)
  other arithmetic  1.6 us (2%)
    all_to_all x1, blocking collectives, per_device(): lax.all_to_all(chip_sum, ('y', 'core'), 0, 0, tiled=True).reshape(-1, width)  31.9 us
    all_gather x1, blocking collectives, per_device(): lax.all_gather((selected * SCALE).astype(F16), ('y', 'core'), tiled=True)  29.4 us
    all_to_all x1, blocking collectives, per_device(): packed = lax.all_to_all(packed, 'mp', 0, 0, tiled=True)  12.7 us
    all_to_all x1, waiting for transfers between devices, per_device(): lax.all_to_all(hidden.reshape(2 * parts, chunk // 2, hidden_width), ('cor...  6.8 us
    all_to_all x1, starting transfers between devices, per_device(): lax.all_to_all(hidden.reshape(2 * parts, chunk // 2, hidden_width), ('cor...  4.38 us
    pallas_call x1, Pallas kernels, up_call(): pl.pallas_call(functools.partial(up_kernel, slots), out_shape=(jax.ShapeD...  2.33 us
    ppermute x1, starting transfers between devices, per_device(): w_near = lax.ppermute(w_down, 'core', [(0, 1), (1, 0)])  2 us
  transfers between devices with their start and end apart: 2, of which 1 were waited for; matrix products, arithmetic and copies ran while one was open for 2% of the time, Pallas kernels for 0%

profile of v8, /device:TPU:1, one launch (start us, length us, event | category | flops | bytes accessed | tf_op | source)
XLA Modules:
  0.0 98.5 jit_solution(5541212264516620243)
XLA Ops:
  0.0 0.7 broadcast_compare_fusion
  0.7 1.6 %fusion.1 = f16[64,1024]{1,0:T(8,128)(2,1)S(1)} fusion(bf16[512,1024]{1,0:T(8,128)(2,1)} %param.6, pred[64]{0:T(512)(128)(4,1)S(1)} %get-tuple-element.21, s32[64]{0:T(128)S(1)} %get-tuple-element.16), kind=kOutput, calls=%fused_computation.7 | convolution fusion | flops 67338240 | bytes 1179968 | tf_op jit(solution)/shard_map/dot_general | solution.py:108
  2.2 29.4 %all-gather.1 = f16[1024,1024]{1,0:T(8,128)(2,1)S(1)} all-gather(f16[64,1024]{1,0:T(8,128)(2,1)S(1)} %fusion.1), channel_id=1, replica_groups=mesh['dp'=8,'y'=8,'core'=2,'mp'=4] {'y','core'}, dimensions={0}, use_global_device_ids=true | all-gather | bytes 2228224 | tf_op jit(solution)/shard_map/all_gather | solution.py:111
  31.6 0.0 copy-start.1
  31.6 0.0 copy-start.4
  31.6 0.0 copy-start
  31.6 0.6 multiply_convert_fusion.rows_ref
  32.3 0.1 copy-done.1
  32.3 0.0 copy-done.4
  32.3 0.6 copy-done
  32.9 2.3 %shard_map.64 = (bf16[4,144,512]{2,1,0:T(8,128)(2,1)S(1)}, s32[16,512]{1,0:T(8,128)S(1)}) custom-call(s32[1]{0:T(128)} %bitcast.core_ref, s32[1]{0:T(128)} %bitcast.1.rank_ref, bf16[1024,1024]{1,0:T(8,128)(2,1)S(1)} %multiply_convert_fusion.rows_ref, f32[1,1024]{1,0:T(1,128)S(1)} %bitcast.25, f32[1,1024]{1,0:T(1,128)S(1)} %bitcast.26, ...), custom_call_target="tpu_custom_call" | custom-call | tf_op jit(solution)/shard_map/pallas_call | solution.py:82
  35.2 0.0 copy-start.2
  35.2 12.7 %all_to_all.15 = bf16[4,144,512]{2,1,0:T(8,128)(2,1)S(1)} all-to-all(bf16[4,144,512]{2,1,0:T(8,128)(2,1)S(1)} %get-tuple-element.12), channel_id=1, replica_groups=mesh['dp'=8,'y'=8,'core'=2,'mp'=4] {'mp'}, dimensions={0} | all-to-all | bytes 1179648 | tf_op jit(solution)/shard_map/all_to_all | solution.py:116
  47.9 0.1 convert_reduce_fusion
  48.0 0.2 fusion.17
  48.2 0.8 broadcast_in_dim.26
  49.1 4.4 %all-to-all-start.1 = ((bf16[8,64,512]{2,1,0:T(8,128)(2,1)}), bf16[8,64,512]{2,1,0:T(8,128)(2,1)S(1)}, u32[]{:S(2)}, u32[]{:S(2)}) async-start(bf16[8,64,512]{2,1,0:T(8,128)(2,1)} %bitcast.8), calls=%async_computation.1 | async-start | bytes 1048576 | tf_op jit(solution)/shard_map/all_to_all | solution.py:130
  53.4 0.0 copy-done.2
  53.4 2.0 %collective-permute-start = (bf16[512,1024]{1,0:T(8,128)(2,1)S(1)}, bf16[512,1024]{1,0:T(8,128)(2,1)S(1)}, u32[]{:S(2)}, u32[]{:S(2)}) collective-permute-start(bf16[512,1024]{1,0:T(8,128)(2,1)S(1)} %copy-done.2), channel_id=1, source_target_pairs={{0,4},{4,0},{1,5},{5,1},{2,6},{6,2},{3,7},{7,3},{8,12},{12,8},{9,1... | collective-permute-start | bytes 3145736 | tf_op jit(solution)/shard_map/ppermute | solution.py:134
  55.5 0.1 reshape.45
  55.6 0.1 rev.3
  55.6 0.1 copy.9
  55.7 0.1 copy.10
  55.8 0.1 reshape.47
  55.9 0.1 reshape.46
  56.0 6.8 %all-to-all-done.1 = bf16[8,64,512]{2,1,0:T(8,128)(2,1)S(1)} async-done(((bf16[8,64,512]{2,1,0:T(8,128)(2,1)}), bf16[8,64,512]{2,1,0:T(8,128)(2,1)S(1)}, u32[]{:S(2)}, u32[]{:S(2)}) %all-to-all-start.1) | async-done | bytes 524320 | tf_op jit(solution)/shard_map/all_to_all | solution.py:130
  62.8 0.5 convolution_convert_fusion
  63.3 0.7 fusion.3
  64.0 0.0 collective-permute-done
  64.1 0.7 add_convert_fusion.1
  64.8 0.0 copy-start.3
  64.8 31.9 %all_to_all.16 = bf16[16,32,1024]{2,1,0:T(8,128)(2,1)S(1)} all-to-all(bf16[16,32,1024]{2,1,0:T(8,128)(2,1)S(1)} %bitcast.27), channel_id=1, replica_groups=mesh['dp'=8,'y'=8,'core'=2,'mp'=4] {'y','core'}, dimensions={0} | all-to-all | bytes 2097152 | tf_op jit(solution)/shard_map/all_to_all | solution.py:146
  96.7 0.0 copy-done.3
  96.7 1.8 %add_convert_fusion = bf16[512,1024]{1,0:T(8,128)(2,1)} fusion(bf16[512,1024]{1,0:T(8,128)(2,1)S(1)} %copy-done.3, bf16[512,1024]{1,0:T(8,128)(2,1)S(1)} %bitcast.29, s32[512]{0:T(512)S(1)} %fusion.22), kind=kOutput, calls=%fused_computation.1 | convolution fusion | flops 538705920 | bytes 3147776 | tf_op jit(solution)/shard_map/dot_general | solution.py:148
  (8 shorter events, 0.1 us)
Async XLA Ops:
  31.6 0.7 copy-start.1
  31.6 0.7 copy-start.4
  31.6 1.3 %copy-start = (bf16[1024,512]{1,0:T(8,128)(2,1)S(1)}, bf16[1024,512]{1,0:T(8,128)(2,1)}, u32[]{:S(2)}) copy-start(bf16[1024,512]{1,0:T(8,128)(2,1)} %w_ref.1) | copy-start | bytes 3145732
  35.2 18.2 %copy-start.2 = (bf16[512,1024]{1,0:T(8,128)(2,1)S(1)}, bf16[512,1024]{1,0:T(8,128)(2,1)}, u32[]{:S(2)}) copy-start(bf16[512,1024]{1,0:T(8,128)(2,1)} %param.11) | copy-start | bytes 3145732
  49.1 13.7 %all-to-all-start.1 = ((bf16[8,64,512]{2,1,0:T(8,128)(2,1)}), bf16[8,64,512]{2,1,0:T(8,128)(2,1)S(1)}, u32[]{:S(2)}, u32[]{:S(2)}) async-start(bf16[8,64,512]{2,1,0:T(8,128)(2,1)} %bitcast.8), calls=%async_computation.1 | async-start | bytes 1048576 | tf_op jit(solution)/shard_map/all_to_all | solution.py:130
  53.4 10.6 %collective-permute-start = (bf16[512,1024]{1,0:T(8,128)(2,1)S(1)}, bf16[512,1024]{1,0:T(8,128)(2,1)S(1)}, u32[]{:S(2)}, u32[]{:S(2)}) collective-permute-start(bf16[512,1024]{1,0:T(8,128)(2,1)S(1)} %copy-done.2), channel_id=1, source_target_pairs={{0,4},{4,0},{1,5},{5,1},{2,6},{6,2},{3,7},{7,3},{8,12},{12,8},{9,1... | collective-permute-start | bytes 3145736 | tf_op jit(solution)/shard_map/ppermute | solution.py:134
  64.8 31.9 %copy-start.3 = (bf16[512,1024]{1,0:T(8,128)(2,1)S(1)}, bf16[512,1024]{1,0:T(8,128)(2,1)}, u32[]{:S(2)}) copy-start(bf16[512,1024]{1,0:T(8,128)(2,1)} %param.6) | copy-start | bytes 3145732

commit v9 on v8

--- a/solution.py
+++ b/solution.py
@@ -91,6 +91,59 @@
     )(core.reshape(1), seq_rank.reshape(1), rows, gain, route, w_up)
 
 
+def gelu_kernel(packed_ref, out_ref):
+    parts, height, hidden_width = packed_ref.shape
+    chunk = height - 16
+    summed = packed_ref[0].astype(F32)
+    for m in range(1, parts):
+        summed += packed_ref[m].astype(F32)
+    sums = jnp.transpose(summed[chunk:, :chunk])
+    inverse = lax.rsqrt((sums[:, :1] + sums[:, 1:2]) / D + 1e-06)
+    scores = jax.nn.sigmoid((sums[:, 2:3] + sums[:, 3:4]) * inverse)
+    hidden = jax.nn.gelu(summed[:chunk] * inverse, approximate=True) * scores
+    hidden = hidden.astype(BF)
+    half = chunk // 2
+    for side in range(2):
+        for m in range(parts):
+            out_ref[side * parts + m] = hidden[side * half : (side + 1) * half]
+
+
+def gelu_call(packed):
+    parts, height, hidden_width = packed.shape
+    vmem = pl.BlockSpec(memory_space=pltpu.VMEM)
+    return pl.pallas_call(
+        gelu_kernel,
+        out_shape=jax.ShapeDtypeStruct((2 * parts, (height - 16) // 2, hidden_width), BF),
+        in_specs=[vmem],
+        out_specs=vmem,
+        compiler_params=pltpu.CompilerParams(vmem_limit_bytes=32 * 1024 * 1024),
+    )(packed)
+
+
+def place_kernel(targets_ref, terms_ref, tokens_ref, out_ref):
+    shape = (tokens_ref.shape[0], terms_ref.shape[0])
+    placer = (iota(shape, 0) == targets_ref[...]).astype(F32).astype(BF)
+    placed = jnp.dot(placer, terms_ref[...], preferred_element_type=F32)
+    out_ref[...] = (tokens_ref[...].astype(F32) + placed).astype(BF)
+
+
+def place_call(targets, terms, tokens):
+    count, width = terms.shape
+    block = width // 2
+    return pl.pallas_call(
+        place_kernel,
+        out_shape=jax.ShapeDtypeStruct(tokens.shape, BF),
+        grid=(2,),
+        in_specs=[
+            pl.BlockSpec((1, count), lambda i: (0, 0)),
+            pl.BlockSpec((count, block), lambda i: (0, i)),
+            pl.BlockSpec((tokens.shape[0], block), lambda i: (0, i)),
+        ],
+        out_specs=pl.BlockSpec((tokens.shape[0], block), lambda i: (0, i)),
+        compiler_params=pltpu.CompilerParams(vmem_limit_bytes=32 * 1024 * 1024),
+    )(targets.reshape(1, -1), terms, tokens)
+
+
 def per_device(tokens, heavy_index, norm_gain, router, w_up, w_down):
     tok_rows, width = tokens.shape
     slots = heavy_index.shape[0]
@@ -100,7 +153,6 @@
     core = lax.axis_index("core")
     used_rows = ROUTED
     share = slots // 2
-    chunk = used_rows // parts
     seq_rank = lax.axis_index("y") * 2 + core
     local_index = heavy_index - seq_rank * tok_rows
     token_iota = jnp.arange(tok_rows, dtype=I32)
@@ -120,15 +172,8 @@
     evens = jnp.broadcast_to(pairs[None], (chips, 2, share)).reshape(chips * slots)
     odds = jnp.broadcast_to(pairs[None, ::-1], (chips, 2, share)).reshape(chips * slots)
     targets = jnp.where(start % 2 == 0, evens, odds)
-    summed = jnp.sum(packed.astype(F32), axis=0)
-    sums = summed[chunk : chunk + 4, :chunk].T
-    inverse = lax.rsqrt((sums[:, :1] + sums[:, 1:2]) / D + 1e-06)
-    scores = jax.nn.sigmoid((sums[:, 2:3] + sums[:, 3:4]) * inverse)
-    hidden = jax.nn.gelu(summed[:chunk] * inverse, approximate=True) * scores
-    hidden = hidden.astype(BF).reshape(2, 1, chunk // 2, hidden_width)
-    hidden = jnp.broadcast_to(hidden, (2, parts, chunk // 2, hidden_width))
     hidden = lax.all_to_all(
-        hidden.reshape(2 * parts, chunk // 2, hidden_width), ("core", "mp"), 0, 0, tiled=True
+        gelu_call(packed), ("core", "mp"), 0, 0, tiled=True
     ).reshape(2, used_rows // 2, hidden_width)
     hidden, targets = lax.optimization_barrier((hidden, targets))
     w_near = lax.ppermute(w_down, "core", [(0, 1), (1, 0)])
@@ -144,11 +189,7 @@
     down += jnp.dot(wanted[:, hidden_width:], w_near, preferred_element_type=F32)
     chip_sum = down.astype(BF).reshape(2 * chips, share, width)
     terms = lax.all_to_all(chip_sum, ("y", "core"), 0, 0, tiled=True).reshape(-1, width)
-    placer = (targets[:, None] == token_iota[None, :]).astype(BF)
-    placed = lax.dot_general(
-        placer, terms, (((0,), (0,)), ((), ())), preferred_element_type=F32
-    )
-    return (tokens.astype(F32) + placed).astype(BF)
+    return place_call(targets, terms, tokens)
 
 
 def solution(mesh):

time: 98.9 us -> 99 us (level)
  Pallas kernels: 2.33 us -> 5.32 us
  matrix products: 5.31 us -> 3.5 us
    pallas_call x0 -> x2, Pallas kernels: none -> 2.99 us  [the longest x1 1.84 us: place_call(): pl.pallas_call(place_kernel, out_shape=jax.ShapeDtypeStruct(tokens.shape,...]
    dot_general x1 -> x0, matrix products: 1.81 us -> none  [per_device(): lax.dot_general(placer, terms, (((0,), (0,)), ((), ())), preferred_elemen...]
where the time goes in v9:
time: 99 us; the launch traced here: 98.6 us
  blocking collectives  74 us (75%)
  waiting for transfers between devices  6.8 us (7%)
  starting transfers between devices  6.38 us (6%)
  Pallas kernels  5.32 us (5%)
  matrix products  3.5 us (4%)
  other arithmetic  1.32 us (1%)
  local copies, waits for them, and re-layouts  1.16 us (1%)
    all_to_all x1, blocking collectives, per_device(): lax.all_to_all(chip_sum, ('y', 'core'), 0, 0, tiled=True).reshape(-1, width)  31.9 us
    all_gather x1, blocking collectives, per_device(): lax.all_gather((selected * SCALE).astype(F16), ('y', 'core'), tiled=True)  29.4 us
    all_to_all x1, blocking collectives, per_device(): packed = lax.all_to_all(packed, 'mp', 0, 0, tiled=True)  12.7 us
    all_to_all x1, waiting for transfers between devices, per_device(): lax.all_to_all(gelu_call(packed), ('core', 'mp'), 0, 0, tiled=True)  6.8 us
    all_to_all x1, starting transfers between devices, per_device(): lax.all_to_all(gelu_call(packed), ('core', 'mp'), 0, 0, tiled=True)  4.38 us
    pallas_call x1, Pallas kernels, up_call(): pl.pallas_call(functools.partial(up_kernel, slots), out_shape=(jax.ShapeD...  2.33 us
    ppermute x1, starting transfers between devices, per_device(): w_near = lax.ppermute(w_down, 'core', [(0, 1), (1, 0)])  2 us
  transfers between devices with their start and end apart: 2, of which 1 were waited for; matrix products, arithmetic and copies ran while one was open for 2% of the time, Pallas kernels for 0%

profile of v9, /device:TPU:1, one launch (start us, length us, event | category | flops | bytes accessed | tf_op | source)
XLA Modules:
  0.0 98.6 jit_solution(16112133345925639331)
XLA Ops:
  0.0 0.7 broadcast_compare_fusion
  0.7 1.6 %fusion.1 = f16[64,1024]{1,0:T(8,128)(2,1)S(1)} fusion(bf16[512,1024]{1,0:T(8,128)(2,1)} %tokens_ref.1, pred[64]{0:T(512)(128)(4,1)S(1)} %get-tuple-element.19, s32[64]{0:T(128)S(1)} %get-tuple-element.16), kind=kOutput, calls=%fused_computation.5 | convolution fusion | flops 67338240 | bytes 1179968 | tf_op jit(solution)/shard_map/dot_general | solution.py:160
  2.2 29.4 %all-gather.1 = f16[1024,1024]{1,0:T(8,128)(2,1)S(1)} all-gather(f16[64,1024]{1,0:T(8,128)(2,1)S(1)} %fusion.1), channel_id=1, replica_groups=mesh['dp'=8,'y'=8,'core'=2,'mp'=4] {'y','core'}, dimensions={0}, use_global_device_ids=true | all-gather | bytes 2228224 | tf_op jit(solution)/shard_map/all_gather | solution.py:163
  31.6 0.0 copy-start.2
  31.6 0.0 copy-start.4
  31.6 0.0 copy-start.1
  31.6 0.6 multiply_convert_fusion.rows_ref
  32.3 0.1 copy-done.2
  32.3 0.0 copy-done.4
  32.3 0.6 copy-done.1
  32.9 2.3 %shard_map.64 = (bf16[4,144,512]{2,1,0:T(8,128)(2,1)S(1)}, s32[16,512]{1,0:T(8,128)S(1)}) custom-call(s32[1]{0:T(128)} %bitcast.core_ref, s32[1]{0:T(128)} %bitcast.1.rank_ref, bf16[1024,1024]{1,0:T(8,128)(2,1)S(1)} %multiply_convert_fusion.rows_ref, f32[1,1024]{1,0:T(1,128)S(1)} %bitcast.19, f32[1,1024]{1,0:T(1,128)S(1)} %bitcast.20, ...), custom_call_target="tpu_custom_call" | custom-call | tf_op jit(solution)/shard_map/pallas_call | solution.py:82
  35.2 0.0 copy-start.3
  35.2 12.7 %all_to_all.15.packed_ref = bf16[4,144,512]{2,1,0:T(8,128)(2,1)S(1)} all-to-all(bf16[4,144,512]{2,1,0:T(8,128)(2,1)S(1)} %get-tuple-element.12), channel_id=1, replica_groups=mesh['dp'=8,'y'=8,'core'=2,'mp'=4] {'mp'}, dimensions={0} | all-to-all | bytes 1179648 | tf_op jit(solution)/shard_map/all_to_all | solution.py:168
  47.9 1.1 %shard_map.65 = bf16[8,64,512]{2,1,0:T(8,128)(2,1)} custom-call(bf16[4,144,512]{2,1,0:T(8,128)(2,1)S(1)} %all_to_all.15.packed_ref), custom_call_target="tpu_custom_call" | custom-call | tf_op jit(solution)/shard_map/pallas_call | solution.py:114
  49.1 4.4 %all-to-all-start.1 = ((bf16[8,64,512]{2,1,0:T(8,128)(2,1)}), bf16[8,64,512]{2,1,0:T(8,128)(2,1)S(1)}, u32[]{:S(2)}, u32[]{:S(2)}) async-start(bf16[8,64,512]{2,1,0:T(8,128)(2,1)} %shard_map.65), calls=%async_computation.1 | async-start | bytes 1048576 | tf_op jit(solution)/shard_map/all_to_all | solution.py:175
  53.4 0.0 copy-done.3
  53.5 2.0 %collective-permute-start = (bf16[512,1024]{1,0:T(8,128)(2,1)S(1)}, bf16[512,1024]{1,0:T(8,128)(2,1)S(1)}, u32[]{:S(2)}, u32[]{:S(2)}) collective-permute-start(bf16[512,1024]{1,0:T(8,128)(2,1)S(1)} %copy-done.3), channel_id=1, source_target_pairs={{0,4},{4,0},{1,5},{5,1},{2,6},{6,2},{3,7},{7,3},{8,12},{12,8},{9,1... | collective-permute-start | bytes 3145736 | tf_op jit(solution)/shard_map/ppermute | solution.py:179
  55.5 0.1 reshape.41
  55.6 0.1 copy.9
  55.7 0.1 rev.3
  55.7 0.1 reshape.42
  55.8 0.1 copy.10
  55.9 0.1 reshape.43
  56.0 6.8 %all-to-all-done.1 = bf16[8,64,512]{2,1,0:T(8,128)(2,1)S(1)} async-done(((bf16[8,64,512]{2,1,0:T(8,128)(2,1)}), bf16[8,64,512]{2,1,0:T(8,128)(2,1)S(1)}, u32[]{:S(2)}, u32[]{:S(2)}) %all-to-all-start.1) | async-done | bytes 524320 | tf_op jit(solution)/shard_map/all_to_all | solution.py:175
  62.9 0.5 convolution_convert_fusion
  63.3 0.7 fusion.3
  64.1 0.0 collective-permute-done
  64.1 0.8 add_convert_fusion
  64.8 0.0 copy-start
  64.8 31.9 %all_to_all.16 = bf16[16,32,1024]{2,1,0:T(8,128)(2,1)S(1)} all-to-all(bf16[16,32,1024]{2,1,0:T(8,128)(2,1)S(1)} %bitcast.22), channel_id=1, replica_groups=mesh['dp'=8,'y'=8,'core'=2,'mp'=4] {'y','core'}, dimensions={0} | all-to-all | bytes 2097152 | tf_op jit(solution)/shard_map/all_to_all | solution.py:191
  96.7 0.0 copy-done
  96.7 1.8 %shard_map.66 = bf16[512,1024]{1,0:T(8,128)(2,1)} custom-call(s32[1,512]{1,0:T(1,128)S(1)} %bitcast.21, bf16[512,1024]{1,0:T(8,128)(2,1)S(1)} %bitcast.18, bf16[512,1024]{1,0:T(8,128)(2,1)S(1)} %copy-done), custom_call_target="tpu_custom_call" | custom-call | tf_op jit(solution)/shard_map/pallas_call | solution.py:133
  (6 shorter events, 0.1 us)
Async XLA Ops:
  31.6 0.7 copy-start.2
  31.6 0.7 copy-start.4
  31.6 1.3 %copy-start.1 = (bf16[1024,512]{1,0:T(8,128)(2,1)S(1)}, bf16[1024,512]{1,0:T(8,128)(2,1)}, u32[]{:S(2)}) copy-start(bf16[1024,512]{1,0:T(8,128)(2,1)} %w_ref.1) | copy-start | bytes 3145732
  35.2 18.2 %copy-start.3 = (bf16[512,1024]{1,0:T(8,128)(2,1)S(1)}, bf16[512,1024]{1,0:T(8,128)(2,1)}, u32[]{:S(2)}) copy-start(bf16[512,1024]{1,0:T(8,128)(2,1)} %param.11) | copy-start | bytes 3145732
  49.1 13.7 %all-to-all-start.1 = ((bf16[8,64,512]{2,1,0:T(8,128)(2,1)}), bf16[8,64,512]{2,1,0:T(8,128)(2,1)S(1)}, u32[]{:S(2)}, u32[]{:S(2)}) async-start(bf16[8,64,512]{2,1,0:T(8,128)(2,1)} %shard_map.65), calls=%async_computation.1 | async-start | bytes 1048576 | tf_op jit(solution)/shard_map/all_to_all | solution.py:175
  53.5 10.6 %collective-permute-start = (bf16[512,1024]{1,0:T(8,128)(2,1)S(1)}, bf16[512,1024]{1,0:T(8,128)(2,1)S(1)}, u32[]{:S(2)}, u32[]{:S(2)}) collective-permute-start(bf16[512,1024]{1,0:T(8,128)(2,1)S(1)} %copy-done.3), channel_id=1, source_target_pairs={{0,4},{4,0},{1,5},{5,1},{2,6},{6,2},{3,7},{7,3},{8,12},{12,8},{9,1... | collective-permute-start | bytes 3145736 | tf_op jit(solution)/shard_map/ppermute | solution.py:179
  64.8 31.9 %copy-start = (bf16[512,1024]{1,0:T(8,128)(2,1)S(1)}, bf16[512,1024]{1,0:T(8,128)(2,1)}, u32[]{:S(2)}) copy-start(bf16[512,1024]{1,0:T(8,128)(2,1)} %tokens_ref.1) | copy-start | bytes 3145732

commit v10 on v8

--- a/solution.py
+++ b/solution.py
@@ -23,7 +23,7 @@
 
 
 def up_kernel(
-    slots, core_ref, rank_ref, rows_ref, gain_ref, route_ref, w_ref, out_ref, place_ref
+    slots, tok_rows, core_ref, rank_ref, index_ref, rows_ref, gain_ref, route_ref, w_ref, out_ref, place_ref
 ):
     count = rows_ref.shape[0]
     parts = out_ref.shape[0]
@@ -55,7 +55,17 @@
     first, number = owners_of(iota((1, count // 2), 1) // share)
     row = first + (first + core) % 2 + 2 * (iota((8, count // 2), 1) % share)
     place_ref[:8] = jnp.where(row < first + number, (row - core) // 2, -1)
-    place_ref[8:] = owners_of(jnp.full((1, count // 2), seq_rank, I32))[0]
+    start = owners_of(jnp.full((1, count // 2), seq_rank, I32))[0]
+    lanes = iota((1, count // 2), 1)
+    sent = 2 * (lanes % share) + (start[:1] + lanes // share) % 2
+    chosen = (iota((slots, count // 2), 0) == sent).astype(F32).astype(BF)
+    local = index_ref[...] - seq_rank * tok_rows
+    local = jnp.broadcast_to(jnp.where(local < 0, -1, local), (8, slots))
+    upper = (local >> 7).astype(F32).astype(BF)
+    lower = (local & 127).astype(F32).astype(BF)
+    target = 128.0 * jnp.dot(upper, chosen, preferred_element_type=F32)
+    target += jnp.dot(lower, chosen, preferred_element_type=F32)
+    place_ref[8:] = target.astype(I32)
 
     compactor = (iota((total, count), 0) == spot[:1]).astype(F32).astype(BF)
     raw = jnp.dot(compactor, rows_ref[...], preferred_element_type=F32)
@@ -77,18 +87,18 @@
         out_ref[m, chunk:, :128] = sums[:, m * chunk : (m + 1) * chunk]
 
 
-def up_call(core, seq_rank, rows, gain, route, w_up, slots, parts):
+def up_call(core, seq_rank, index, tok_rows, rows, gain, route, w_up, slots, parts):
     vmem = pl.BlockSpec(memory_space=pltpu.VMEM)
     return pl.pallas_call(
-        functools.partial(up_kernel, slots),
+        functools.partial(up_kernel, slots, tok_rows),
         out_shape=(
             jax.ShapeDtypeStruct((parts, ROUTED // parts + 16, w_up.shape[1]), BF),
             jax.ShapeDtypeStruct((16, rows.shape[0] // 2), I32),
         ),
-        in_specs=[pl.BlockSpec(memory_space=pltpu.SMEM)] * 2 + [vmem] * 4,
+        in_specs=[pl.BlockSpec(memory_space=pltpu.SMEM)] * 2 + [vmem] * 5,
         out_specs=(vmem, vmem),
         compiler_params=pltpu.CompilerParams(vmem_limit_bytes=40 * 1024 * 1024),
-    )(core.reshape(1), seq_rank.reshape(1), rows, gain, route, w_up)
+    )(core.reshape(1), seq_rank.reshape(1), index.reshape(1, -1), rows, gain, route, w_up)
 
 
 def per_device(tokens, heavy_index, norm_gain, router, w_up, w_down):
@@ -109,17 +119,20 @@
     selected = jnp.where(local_index[:, None] >= 0, selected, EMPTY)
 
     rows = lax.all_gather((selected * SCALE).astype(F16), ("y", "core"), tiled=True)
+    rows, w_here = lax.optimization_barrier((rows, w_down))
+    w_near = lax.ppermute(w_here, "core", [(0, 1), (1, 0)])
     rows = (rows.astype(F32) * (1.0 / SCALE)).astype(BF)
     gain = norm_gain[None]
     route = gain * router.astype(F32)[None]
-    packed, place = up_call(core, seq_rank, rows, gain, route, w_up, slots, parts)
+    packed, place = up_call(
+        core, seq_rank, heavy_index, tok_rows, rows, gain, route, w_up, slots, parts
+    )
+    lower_core = jnp.broadcast_to(core == 0, (1, 1))
+    packed, mine, targets, lower_core = lax.optimization_barrier(
+        (packed, place[0], place[8], lower_core)
+    )
     packed = lax.all_to_all(packed, "mp", 0, 0, tiled=True)
-    packed, place, local_index = lax.optimization_barrier((packed, place, local_index))
-    mine, start = place[0], place[8]
-    pairs = local_index.reshape(share, 2).T
-    evens = jnp.broadcast_to(pairs[None], (chips, 2, share)).reshape(chips * slots)
-    odds = jnp.broadcast_to(pairs[None, ::-1], (chips, 2, share)).reshape(chips * slots)
-    targets = jnp.where(start % 2 == 0, evens, odds)
+    packed, w_near = lax.optimization_barrier((packed, w_near))
     summed = jnp.sum(packed.astype(F32), axis=0)
     sums = summed[chunk : chunk + 4, :chunk].T
     inverse = lax.rsqrt((sums[:, :1] + sums[:, 1:2]) / D + 1e-06)
@@ -130,10 +143,8 @@
     hidden = lax.all_to_all(
         hidden.reshape(2 * parts, chunk // 2, hidden_width), ("core", "mp"), 0, 0, tiled=True
     ).reshape(2, used_rows // 2, hidden_width)
-    hidden, targets = lax.optimization_barrier((hidden, targets))
-    w_near = lax.ppermute(w_down, "core", [(0, 1), (1, 0)])
-    here = jnp.where(core == 0, hidden[0], hidden[1])
-    near = jnp.where(core == 0, hidden[1], hidden[0])
+    here = jnp.where(lower_core, hidden[0], hidden[1])
+    near = jnp.where(lower_core, hidden[1], hidden[0])
 
     expander = (mine[:, None] == jnp.arange(used_rows // 2, dtype=I32)[None, :]).astype(BF)
     wanted = jnp.dot(

time: 98.9 us -> 100 us (1.011)
  blocking collectives: 74 us -> 86.6 us
  waiting for transfers between devices: 6.8 us -> 0.01 us
  starting transfers between devices: 6.38 us -> 2.05 us
  local copies, waits for them, and re-layouts: 2 us -> 0.67 us
  matrix products: 5.31 us -> 6.55 us
    all_to_all x0 -> x1, blocking collectives: none -> 13.3 us  [per_device(): lax.all_to_all(hidden.reshape(2 * parts, chunk // 2, hidden_width), ('cor...]
    all_to_all x1 -> x0, waiting for transfers between devices: 6.8 us -> none  [per_device(): lax.all_to_all(hidden.reshape(2 * parts, chunk // 2, hidden_width), ('cor...]
    all_to_all x1 -> x0, starting transfers between devices: 4.38 us -> none  [per_device(): lax.all_to_all(hidden.reshape(2 * parts, chunk // 2, hidden_width), ('cor...]
    dot_general x1, matrix products: 0.75 us -> 1.97 us  [per_device(): jnp.dot(wanted[:, hidden_width:], w_near, preferred_element_type=F32)]
  transfers between devices with their start and end apart: 2 -> 1, of which waited for: 1 -> 0; matrix products, arithmetic and copies ran while one was open for 2% -> 1% of each run, Pallas kernels for 0% -> 2%
where the time goes in v10:
time: 100 us
  blocking collectives  86.6 us (87%)
  matrix products  6.55 us (7%)
  Pallas kernels  2.44 us (2%)
  starting transfers between devices  2.05 us (2%)
  other arithmetic  1.67 us (2%)
    all_to_all x1, blocking collectives, per_device(): lax.all_to_all(chip_sum, ('y', 'core'), 0, 0, tiled=True).reshape(-1, width)  31.9 us
    all_gather x1, blocking collectives, per_device(): lax.all_gather((selected * SCALE).astype(F16), ('y', 'core'), tiled=True)  29.4 us
    all_to_all x1, blocking collectives, per_device(): lax.all_to_all(hidden.reshape(2 * parts, chunk // 2, hidden_width), ('cor...  13.3 us
    all_to_all x1, blocking collectives, per_device(): packed = lax.all_to_all(packed, 'mp', 0, 0, tiled=True)  12 us
    pallas_call x1, Pallas kernels, up_call(): pl.pallas_call(functools.partial(up_kernel, slots, tok_rows), out_shape=(...  2.44 us
    ppermute x1, starting transfers between devices, per_device(): w_near = lax.ppermute(w_here, 'core', [(0, 1), (1, 0)])  2.05 us
  transfers between devices with their start and end apart: 1, of which 0 were waited for; matrix products, arithmetic and copies ran while one was open for 1% of the time, Pallas kernels for 2%

profile of v10, /device:TPU:1, one launch (start us, length us, event | category | flops | bytes accessed | tf_op | source)
XLA Modules:
  0.0 100.1 jit_solution(13841443194110511793)
XLA Ops:
  0.0 0.0 copy-start.3
  0.0 0.0 copy-start.1
  0.0 0.0 copy-start.5
  0.0 0.7 broadcast_compare_fusion
  0.8 1.6 %fusion.1 = f16[64,1024]{1,0:T(8,128)(2,1)S(1)} fusion(bf16[512,1024]{1,0:T(8,128)(2,1)} %param.6, pred[64]{0:T(512)(128)(4,1)S(1)} %get-tuple-element.27, s32[64]{0:T(128)S(1)} %get-tuple-element.28), kind=kOutput, calls=%fused_computation.7 | convolution fusion | flops 67338240 | bytes 1179968 | tf_op jit(solution)/shard_map/dot_general | solution.py:118
  2.3 29.4 %all-gather.1 = f16[1024,1024]{1,0:T(8,128)(2,1)S(1)} all-gather(f16[64,1024]{1,0:T(8,128)(2,1)S(1)} %fusion.1), channel_id=1, replica_groups=mesh['dp'=8,'y'=8,'core'=2,'mp'=4] {'y','core'}, dimensions={0}, use_global_device_ids=true | all-gather | bytes 2228224 | tf_op jit(solution)/shard_map/all_gather | solution.py:121
  31.7 0.0 copy-done.3
  31.7 2.0 %collective-permute-start = (bf16[512,1024]{1,0:T(8,128)(2,1)S(1)}, bf16[512,1024]{1,0:T(8,128)(2,1)}, u32[]{:S(2)}, u32[]{:S(2)}) collective-permute-start(bf16[512,1024]{1,0:T(8,128)(2,1)S(1)} %copy-done.3), channel_id=1, source_target_pairs={{0,4},{4,0},{1,5},{5,1},{2,6},{6,2},{3,7},{7,3},{8,12},{12,8},{9,1... | collective-permute-start | bytes 3145736 | tf_op jit(solution)/shard_map/ppermute | solution.py:123
  33.8 0.0 copy-done.1
  33.8 0.0 copy-done.5
  33.8 0.0 copy-start
  33.8 0.0 copy-start.2
  33.8 0.6 multiply_convert_fusion.rows_ref
  34.5 0.6 copy-done
  35.0 0.0 copy-done.2
  35.1 2.4 %shard_map.64 = (bf16[4,144,512]{2,1,0:T(8,128)(2,1)S(1)}, s32[16,512]{1,0:T(8,128)S(1)}) custom-call(s32[1]{0:T(128)} %bitcast.core_ref, s32[1]{0:T(128)} %bitcast.1.rank_ref, s32[1,64]{1,0:T(1,128)S(1)} %bitcast.26, bf16[1024,1024]{1,0:T(8,128)(2,1)S(1)} %multiply_convert_fusion.rows_ref, f32[1,1024]{1,0:T(1,128)S(1)} %bitcast.24, f32[1,1024]{1,0:T(1,128)S(1)} %bitcast.25, ...), custom_call_target="tpu_custom_call" | custom-call | tf_op jit(solution)/shard_map/pallas_call | solution.py:92
  37.5 12.0 %all_to_all.15 = bf16[4,144,512]{2,1,0:T(8,128)(2,1)S(1)} all-to-all(bf16[4,144,512]{2,1,0:T(8,128)(2,1)S(1)} %get-tuple-element.21), channel_id=1, replica_groups=mesh['dp'=8,'y'=8,'core'=2,'mp'=4] {'mp'}, dimensions={0} | all-to-all | bytes 1179648 | tf_op jit(solution)/shard_map/all_to_all | solution.py:134
  49.5 0.0 collective-permute-done
  49.5 0.1 convert_reduce_fusion
  49.7 0.2 fusion.17
  49.9 13.3 %all_to_all.16 = bf16[8,64,512]{2,1,0:T(8,128)(2,1)S(1)} all-to-all(bf16[8,64,512]{2,1,0:T(8,128)(2,1)S(1)} %bitcast.28), channel_id=1, replica_groups=mesh['dp'=8,'y'=8,'core'=2,'mp'=4] {'core','mp'}, dimensions={0} | all-to-all | bytes 1048576 | tf_op jit(solution)/shard_map/all_to_all | solution.py:143
  63.2 0.5 convolution_convert_fusion
  63.7 0.7 fusion.3
  64.4 2.0 %add_convert_fusion.1 = bf16[512,1024]{1,0:T(8,128)(2,1)S(1)} fusion(f32[512,1024]{1,0:T(8,128)S(1)} %fusion.3, bf16[512,1024]{1,0:T(8,128)(2,1)} %collective-permute-done, bf16[512,1024]{1,0:T(8,128)(2,1)S(1)} %convolution_convert_fusion), kind=kOutput, calls=%fused_computation.2 | convolution fusion | flops 537919488 | bytes 4718592 | tf_op jit(solution)/shard_map/dot_general | solution.py:155
  66.4 0.0 copy-start.4
  66.4 31.9 %all_to_all.17 = bf16[16,32,1024]{2,1,0:T(8,128)(2,1)S(1)} all-to-all(bf16[16,32,1024]{2,1,0:T(8,128)(2,1)S(1)} %bitcast.27), channel_id=1, replica_groups=mesh['dp'=8,'y'=8,'core'=2,'mp'=4] {'y','core'}, dimensions={0} | all-to-all | bytes 2097152 | tf_op jit(solution)/shard_map/all_to_all | solution.py:157
  98.3 0.0 copy-done.4
  98.3 1.8 %add_convert_fusion = bf16[512,1024]{1,0:T(8,128)(2,1)} fusion(bf16[512,1024]{1,0:T(8,128)(2,1)S(1)} %copy-done.4, bf16[512,1024]{1,0:T(8,128)(2,1)S(1)} %bitcast.29, s32[512]{0:T(512)S(1)} %bitcast.34), kind=kOutput, calls=%fused_computation.1 | convolution fusion | flops 538705920 | bytes 3147776 | tf_op jit(solution)/shard_map/dot_general | solution.py:159
  (6 shorter events, 0.1 us)
Async XLA Ops:
  0.0 31.7 %copy-start.3 = (bf16[512,1024]{1,0:T(8,128)(2,1)S(1)}, bf16[512,1024]{1,0:T(8,128)(2,1)}, u32[]{:S(2)}) copy-start(bf16[512,1024]{1,0:T(8,128)(2,1)} %param.11) | copy-start | bytes 3145732
  0.0 33.8 %copy-start.1 = (f32[1024]{0:T(1024)S(1)}, f32[1024]{0:T(1024)}, u32[]{:S(2)}) copy-start(f32[1024]{0:T(1024)} %param.8) | copy-start | bytes 12292
  0.0 33.8 %copy-start.5 = (bf16[1024]{0:T(1024)(128)(2,1)S(1)}, bf16[1024]{0:T(1024)(128)(2,1)}, u32[]{:S(2)}) copy-start(bf16[1024]{0:T(1024)(128)(2,1)} %param.9) | copy-start | bytes 6148
  31.7 17.8 %collective-permute-start = (bf16[512,1024]{1,0:T(8,128)(2,1)S(1)}, bf16[512,1024]{1,0:T(8,128)(2,1)}, u32[]{:S(2)}, u32[]{:S(2)}) collective-permute-start(bf16[512,1024]{1,0:T(8,128)(2,1)S(1)} %copy-done.3), channel_id=1, source_target_pairs={{0,4},{4,0},{1,5},{5,1},{2,6},{6,2},{3,7},{7,3},{8,12},{12,8},{9,1... | collective-permute-start | bytes 3145736 | tf_op jit(solution)/shard_map/ppermute | solution.py:123
  33.8 1.2 %copy-start = (bf16[1024,512]{1,0:T(8,128)(2,1)S(1)}, bf16[1024,512]{1,0:T(8,128)(2,1)}, u32[]{:S(2)}) copy-start(bf16[1024,512]{1,0:T(8,128)(2,1)} %w_ref.1) | copy-start | bytes 3145732
  33.8 1.2 %copy-start.2 = (s32[64]{0:T(128)S(1)}, s32[64]{0:T(128)}, u32[]{:S(2)}) copy-start(s32[64]{0:T(128)} %param.7) | copy-start | bytes 772
  66.4 31.9 %copy-start.4 = (bf16[512,1024]{1,0:T(8,128)(2,1)S(1)}, bf16[512,1024]{1,0:T(8,128)(2,1)}, u32[]{:S(2)}) copy-start(bf16[512,1024]{1,0:T(8,128)(2,1)} %param.6) | copy-start | bytes 3145732

commit v11 on v9

--- a/solution.py
+++ b/solution.py
@@ -120,30 +120,6 @@
     )(packed)
 
 
-def place_kernel(targets_ref, terms_ref, tokens_ref, out_ref):
-    shape = (tokens_ref.shape[0], terms_ref.shape[0])
-    placer = (iota(shape, 0) == targets_ref[...]).astype(F32).astype(BF)
-    placed = jnp.dot(placer, terms_ref[...], preferred_element_type=F32)
-    out_ref[...] = (tokens_ref[...].astype(F32) + placed).astype(BF)
-
-
-def place_call(targets, terms, tokens):
-    count, width = terms.shape
-    block = width // 2
-    return pl.pallas_call(
-        place_kernel,
-        out_shape=jax.ShapeDtypeStruct(tokens.shape, BF),
-        grid=(2,),
-        in_specs=[
-            pl.BlockSpec((1, count), lambda i: (0, 0)),
-            pl.BlockSpec((count, block), lambda i: (0, i)),
-            pl.BlockSpec((tokens.shape[0], block), lambda i: (0, i)),
-        ],
-        out_specs=pl.BlockSpec((tokens.shape[0], block), lambda i: (0, i)),
-        compiler_params=pltpu.CompilerParams(vmem_limit_bytes=32 * 1024 * 1024),
-    )(targets.reshape(1, -1), terms, tokens)
-
-
 def per_device(tokens, heavy_index, norm_gain, router, w_up, w_down):
     tok_rows, width = tokens.shape
     slots = heavy_index.shape[0]
@@ -189,7 +165,11 @@
     down += jnp.dot(wanted[:, hidden_width:], w_near, preferred_element_type=F32)
     chip_sum = down.astype(BF).reshape(2 * chips, share, width)
     terms = lax.all_to_all(chip_sum, ("y", "core"), 0, 0, tiled=True).reshape(-1, width)
-    return place_call(targets, terms, tokens)
+    placer = (targets[:, None] == token_iota[None, :]).astype(BF)
+    placed = lax.dot_general(
+        placer, terms, (((0,), (0,)), ((), ())), preferred_element_type=F32
+    )
+    return (tokens.astype(F32) + placed).astype(BF)
 
 
 def solution(mesh):

time: 99 us -> 98.9 us (level)
  Pallas kernels: 5.32 us -> 3.48 us
  matrix products: 3.5 us -> 5.31 us
    pallas_call x1 -> x0, Pallas kernels: 1.84 us -> none  [place_call(): pl.pallas_call(place_kernel, out_shape=jax.ShapeDtypeStruct(tokens.shape,...]
    dot_general x0 -> x1, matrix products: none -> 1.81 us  [per_device(): lax.dot_general(placer, terms, (((0,), (0,)), ((), ())), preferred_elemen...]
where the time goes in v11:
time: 98.9 us; the launch traced here: 98.6 us
  blocking collectives  74 us (75%)
  waiting for transfers between devices  6.8 us (7%)
  starting transfers between devices  6.38 us (6%)
  matrix products  5.31 us (5%)
  Pallas kernels  3.48 us (4%)
  other arithmetic  1.33 us (1%)
  local copies, waits for them, and re-layouts  1.16 us (1%)
    all_to_all x1, blocking collectives, per_device(): lax.all_to_all(chip_sum, ('y', 'core'), 0, 0, tiled=True).reshape(-1, width)  31.9 us
    all_gather x1, blocking collectives, per_device(): lax.all_gather((selected * SCALE).astype(F16), ('y', 'core'), tiled=True)  29.4 us
    all_to_all x1, blocking collectives, per_device(): packed = lax.all_to_all(packed, 'mp', 0, 0, tiled=True)  12.7 us
    all_to_all x1, waiting for transfers between devices, per_device(): lax.all_to_all(gelu_call(packed), ('core', 'mp'), 0, 0, tiled=True)  6.8 us
    all_to_all x1, starting transfers between devices, per_device(): lax.all_to_all(gelu_call(packed), ('core', 'mp'), 0, 0, tiled=True)  4.38 us
    pallas_call x1, Pallas kernels, up_call(): pl.pallas_call(functools.partial(up_kernel, slots), out_shape=(jax.ShapeD...  2.33 us
    ppermute x1, starting transfers between devices, per_device(): w_near = lax.ppermute(w_down, 'core', [(0, 1), (1, 0)])  2 us
  transfers between devices with their start and end apart: 2, of which 1 were waited for; matrix products, arithmetic and copies ran while one was open for 2% of the time, Pallas kernels for 0%

profile of v11, /device:TPU:1, one launch (start us, length us, event | category | flops | bytes accessed | tf_op | source)
XLA Modules:
  0.0 98.6 jit_solution(9472316999373373341)
XLA Ops:
  0.0 0.7 broadcast_compare_fusion
  0.7 1.6 %fusion.1 = f16[64,1024]{1,0:T(8,128)(2,1)S(1)} fusion(bf16[512,1024]{1,0:T(8,128)(2,1)} %param.6, pred[64]{0:T(512)(128)(4,1)S(1)} %get-tuple-element.19, s32[64]{0:T(128)S(1)} %get-tuple-element.16), kind=kOutput, calls=%fused_computation.6 | convolution fusion | flops 67338240 | bytes 1179968 | tf_op jit(solution)/shard_map/dot_general | solution.py:136
  2.2 29.4 %all-gather.1 = f16[1024,1024]{1,0:T(8,128)(2,1)S(1)} all-gather(f16[64,1024]{1,0:T(8,128)(2,1)S(1)} %fusion.1), channel_id=1, replica_groups=mesh['dp'=8,'y'=8,'core'=2,'mp'=4] {'y','core'}, dimensions={0}, use_global_device_ids=true | all-gather | bytes 2228224 | tf_op jit(solution)/shard_map/all_gather | solution.py:139
  31.6 0.0 copy-start.1
  31.6 0.0 copy-start.4
  31.6 0.0 copy-start
  31.6 0.6 multiply_convert_fusion.rows_ref
  32.3 0.1 copy-done.1
  32.3 0.0 copy-done.4
  32.3 0.6 copy-done
  32.9 2.3 %shard_map.64 = (bf16[4,144,512]{2,1,0:T(8,128)(2,1)S(1)}, s32[16,512]{1,0:T(8,128)S(1)}) custom-call(s32[1]{0:T(128)} %bitcast.core_ref, s32[1]{0:T(128)} %bitcast.1.rank_ref, bf16[1024,1024]{1,0:T(8,128)(2,1)S(1)} %multiply_convert_fusion.rows_ref, f32[1,1024]{1,0:T(1,128)S(1)} %bitcast.18, f32[1,1024]{1,0:T(1,128)S(1)} %bitcast.19, ...), custom_call_target="tpu_custom_call" | custom-call | tf_op jit(solution)/shard_map/pallas_call | solution.py:82
  35.2 0.0 copy-start.2
  35.2 12.7 %all_to_all.15.packed_ref = bf16[4,144,512]{2,1,0:T(8,128)(2,1)S(1)} all-to-all(bf16[4,144,512]{2,1,0:T(8,128)(2,1)S(1)} %get-tuple-element.12), channel_id=1, replica_groups=mesh['dp'=8,'y'=8,'core'=2,'mp'=4] {'mp'}, dimensions={0} | all-to-all | bytes 1179648 | tf_op jit(solution)/shard_map/all_to_all | solution.py:144
  47.9 1.1 %shard_map.65 = bf16[8,64,512]{2,1,0:T(8,128)(2,1)} custom-call(bf16[4,144,512]{2,1,0:T(8,128)(2,1)S(1)} %all_to_all.15.packed_ref), custom_call_target="tpu_custom_call" | custom-call | tf_op jit(solution)/shard_map/pallas_call | solution.py:114
  49.1 4.4 %all-to-all-start.1 = ((bf16[8,64,512]{2,1,0:T(8,128)(2,1)}), bf16[8,64,512]{2,1,0:T(8,128)(2,1)S(1)}, u32[]{:S(2)}, u32[]{:S(2)}) async-start(bf16[8,64,512]{2,1,0:T(8,128)(2,1)} %shard_map.65), calls=%async_computation.1 | async-start | bytes 1048576 | tf_op jit(solution)/shard_map/all_to_all | solution.py:151
  53.4 0.0 copy-done.2
  53.5 2.0 %collective-permute-start = (bf16[512,1024]{1,0:T(8,128)(2,1)S(1)}, bf16[512,1024]{1,0:T(8,128)(2,1)S(1)}, u32[]{:S(2)}, u32[]{:S(2)}) collective-permute-start(bf16[512,1024]{1,0:T(8,128)(2,1)S(1)} %copy-done.2), channel_id=1, source_target_pairs={{0,4},{4,0},{1,5},{5,1},{2,6},{6,2},{3,7},{7,3},{8,12},{12,8},{9,1... | collective-permute-start | bytes 3145736 | tf_op jit(solution)/shard_map/ppermute | solution.py:155
  55.5 0.1 reshape.39
  55.6 0.1 rev.3
  55.7 0.1 copy.9
  55.7 0.1 copy.10
  55.8 0.1 reshape.41
  55.9 0.1 reshape.40
  56.0 6.8 %all-to-all-done.1 = bf16[8,64,512]{2,1,0:T(8,128)(2,1)S(1)} async-done(((bf16[8,64,512]{2,1,0:T(8,128)(2,1)}), bf16[8,64,512]{2,1,0:T(8,128)(2,1)S(1)}, u32[]{:S(2)}, u32[]{:S(2)}) %all-to-all-start.1) | async-done | bytes 524320 | tf_op jit(solution)/shard_map/all_to_all | solution.py:151
  62.9 0.5 convolution_convert_fusion
  63.3 0.7 fusion.3
  64.1 0.0 collective-permute-done
  64.1 0.8 add_convert_fusion.1
  64.8 0.0 copy-start.3
  64.8 31.9 %all_to_all.16 = bf16[16,32,1024]{2,1,0:T(8,128)(2,1)S(1)} all-to-all(bf16[16,32,1024]{2,1,0:T(8,128)(2,1)S(1)} %bitcast.20), channel_id=1, replica_groups=mesh['dp'=8,'y'=8,'core'=2,'mp'=4] {'y','core'}, dimensions={0} | all-to-all | bytes 2097152 | tf_op jit(solution)/shard_map/all_to_all | solution.py:167
  96.7 0.0 copy-done.3
  96.7 1.8 %add_convert_fusion = bf16[512,1024]{1,0:T(8,128)(2,1)} fusion(bf16[512,1024]{1,0:T(8,128)(2,1)S(1)} %copy-done.3, bf16[512,1024]{1,0:T(8,128)(2,1)S(1)} %bitcast.22, s32[512]{0:T(512)S(1)} %fusion.13), kind=kOutput, calls=%fused_computation.1 | convolution fusion | flops 538705920 | bytes 3147776 | tf_op jit(solution)/shard_map/dot_general | solution.py:169
  (6 shorter events, 0.1 us)
Async XLA Ops:
  31.6 0.7 copy-start.1
  31.6 0.7 copy-start.4
  31.6 1.3 %copy-start = (bf16[1024,512]{1,0:T(8,128)(2,1)S(1)}, bf16[1024,512]{1,0:T(8,128)(2,1)}, u32[]{:S(2)}) copy-start(bf16[1024,512]{1,0:T(8,128)(2,1)} %w_ref.1) | copy-start | bytes 3145732
  35.2 18.2 %copy-start.2 = (bf16[512,1024]{1,0:T(8,128)(2,1)S(1)}, bf16[512,1024]{1,0:T(8,128)(2,1)}, u32[]{:S(2)}) copy-start(bf16[512,1024]{1,0:T(8,128)(2,1)} %param.11) | copy-start | bytes 3145732
  49.1 13.7 %all-to-all-start.1 = ((bf16[8,64,512]{2,1,0:T(8,128)(2,1)}), bf16[8,64,512]{2,1,0:T(8,128)(2,1)S(1)}, u32[]{:S(2)}, u32[]{:S(2)}) async-start(bf16[8,64,512]{2,1,0:T(8,128)(2,1)} %shard_map.65), calls=%async_computation.1 | async-start | bytes 1048576 | tf_op jit(solution)/shard_map/all_to_all | solution.py:151
  53.5 10.6 %collective-permute-start = (bf16[512,1024]{1,0:T(8,128)(2,1)S(1)}, bf16[512,1024]{1,0:T(8,128)(2,1)S(1)}, u32[]{:S(2)}, u32[]{:S(2)}) collective-permute-start(bf16[512,1024]{1,0:T(8,128)(2,1)S(1)} %copy-done.2), channel_id=1, source_target_pairs={{0,4},{4,0},{1,5},{5,1},{2,6},{6,2},{3,7},{7,3},{8,12},{12,8},{9,1... | collective-permute-start | bytes 3145736 | tf_op jit(solution)/shard_map/ppermute | solution.py:155
  64.8 31.9 %copy-start.3 = (bf16[512,1024]{1,0:T(8,128)(2,1)S(1)}, bf16[512,1024]{1,0:T(8,128)(2,1)}, u32[]{:S(2)}) copy-start(bf16[512,1024]{1,0:T(8,128)(2,1)} %param.6) | copy-start | bytes 3145732
